TPU v7x, 512 devices: a whole 4x8x8 slice. The times are simulated.
512 devices in a mesh: pipe: 16 (over x, y_lo), expert: 32 (over z, y_hi, core).
Axes of the slice: x: 4, y: 8 (y_hi: 2, y_lo: 4; y = y_hi * 4 + y_lo), z: 8, core: 2. Of those that a mesh axis runs over, the one named last changes fastest.
Arguments:
- fwd_tokens: bfloat16 [16, 2048, 3584], P('pipe', 'expert'), may hold values from -6 to 6
- bwd_tokens: bfloat16 [16, 2048, 3584], P('pipe', 'expert'), may hold values from -6 to 6
- bwd_cotangent: bfloat16 [16, 2048, 3584], P('pipe', 'expert'), may hold values from -6 to 6
- fwd_routes: int32 [16, 2048, 1], P('pipe', 'expert'), may hold values from 0 to 3; in each aligned block of 64 rows (0 to 63, 64 to 127, ..., all dimensions but the last counted through in order) at most 20 rows name the same one
- bwd_routes: int32 [16, 2048, 1], P('pipe', 'expert'), may hold values from 0 to 3; in each aligned block of 64 rows (0 to 63, 64 to 127, ..., all dimensions but the last counted through in order) at most 20 rows name the same one
- fwd_probs: float32 [16, 2048, 1], P('pipe', 'expert'), may hold values from 0.2 to 1
- bwd_probs: float32 [16, 2048, 1], P('pipe', 'expert'), may hold values from 0.2 to 1
- expert_in: bfloat16 [16, 32, 1792, 256], P('pipe', 'expert'), may hold values from -0.09375 to 0.09375
- expert_out: bfloat16 [16, 32, 256, 1792], P('pipe', 'expert'), may hold values from -0.1875 to 0.1875
Outputs:
- fwd_handoff: bfloat16 [16, 2048, 3584], P('pipe', 'expert')
- bwd_handoff: bfloat16 [16, 2048, 3584], P('pipe', 'expert')
Inputs may be any that keep to these rules, and one draw needn't show every extreme that they name: `fwd_routes`: each token names 1 different experts; among the 64 tokens of one device of expert no expert is named more than 20 times, a bound that some block reaches. `bwd_routes`: as for fwd_routes.
All inputs are finite; a program needn't handle non-finite values.
Results may differ from a plain program's by a relative error of at most 0.008.
Values may be sent and summed in bfloat16 or wider, within the bound.
No kernel may reach another device: no remote copies, remote signals or barrier semaphores. Data moves between devices by JAX's collectives and lax.ppermute only.
A program may use at most 64 MiB of HBM per device.

v0:
```python
import jax
import jax.numpy as jnp
from jax import lax
from jax.sharding import PartitionSpec as P

EXPERTS = 4
CAP = 20


def partner(shard, axis, stride):
    return lax.ppermute(shard, axis, [(i, i ^ 1 << stride) for i in range(lax.axis_size(axis))])


def from_behind(value, axis, steps):
    count = lax.axis_size(axis)
    pairs = [(source, (source + steps) % count) for source in range(count)]
    return lax.ppermute(value, axis, pairs)


def route_tables(routes, probs, experts, capacity):
    tok_rows = routes.shape[0]
    top_count = routes.shape[1]
    chosen = routes.reshape(-1)
    onehot = (chosen[:, None] == jnp.arange(experts, dtype=jnp.int32)[None, :]).astype(jnp.int32)
    slots = jnp.sum((jnp.cumsum(onehot, axis=0) - 1) * onehot, axis=1)
    target = chosen * capacity + slots
    lookup = (target[:, None] == jnp.arange(experts * capacity, dtype=jnp.int32)[None, :]).astype(
        jnp.float32
    )
    lookup = lookup.reshape(tok_rows, top_count, experts * capacity)
    sender = jnp.sum(lookup, axis=1).T.astype(jnp.bfloat16).reshape(experts, capacity, tok_rows)
    merger = jnp.einsum("tk,tkc->tc", probs, lookup, precision=lax.Precision.HIGHEST)
    return (sender, merger.reshape(tok_rows, experts, capacity))


def local(
    fwd_tokens,
    bwd_tokens,
    bwd_cotangent,
    fwd_routes,
    bwd_routes,
    fwd_probs,
    bwd_probs,
    expert_in,
    expert_out,
):
    devices = lax.axis_size("expert")
    experts = EXPERTS
    capacity = CAP
    pieces = devices // experts // 2
    width = fwd_tokens.shape[2]
    half = width // 2
    w_in = expert_in[0, 0]
    w_out = expert_out[0, 0]
    fwd_rows = fwd_tokens[0]
    bwd_rows = bwd_tokens[0]
    cot_rows = bwd_cotangent[0]
    fwd_sender, fwd_merger = route_tables(fwd_routes[0], fwd_probs[0], experts, capacity)
    bwd_sender, bwd_merger = route_tables(bwd_routes[0], bwd_probs[0], experts, capacity)

    def pack_rows(sender, values):
        split = values.reshape(values.shape[0], 2, half)
        packed = jnp.einsum(
            "ect,thd->ehcd", sender, split, preferred_element_type=jnp.float32
        ).astype(jnp.bfloat16)
        spread = jnp.broadcast_to(packed[:, None], (experts, pieces, 2, capacity, half))
        return spread.reshape(devices, capacity, half)

    def run_backward(received):
        rows_in = received[0].reshape(-1, half)
        cots_in = received[1].reshape(-1, half)
        partial_act = jnp.dot(rows_in, w_in, preferred_element_type=jnp.float32)
        partial_grad = lax.dot_general(
            cots_in, w_out, (((1,), (1,)), ((), ())), preferred_element_type=jnp.float32
        )
        other_act, other_grad = (
            partner(partial_act.astype(jnp.bfloat16), "expert", 0).astype(partial_act.dtype),
            partner(partial_grad.astype(jnp.bfloat16), "expert", 0).astype(partial_grad.dtype),
        )
        pre_act = partial_act + other_act
        d_hidden = partial_grad + other_grad
        sigma_act = jax.nn.sigmoid(pre_act)
        d_pre = (d_hidden * sigma_act * (1.0 + pre_act * (1.0 - sigma_act))).astype(jnp.bfloat16)
        result = lax.dot_general(
            d_pre, w_in, (((1,), (1,)), ((), ())), preferred_element_type=jnp.float32
        ).astype(jnp.bfloat16)
        return result.reshape(received[0].shape)

    def merge_rows(merger, returned):
        grouped = returned.reshape(experts, pieces, 2, capacity, half)
        summed = jnp.sum(grouped, axis=1, dtype=jnp.float32)
        mixed = jnp.einsum("tec,ehcd->thd", merger, summed, precision=lax.Precision.HIGHEST)
        return mixed.reshape(-1, width)

    fwd_buffer = pack_rows(fwd_sender, fwd_rows)
    bwd_buffer = pack_rows(bwd_sender, bwd_rows)
    cot_buffer = pack_rows(bwd_sender, cot_rows)
    received = (
        lax.all_to_all(fwd_buffer, "expert", split_axis=0, concat_axis=0, tiled=True),
        lax.all_to_all(bwd_buffer, "expert", split_axis=0, concat_axis=0, tiled=True),
        lax.all_to_all(cot_buffer, "expert", split_axis=0, concat_axis=0, tiled=True),
    )
    run_received = received[0]
    rows_in = run_received.reshape(-1, half)
    partial_value = jnp.dot(rows_in, w_in, preferred_element_type=jnp.float32)
    pre_act = partial_value + partner(partial_value.astype(jnp.bfloat16), "expert", 0).astype(
        partial_value.dtype
    )
    hidden = jax.nn.silu(pre_act).astype(jnp.bfloat16)
    result = jnp.dot(hidden, w_out, preferred_element_type=jnp.float32).astype(jnp.bfloat16)
    fwd_back = result.reshape(run_received.shape)
    bwd_back = run_backward((received[1], received[2]))
    fwd_return, bwd_return = (
        lax.all_to_all(fwd_back, "expert", split_axis=0, concat_axis=0, tiled=True),
        lax.all_to_all(bwd_back, "expert", split_axis=0, concat_axis=0, tiled=True),
    )
    forward_out = (fwd_rows.astype(jnp.float32) + merge_rows(fwd_merger, fwd_return)).astype(
        jnp.bfloat16
    )
    fwd_handoff = from_behind(forward_out[None], "pipe", 1)
    input_grad = (cot_rows.astype(jnp.float32) + merge_rows(bwd_merger, bwd_return)).astype(
        jnp.bfloat16
    )
    bwd_handoff = from_behind(input_grad[None], "pipe", -1)
    return (fwd_handoff, bwd_handoff)


def solution(mesh):
    return jax.shard_map(
        local,
        mesh=mesh,
        in_specs=(
            P("pipe", "expert", None),
            P("pipe", "expert", None),
            P("pipe", "expert", None),
            P("pipe", "expert", None),
            P("pipe", "expert", None),
            P("pipe", "expert", None),
            P("pipe", "expert", None),
            P("pipe", "expert", None, None),
            P("pipe", "expert", None, None),
        ),
        out_specs=(P("pipe", "expert", None), P("pipe", "expert", None)),
        check_vma=False,
    )
```

profile of v0, /device:TPU:182, one launch (start us, length us, event | category | flops | bytes accessed | tf_op | source)
XLA Modules:
  0.0 546.3 jit_solution(8293560066033965495)
XLA Ops:
  6.3 14.2 %all-to-all-start.2 = ((bf16[32,20,1792]{2,1,0:T(8,128)(2,1)}), bf16[32,20,1792]{2,1,0:T(8,128)(2,1)}, u32[]{:S(2)}, u32[]{:S(2)}) async-start(bf16[32,20,1792]{2,1,0:T(8,128)(2,1)} %bitcast.102), calls=%async_computation.2 | async-start | bytes 5505024 | tf_op jit(solution)/shard_map/all_to_all | solution.py:101
  21.1 66.0 %all-to-all-done.2 = bf16[32,20,1792]{2,1,0:T(8,128)(2,1)} async-done(((bf16[32,20,1792]{2,1,0:T(8,128)(2,1)}), bf16[32,20,1792]{2,1,0:T(8,128)(2,1)}, u32[]{:S(2)}, u32[]{:S(2)}) %all-to-all-start.2) | async-done | bytes 2293792 | tf_op jit(solution)/shard_map/all_to_all | solution.py:101
  88.8 12.5 %all-to-all-start.3 = ((bf16[32,20,1792]{2,1,0:T(8,128)(2,1)}), bf16[32,20,1792]{2,1,0:T(8,128)(2,1)}, u32[]{:S(2)}, u32[]{:S(2)}) async-start(bf16[32,20,1792]{2,1,0:T(8,128)(2,1)} %bitcast.101), calls=%async_computation.3 | async-start | bytes 5505024 | tf_op jit(solution)/shard_map/all_to_all | solution.py:100
  102.2 83.7 %all-to-all-done.3 = bf16[32,20,1792]{2,1,0:T(8,128)(2,1)} async-done(((bf16[32,20,1792]{2,1,0:T(8,128)(2,1)}), bf16[32,20,1792]{2,1,0:T(8,128)(2,1)}, u32[]{:S(2)}, u32[]{:S(2)}) %all-to-all-start.3) | async-done | bytes 2293792 | tf_op jit(solution)/shard_map/all_to_all | solution.py:100
  187.7 9.2 %all-to-all-start = ((bf16[32,20,1792]{2,1,0:T(8,128)(2,1)}), bf16[32,20,1792]{2,1,0:T(8,128)(2,1)}, u32[]{:S(2)}, u32[]{:S(2)}) async-start(bf16[32,20,1792]{2,1,0:T(8,128)(2,1)} %bitcast.100), calls=%async_computation | async-start | bytes 5505024 | tf_op jit(solution)/shard_map/all_to_all | solution.py:99
  196.9 2.7 reshape.164
  199.6 2.9 fusion.44
  202.5 2.0 collective-permute-start.2
  204.6 2.7 reshape.166
  208.1 2.3 collective-permute-start.3
  212.6 2.3 reshape.167
  214.9 71.8 %all-to-all-done = bf16[32,20,1792]{2,1,0:T(8,128)(2,1)} async-done(((bf16[32,20,1792]{2,1,0:T(8,128)(2,1)}), bf16[32,20,1792]{2,1,0:T(8,128)(2,1)}, u32[]{:S(2)}, u32[]{:S(2)}) %all-to-all-start) | async-done | bytes 2293792 | tf_op jit(solution)/shard_map/all_to_all | solution.py:99
  286.7 9.7 %all-to-all-start.4 = ((bf16[32,20,1792]{2,1,0:T(8,128)(2,1)}), bf16[32,20,1792]{2,1,0:T(8,128)(2,1)}, u32[]{:S(2)}, u32[]{:S(2)}) async-start(bf16[32,20,1792]{2,1,0:T(8,128)(2,1)} %reshape.167), calls=%async_computation.4 | async-start | bytes 5505024 | tf_op jit(solution)/shard_map/all_to_all | solution.py:115
  296.4 2.7 reshape.159
  299.9 2.1 collective-permute-start
  304.3 2.2 reshape.160
  306.5 69.9 %all-to-all-done.4 = bf16[32,20,1792]{2,1,0:T(8,128)(2,1)} async-done(((bf16[32,20,1792]{2,1,0:T(8,128)(2,1)}), bf16[32,20,1792]{2,1,0:T(8,128)(2,1)}, u32[]{:S(2)}, u32[]{:S(2)}) %all-to-all-start.4) | async-done | bytes 2293792 | tf_op jit(solution)/shard_map/all_to_all | solution.py:115
  376.4 70.1 %all-to-all-start.1 = ((bf16[32,20,1792]{2,1,0:T(8,128)(2,1)}), bf16[32,20,1792]{2,1,0:T(8,128)(2,1)}, u32[]{:S(2)}, u32[]{:S(2)}) async-start(bf16[32,20,1792]{2,1,0:T(8,128)(2,1)} %reshape.160), calls=%async_computation.1 | async-start | bytes 5505024 | tf_op jit(solution)/shard_map/all_to_all | solution.py:114
  446.5 2.4 convert_reduce_fusion
  450.5 2.9 fusion.4
  455.3 68.5 %all-to-all-done.1 = bf16[32,20,1792]{2,1,0:T(8,128)(2,1)} async-done(((bf16[32,20,1792]{2,1,0:T(8,128)(2,1)}), bf16[32,20,1792]{2,1,0:T(8,128)(2,1)}, u32[]{:S(2)}, u32[]{:S(2)}) %all-to-all-start.1) | async-done | bytes 2293792 | tf_op jit(solution)/shard_map/all_to_all | solution.py:114
  523.8 2.4 convert_reduce_fusion.1
  527.7 2.1 fusion.5
  531.7 12.0 %collective-permute-done.1 = bf16[1,64,3584]{2,1,0:T(8,128)(2,1)S(1)} collective-permute-done((bf16[1,64,3584]{2,1,0:T(8,128)(2,1)S(1)}, bf16[1,64,3584]{2,1,0:T(8,128)(2,1)S(1)}, u32[]{:S(2)}, u32[]{:S(2)}) %collective-permute-start.1) | collective-permute-done | bytes 458784 | tf_op jit(solution)/shard_map/ppermute | solution.py:17
  (54 shorter events, 26.0 us)
Async XLA Ops:
  0.6 206.7 %copy-start = (bf16[1,1,1792,256]{3,2,1,0:T(8,128)(2,1)S(1)}, bf16[1,1,1792,256]{3,2,1,0:T(8,128)(2,1)}, u32[]{:S(2)}) copy-start(bf16[1,1,1792,256]{3,2,1,0:T(8,128)(2,1)} %param.16) | copy-start | bytes 2752516
  6.3 14.2 %copy-start.2 = (bf16[1,64,3584]{2,1,0:T(8,128)(2,1)S(1)}, bf16[1,64,3584]{2,1,0:T(8,128)(2,1)}, u32[]{:S(2)}) copy-start(bf16[1,64,3584]{2,1,0:T(8,128)(2,1)} %param.10) | copy-start | bytes 1376260
  6.3 80.7 %all-to-all-start.2 = ((bf16[32,20,1792]{2,1,0:T(8,128)(2,1)}), bf16[32,20,1792]{2,1,0:T(8,128)(2,1)}, u32[]{:S(2)}, u32[]{:S(2)}) async-start(bf16[32,20,1792]{2,1,0:T(8,128)(2,1)} %bitcast.102), calls=%async_computation.2 | async-start | bytes 5505024 | tf_op jit(solution)/shard_map/all_to_all | solution.py:101
  88.8 12.6 %copy-start.3 = (s32[1,64,1]{1,2,0:T(1,128)S(1)}, s32[1,64,1]{1,2,0:T(1,128)}, u32[]{:S(2)}) copy-start(s32[1,64,1]{1,2,0:T(1,128)} %param.12) | copy-start | bytes 772
  88.8 12.7 %copy-start.1 = (bf16[1,64,3584]{2,1,0:T(8,128)(2,1)S(1)}, bf16[1,64,3584]{2,1,0:T(8,128)(2,1)}, u32[]{:S(2)}) copy-start(bf16[1,64,3584]{2,1,0:T(8,128)(2,1)} %param.9) | copy-start | bytes 1376260
  88.8 97.1 %all-to-all-start.3 = ((bf16[32,20,1792]{2,1,0:T(8,128)(2,1)}), bf16[32,20,1792]{2,1,0:T(8,128)(2,1)}, u32[]{:S(2)}, u32[]{:S(2)}) async-start(bf16[32,20,1792]{2,1,0:T(8,128)(2,1)} %bitcast.101), calls=%async_computation.3 | async-start | bytes 5505024 | tf_op jit(solution)/shard_map/all_to_all | solution.py:100
  187.7 99.1 %all-to-all-start = ((bf16[32,20,1792]{2,1,0:T(8,128)(2,1)}), bf16[32,20,1792]{2,1,0:T(8,128)(2,1)}, u32[]{:S(2)}, u32[]{:S(2)}) async-start(bf16[32,20,1792]{2,1,0:T(8,128)(2,1)} %bitcast.100), calls=%async_computation | async-start | bytes 5505024 | tf_op jit(solution)/shard_map/all_to_all | solution.py:99
  202.5 7.8 %collective-permute-start.2 = (bf16[640,256]{1,0:T(8,128)(2,1)}, bf16[640,256]{1,0:T(8,128)(2,1)S(1)}, u32[]{:S(2)}, u32[]{:S(2)}) collective-permute-start(bf16[640,256]{1,0:T(8,128)(2,1)} %get-tuple-element.6), channel_id=1, source_target_pairs={{0,1},{1,0},{2,3},{3,2},{4,5},{5,4},{6,7},{7,6},{8,9},{9,8},{10,11... | collective-permute-start | bytes 983048 | tf_op jit(solution)/shard_map/ppermute | solution.py:11
  207.3 4.3 copy-start.7
  208.1 3.5 collective-permute-start.3
  286.7 89.7 %all-to-all-start.4 = ((bf16[32,20,1792]{2,1,0:T(8,128)(2,1)}), bf16[32,20,1792]{2,1,0:T(8,128)(2,1)}, u32[]{:S(2)}, u32[]{:S(2)}) async-start(bf16[32,20,1792]{2,1,0:T(8,128)(2,1)} %reshape.167), calls=%async_computation.4 | async-start | bytes 5505024 | tf_op jit(solution)/shard_map/all_to_all | solution.py:115
  299.1 4.3 copy-start.6
  299.9 3.5 collective-permute-start
  306.5 140.0 %copy-start.4 = (f32[1,64,1]{1,2,0:T(1,128)S(1)}, f32[1,64,1]{1,2,0:T(1,128)}, u32[]{:S(2)}) copy-start(f32[1,64,1]{1,2,0:T(1,128)} %param.15) | copy-start | bytes 772
  306.5 140.0 %copy-start.5 = (f32[1,64,1]{1,2,0:T(1,128)S(1)}, f32[1,64,1]{1,2,0:T(1,128)}, u32[]{:S(2)}) copy-start(f32[1,64,1]{1,2,0:T(1,128)} %param.14) | copy-start | bytes 772
  376.4 147.4 %all-to-all-start.1 = ((bf16[32,20,1792]{2,1,0:T(8,128)(2,1)}), bf16[32,20,1792]{2,1,0:T(8,128)(2,1)}, u32[]{:S(2)}, u32[]{:S(2)}) async-start(bf16[32,20,1792]{2,1,0:T(8,128)(2,1)} %reshape.160), calls=%async_computation.1 | async-start | bytes 5505024 | tf_op jit(solution)/shard_map/all_to_all | solution.py:114
  453.3 78.4 %collective-permute-start.4 = (bf16[1,64,3584]{2,1,0:T(8,128)(2,1)}, bf16[1,64,3584]{2,1,0:T(8,128)(2,1)}, u32[]{:S(2)}, u32[]{:S(2)}) collective-permute-start(bf16[1,64,3584]{2,1,0:T(8,128)(2,1)} %fusion.4), channel_id=1, source_target_pairs={{0,480},{32,0},{64,32},{96,64},{128,96},{160,128},{192,160},{224,1... | collective-permute-start | bytes 1376264 | tf_op jit(solution)/shard_map/ppermute | solution.py:17
  529.8 14.0 %collective-permute-start.1 = (bf16[1,64,3584]{2,1,0:T(8,128)(2,1)S(1)}, bf16[1,64,3584]{2,1,0:T(8,128)(2,1)S(1)}, u32[]{:S(2)}, u32[]{:S(2)}) collective-permute-start(bf16[1,64,3584]{2,1,0:T(8,128)(2,1)S(1)} %fusion.5), channel_id=1, source_target_pairs={{0,32},{32,64},{64,96},{96,128},{128,160},{160,192},{192,224},{224... | collective-permute-start | bytes 1376264 | tf_op jit(solution)/shard_map/ppermute | solution.py:17
where the time goes:
time: 547 us; the launch traced here: 546 us
  waiting for transfers between devices  375 us (69%)
  starting transfers between devices  126 us (23%)
  local copies, waits for them, and re-layouts  24.8 us (5%)
  matrix products  12.5 us (2%)
  other arithmetic  7.55 us (1%)
    all_to_all x1, waiting for transfers between devices, local(): lax.all_to_all(bwd_buffer, 'expert', split_axis=0, concat_axis=0, tiled=T...  83.7 us
    all_to_all x1, waiting for transfers between devices, local(): lax.all_to_all(fwd_buffer, 'expert', split_axis=0, concat_axis=0, tiled=T...  71.8 us
    all_to_all x1, starting transfers between devices, local(): lax.all_to_all(fwd_back, 'expert', split_axis=0, concat_axis=0, tiled=True)  70.1 us
    all_to_all x1, waiting for transfers between devices, local(): lax.all_to_all(bwd_back, 'expert', split_axis=0, concat_axis=0, tiled=True)  69.9 us
    all_to_all x1, waiting for transfers between devices, local(): lax.all_to_all(fwd_back, 'expert', split_axis=0, concat_axis=0, tiled=True)  68.5 us
    all_to_all x1, waiting for transfers between devices, local(): lax.all_to_all(cot_buffer, 'expert', split_axis=0, concat_axis=0, tiled=T...  66 us
    all_to_all x1, starting transfers between devices, local(): lax.all_to_all(cot_buffer, 'expert', split_axis=0, concat_axis=0, tiled=T...  14.2 us
    all_to_all x1, starting transfers between devices, local(): lax.all_to_all(bwd_buffer, 'expert', split_axis=0, concat_axis=0, tiled=T...  12.5 us
  transfers between devices with their start and end apart: 10, of which 8 were waited for; matrix products, arithmetic and copies ran while one was open for 6% of the time, Pallas kernels for 0%

commit v1 on v0

v1 whole, which is shorter than its diff:
```python
import jax
import jax.numpy as jnp
from jax import lax
from jax.experimental import pallas as pl
from jax.experimental.pallas import tpu as pltpu
from jax.sharding import PartitionSpec as P

EXPERTS = 4
CAP = 20
RINGS = 8
F32 = jnp.float32
BF16 = jnp.bfloat16
NN = (((1,), (0,)), ((), ()))
NT = (((1,), (1,)), ((), ()))
TN = (((0,), (0,)), ((), ()))
CORE, PLANE, PAIR = 1, 2, 4
LIMIT = 32 * 1024 * 1024


def dot(left, right, dims=NN):
    return lax.dot_general(left, right, dims, preferred_element_type=F32)


def swap(value, mask, who=None):
    count = lax.axis_size("expert")
    return lax.ppermute(value, "expert", [(i, i ^ mask) for i in range(count) if who is None or who(i)])


def keeps(index):
    return (index >> 2 & 1) == (index & 1)


def moves(index):
    return not keeps(index)


def from_behind(value, steps):
    count = lax.axis_size("pipe")
    return lax.ppermute(value, "pipe", [(i, (i + steps) % count) for i in range(count)])


def ring_exchange(value):
    count = lax.axis_size("expert")
    rings = count // 4
    groups = [[z * 4 + b for z in range(rings)] for b in range(4)]
    cut = value.reshape(rings, -1, value.shape[-1])
    got = lax.all_to_all(cut, "expert", split_axis=0, concat_axis=0, tiled=True, axis_index_groups=groups)
    return got.reshape(value.shape)


def call(body, outs, *args):
    shapes = [jax.ShapeDtypeStruct(s, d) for s, d in outs]
    return pl.pallas_call(
        body,
        out_shape=shapes,
        in_specs=[pl.BlockSpec(memory_space=pltpu.VMEM) for _ in args],
        out_specs=[pl.BlockSpec(memory_space=pltpu.VMEM) for _ in outs],
        compiler_params=pltpu.CompilerParams(vmem_limit_bytes=LIMIT),
    )(*args)


def senders(routes, expert):
    count = routes.shape[1]
    mine = jnp.broadcast_to(routes == expert, (2 * CAP, count))
    upto = lax.broadcasted_iota(jnp.int32, (count, count), 0) <= lax.broadcasted_iota(jnp.int32, (count, count), 1)
    rank = dot(mine.astype(F32).astype(BF16), upto.astype(F32).astype(BF16)).astype(jnp.int32) - 1
    row = lax.broadcasted_iota(jnp.int32, (2 * CAP, count), 0)
    low = mine & (rank == row)
    high = mine & (rank == row - CAP)
    return low.astype(F32).astype(BF16), high.astype(F32).astype(BF16)


def pack_body(routes, low_rows, high_rows, out):
    wide = out.shape[2]
    step = low_rows.shape[1] // 2
    shift = 0 if high_rows.shape[1] == wide * 2 else wide
    for e in range(EXPERTS):
        low, high = senders(routes[...], e)
        for h in range(2):
            part = dot(low, low_rows[:, pl.ds(h * step, wide)])
            part += dot(high, high_rows[:, pl.ds(h * step + shift, wide)])
            out[2 * e + h] = part.astype(BF16)


def halves(rows):
    row = lax.broadcasted_iota(jnp.int32, (rows // 2, rows), 0)
    col = lax.broadcasted_iota(jnp.int32, (rows // 2, rows), 1)
    block = row // CAP
    low = col == row + block * CAP
    high = col == row + block * CAP + CAP
    return low.astype(F32).astype(BF16), high.astype(F32).astype(BF16)


def act_fwd_body(own, other, in1, in2, act, sent):
    rows, wide = own.shape
    low, high = halves(rows)
    for k, ref in enumerate((own, other)):
        a = dot(low, ref[...]).astype(BF16)
        b = dot(high, ref[...]).astype(BF16)
        at = pl.ds(k * (rows // 2), rows // 2)
        for q, w in enumerate((in1, in2)):
            n = w.shape[1]
            part = dot(a, w[pl.ds(0, wide), :]) + dot(b, w[pl.ds(wide, wide), :])
            act[at, pl.ds(q * n, n)] = part
            sent[at, pl.ds(q * n, n)] = part.astype(BF16)


def act_bwd_body(own, other, in1, in2, out1, out2, act, grad, sent_act, sent_grad):
    rows = own.shape[0]
    low, high = halves(rows)
    for k, ref in enumerate((own, other)):
        a = dot(low, ref[...]).astype(BF16)
        b = dot(high, ref[...]).astype(BF16)
        at = pl.ds(k * (rows // 2), rows // 2)
        for q, (wi, wo) in enumerate(((in1, out1), (in2, out2))):
            n = wi.shape[1]
            part = dot(a, wi[...])
            act[at, pl.ds(q * n, n)] = part
            sent_act[at, pl.ds(q * n, n)] = part.astype(BF16)
            part = dot(b, wo[...], NT)
            grad[at, pl.ds(q * n, n)] = part
            sent_grad[at, pl.ds(q * n, n)] = part.astype(BF16)


def out_fwd_body(act, got, out1, out2, own, sent):
    a = act[...] + got[...].astype(F32)
    h = (a * jax.nn.sigmoid(a)).astype(BF16)
    n = out1.shape[0]
    o = dot(h[:, :n], out1[...]) + dot(h[:, n:], out2[...])
    half = own.shape[0]
    own[...] = o[:half]
    sent[...] = o[half:].astype(BF16)


def out_bwd_body(act, got_act, grad, got_grad, in1, in2, own, sent):
    a = act[...] + got_act[...].astype(F32)
    g = grad[...] + got_grad[...].astype(F32)
    s = jax.nn.sigmoid(a)
    r = (g * s * (1.0 + a * (1.0 - s))).astype(BF16)
    n = in1.shape[1]
    u = dot(r[:, :n], in1[...], NT) + dot(r[:, n:], in2[...], NT)
    half = own.shape[0]
    own[...] = u[:half]
    sent[...] = u[half:].astype(BF16)


def finish_body(own, got, out):
    total = (own[...] + got[...].astype(F32)).astype(BF16)
    low, high = halves(out.shape[0])
    wide = out.shape[1]
    out[...] = (dot(low, total[:, :wide], TN) + dot(high, total[:, wide:], TN)).astype(BF16)


def merge_body(routes, probs, rows, got, out):
    wide = got.shape[1]
    block = 2 * CAP
    pairs = [senders(routes[...], e) for e in range(EXPERTS)]
    for h in range(2):
        for q in range(2):
            total = None
            for e in range(EXPERTS):
                part = dot(pairs[e][q], got[pl.ds((2 * e + h) * block, block), :], TN)
                total = part if total is None else total + part
            at = pl.ds((2 * h + q) * wide, wide)
            out[:, at] = (rows[:, at].astype(F32) + probs[...] * total).astype(BF16)


def local(
    fwd_tokens,
    bwd_tokens,
    bwd_cotangent,
    fwd_routes,
    bwd_routes,
    fwd_probs,
    bwd_probs,
    expert_in,
    expert_out,
):
    rings = lax.axis_size("expert") // 4
    index = lax.axis_index("expert")
    keep = (index >> 2 & 1) == (index & 1)
    own_in, own_out = expert_in[0, 0], expert_out[0, 0]
    features, hidden = own_in.shape
    quarter = features // 2
    slots = rings * CAP
    tokens = fwd_tokens.shape[1]
    rows_f, rows_b, rows_c = fwd_tokens[0], bwd_tokens[0], bwd_cotangent[0]
    routes_f, routes_b = fwd_routes.reshape(1, tokens), bwd_routes.reshape(1, tokens)
    probs_f, probs_b = fwd_probs.reshape(tokens, 1), bwd_probs.reshape(tokens, 1)

    z_in, z_out = swap(own_in, PAIR | CORE, moves), swap(own_out, PAIR | CORE, moves)
    y_in, y_out = swap(own_in, PLANE, keeps), swap(own_out, PLANE, keeps)
    v_in, v_out = swap(z_in, PLANE, moves), swap(z_out, PLANE, moves)
    in1, out1 = jnp.where(keep, own_in, z_in), jnp.where(keep, own_out, z_out)
    in2, out2 = jnp.where(keep, y_in, v_in), jnp.where(keep, y_out, v_out)

    (send_f,) = call(pack_body, [((2 * EXPERTS, 2 * CAP, quarter), BF16)], routes_f, rows_f, rows_f)
    (send_b,) = call(pack_body, [((2 * EXPERTS, 2 * CAP, features), BF16)], routes_b, rows_b, rows_c)
    send_f, send_b, z_in, z_out = lax.optimization_barrier((send_f, send_b, z_in, z_out))
    got_f = ring_exchange(send_f).reshape(2 * slots, quarter)
    got_b = ring_exchange(send_b).reshape(2 * slots, features)
    far_f, far_b = swap(got_f, CORE), swap(got_b, CORE)

    pre = (2 * slots, 2 * hidden)
    act_f, sent_f = call(act_fwd_body, [(pre, F32), (pre, BF16)], got_f, far_f, in1, in2)
    act_b, grad_b, sent_a, sent_g = call(
        act_bwd_body, [(pre, F32), (pre, F32), (pre, BF16), (pre, BF16)], got_b, far_b, in1, in2, out1, out2
    )
    back_f, back_a, back_g = swap(sent_f, PAIR), swap(sent_a, PAIR), swap(sent_g, PAIR)
    outs = [((slots, features), F32), ((slots, features), BF16)]
    own_f, cross_f = call(out_fwd_body, outs, act_f, back_f, out1, out2)
    own_b, cross_b = call(out_bwd_body, outs, act_b, back_a, grad_b, back_g, in1, in2)
    cross_f, cross_b = swap(cross_f, CORE), swap(cross_b, CORE)
    shape = [((2 * slots, quarter), BF16)]
    (ret_f,) = call(finish_body, shape, own_f, cross_f)
    (ret_b,) = call(finish_body, shape, own_b, cross_b)
    home_f = ring_exchange(ret_f)
    home_b = ring_exchange(ret_b)
    shape = [((tokens, 2 * features), BF16)]
    (y,) = call(merge_body, shape, routes_f, probs_f, rows_f, home_f)
    (dx,) = call(merge_body, shape, routes_b, probs_b, rows_c, home_b)
    return from_behind(y[None], 1), from_behind(dx[None], -1)


def solution(mesh):
    row = P("pipe", "expert", None)
    block = P("pipe", "expert", None, None)
    return jax.shard_map(
        local,
        mesh=mesh,
        in_specs=(row,) * 7 + (block,) * 2,
        out_specs=(row, row),
        check_vma=False,
    )
```

time: 547 us -> 241 us (0.44)
  the two profiles are of different devices: /device:TPU:182 before, /device:TPU:1 now
where the time goes in v1:
time: 241 us; the launch traced here: 238 us
  waiting for transfers between devices  116 us (48%)
  starting transfers between devices  68.9 us (29%)
  blocking collectives  25.8 us (11%)
  Pallas kernels  16.5 us (7%)
  local copies, waits for them, and re-layouts  5.6 us (2%)
  other arithmetic  4.22 us (2%)
    ppermute x13, waiting for transfers between devices, swap(): lax.ppermute(value, 'expert', [(i, i ^ mask) for i in range(count) if who...  91.2 us
    ppermute x13, starting transfers between devices, swap(): lax.ppermute(value, 'expert', [(i, i ^ mask) for i in range(count) if who...  45.5 us
    all_to_all x1, blocking collectives, ring_exchange(): lax.all_to_all(cut, 'expert', split_axis=0, concat_axis=0, tiled=True, ax...  25.8 us
    all_to_all x3, starting transfers between devices, ring_exchange(): lax.all_to_all(cut, 'expert', split_axis=0, concat_axis=0, tiled=True, ax...  16.7 us
    pallas_call x10, Pallas kernels, call(): pl.pallas_call(body, out_shape=shapes, in_specs=[pl.BlockSpec(memory_spac...  16.5 us
    all_to_all x3, waiting for transfers between devices, ring_exchange(): lax.all_to_all(cut, 'expert', split_axis=0, concat_axis=0, tiled=True, ax...  14.7 us
    ppermute x2, waiting for transfers between devices, from_behind(): lax.ppermute(value, 'pipe', [(i, (i + steps) % count) for i in range(coun...  9.97 us
    ppermute x2, starting transfers between devices, from_behind(): lax.ppermute(value, 'pipe', [(i, (i + steps) % count) for i in range(coun...  6.74 us
  transfers between devices with their start and end apart: 18, of which 10 were waited for; matrix products, arithmetic and copies ran while one was open for 2% of the time, Pallas kernels for 7%

profile of v1, /device:TPU:1, one launch (start us, length us, event | category | flops | bytes accessed | tf_op | source)
XLA Modules:
  0.0 237.8 jit_solution(6046149691285352005)
XLA Ops:
  0.6 5.4 %collective-permute-start = (bf16[1792,256]{1,0:T(8,128)(2,1)}, bf16[1792,256]{1,0:T(8,128)(2,1)}, u32[]{:S(2)}, u32[]{:S(2)}) collective-permute-start(bf16[1792,256]{1,0:T(8,128)(2,1)} %bitcast.35), channel_id=1, source_target_pairs={{1,4},{3,6},{4,1},{6,3},{9,12},{11,14},{12,9},{14,11},{17,20},{19,... | collective-permute-start | bytes 2752520 | tf_op jit(solution)/shard_map/ppermute | solution.py:26
  10.8 2.4 %shard_map.105 = bf16[8,40,1792]{2,1,0:T(8,128)(2,1)} custom-call(s32[1,64]{1,0:T(1,128)S(1)} %bitcast.33, bf16[64,3584]{1,0:T(8,128)(2,1)S(1)} %bitcast.28, bf16[64,3584]{1,0:T(8,128)(2,1)S(1)} %bitcast.26), custom_call_target="tpu_custom_call" | custom-call | tf_op jit(solution)/shard_map/pallas_call | solution.py:53
  13.2 4.2 %collective-permute-done = bf16[1792,256]{1,0:T(8,128)(2,1)} collective-permute-done((bf16[1792,256]{1,0:T(8,128)(2,1)}, bf16[1792,256]{1,0:T(8,128)(2,1)}, u32[]{:S(2)}, u32[]{:S(2)}) %collective-permute-start) | collective-permute-done | bytes 917536 | tf_op jit(solution)/shard_map/ppermute | solution.py:26
  17.4 9.8 %collective-permute-done.1 = bf16[256,1792]{1,0:T(8,128)(2,1)} collective-permute-done((bf16[256,1792]{1,0:T(8,128)(2,1)}, bf16[256,1792]{1,0:T(8,128)(2,1)}, u32[]{:S(2)}, u32[]{:S(2)}) %collective-permute-start.1) | collective-permute-done | bytes 917536 | tf_op jit(solution)/shard_map/ppermute | solution.py:26
  27.3 25.8 %all_to_all.20 = bf16[8,40,896]{2,1,0:T(8,128)(2,1)S(1)} all-to-all(bf16[8,40,896]{2,1,0:T(8,128)(2,1)S(1)} %shard_map.104), channel_id=1, replica_groups={{0,4,8,12,16,20,24,28},{1,5,9,13,17,21,25,29},{2,6,10,14,18,22,26,30},{..., dimensions={0} | all-to-all | bytes 1146880 | tf_op jit(solution)/shard_map/all_to_all | solution.py:47
  53.0 4.4 %all-to-all-start.2 = ((bf16[8,40,1792]{2,1,0:T(8,128)(2,1)}), bf16[8,40,1792]{2,1,0:T(8,128)(2,1)}, u32[]{:S(2)}, u32[]{:S(2)}) async-start(bf16[8,40,1792]{2,1,0:T(8,128)(2,1)} %shard_map.105), calls=%async_computation.2 | async-start | bytes 2293760 | tf_op jit(solution)/shard_map/all_to_all | solution.py:47
  60.6 7.4 %collective-permute-start.4 = (bf16[1792,256]{1,0:T(8,128)(2,1)}, bf16[1792,256]{1,0:T(8,128)(2,1)S(1)}, u32[]{:S(2)}, u32[]{:S(2)}) collective-permute-start(bf16[1792,256]{1,0:T(8,128)(2,1)} %collective-permute-done), channel_id=1, source_target_pairs={{1,3},{3,1},{4,6},{6,4},{9,11},{11,9},{12,14},{14,12},{17,19},{19,... | collective-permute-start | bytes 2752520 | tf_op jit(solution)/shard_map/ppermute | solution.py:26
  71.3 2.9 %collective-permute-start.2 = (bf16[320,896]{1,0:T(8,128)(2,1)S(1)}, bf16[320,896]{1,0:T(8,128)(2,1)S(1)}, u32[]{:S(2)}, u32[]{:S(2)}) collective-permute-start(bf16[320,896]{1,0:T(8,128)(2,1)S(1)} %bitcast.24), channel_id=1, source_target_pairs={{0,1},{1,0},{2,3},{3,2},{4,5},{5,4},{6,7},{7,6},{8,9},{9,8},{10,11... | collective-permute-start | bytes 1720328 | tf_op jit(solution)/shard_map/ppermute | solution.py:26
  75.8 23.0 %collective-permute-done.4 = bf16[1792,256]{1,0:T(8,128)(2,1)S(1)} collective-permute-done((bf16[1792,256]{1,0:T(8,128)(2,1)}, bf16[1792,256]{1,0:T(8,128)(2,1)S(1)}, u32[]{:S(2)}, u32[]{:S(2)}) %collective-permute-start.4) | collective-permute-done | bytes 917536 | tf_op jit(solution)/shard_map/ppermute | solution.py:26
  98.9 2.2 shard_map.106
  103.9 10.2 %collective-permute-start.10 = (bf16[320,1792]{1,0:T(8,128)(2,1)}, bf16[320,1792]{1,0:T(8,128)(2,1)}, u32[]{:S(2)}, u32[]{:S(2)}) collective-permute-start(bf16[320,1792]{1,0:T(8,128)(2,1)} %bitcast.13.own), channel_id=1, source_target_pairs={{0,1},{1,0},{2,3},{3,2},{4,5},{5,4},{6,7},{7,6},{8,9},{9,8},{10,11... | collective-permute-start | bytes 3440648 | tf_op jit(solution)/shard_map/ppermute | solution.py:26
  114.2 33.7 %collective-permute-done.7 = bf16[256,1792]{1,0:T(8,128)(2,1)} collective-permute-done((bf16[256,1792]{1,0:T(8,128)(2,1)}, bf16[256,1792]{1,0:T(8,128)(2,1)}, u32[]{:S(2)}, u32[]{:S(2)}) %collective-permute-start.7) | collective-permute-done | bytes 917536 | tf_op jit(solution)/shard_map/ppermute | solution.py:26
  152.0 1.9 collective-permute-done.8.got
  155.3 6.7 %all-to-all-start.1 = ((bf16[8,40,896]{2,1,0:T(8,128)(2,1)}), bf16[8,40,896]{2,1,0:T(8,128)(2,1)S(1)}, u32[]{:S(2)}, u32[]{:S(2)}) async-start(bf16[8,40,896]{2,1,0:T(8,128)(2,1)} %bitcast.9), calls=%async_computation.1 | async-start | bytes 1146880 | tf_op jit(solution)/shard_map/all_to_all | solution.py:47
  163.2 4.8 %shard_map.110 = (f32[320,512]{1,0:T(8,128)S(1)}, f32[320,512]{1,0:T(8,128)S(1)}, bf16[320,512]{1,0:T(8,128)(2,1)S(1)}, bf16[320,512]{1,0:T(8,128)(2,1)S(1)}) custom-call(bf16[320,1792]{1,0:T(8,128)(2,1)} %bitcast.13.own, bf16[320,1792]{1,0:T(8,128)(2,1)} %collective-permute-done.10.other, bf16[1792,256]{1,0:T(8,128)(2,1)S(1)} %broadcast_select_fusion.3.in1, ...), custom_call_target="tpu_custom_call" | custom-call | tf_op jit(solution)/shard_map/pallas_call | solution.py:53
  168.0 3.4 %collective-permute-start.11 = (bf16[320,512]{1,0:T(8,128)(2,1)S(1)}, bf16[320,512]{1,0:T(8,128)(2,1)S(1)}, u32[]{:S(2)}, u32[]{:S(2)}) collective-permute-start(bf16[320,512]{1,0:T(8,128)(2,1)S(1)} %get-tuple-element.21), channel_id=1, source_target_pairs={{0,4},{1,5},{2,6},{3,7},{4,0},{5,1},{6,2},{7,3},{8,12},{9,13},{10,... | collective-permute-start | bytes 983048 | tf_op jit(solution)/shard_map/ppermute | solution.py:26
  173.3 9.9 %collective-permute-done.11.got_act = bf16[320,512]{1,0:T(8,128)(2,1)S(1)} collective-permute-done((bf16[320,512]{1,0:T(8,128)(2,1)S(1)}, bf16[320,512]{1,0:T(8,128)(2,1)S(1)}, u32[]{:S(2)}, u32[]{:S(2)}) %collective-permute-start.11) | collective-permute-done | bytes 327712 | tf_op jit(solution)/shard_map/ppermute | solution.py:26
  183.1 7.0 %collective-permute-done.12.got_grad = bf16[320,512]{1,0:T(8,128)(2,1)S(1)} collective-permute-done((bf16[320,512]{1,0:T(8,128)(2,1)S(1)}, bf16[320,512]{1,0:T(8,128)(2,1)S(1)}, u32[]{:S(2)}, u32[]{:S(2)}) %collective-permute-start.12) | collective-permute-done | bytes 327712 | tf_op jit(solution)/shard_map/ppermute | solution.py:26
  191.0 3.4 %collective-permute-start.13 = (bf16[160,1792]{1,0:T(8,128)(2,1)S(1)}, bf16[160,1792]{1,0:T(8,128)(2,1)S(1)}, u32[]{:S(2)}, u32[]{:S(2)}) collective-permute-start(bf16[160,1792]{1,0:T(8,128)(2,1)S(1)} %get-tuple-element.25), channel_id=1, source_target_pairs={{0,1},{1,0},{2,3},{3,2},{4,5},{5,4},{6,7},{7,6},{8,9},{9,8},{10,11... | collective-permute-start | bytes 1720328 | tf_op jit(solution)/shard_map/ppermute | solution.py:26
  197.4 5.6 %all-to-all-start.3 = ((bf16[8,40,896]{2,1,0:T(8,128)(2,1)}), bf16[8,40,896]{2,1,0:T(8,128)(2,1)S(1)}, u32[]{:S(2)}, u32[]{:S(2)}) async-start(bf16[8,40,896]{2,1,0:T(8,128)(2,1)} %bitcast.14), calls=%async_computation.3 | async-start | bytes 1146880 | tf_op jit(solution)/shard_map/all_to_all | solution.py:47
  204.0 3.2 %collective-permute-start.9 = (bf16[1,64,3584]{2,1,0:T(8,128)(2,1)S(1)}, bf16[1,64,3584]{2,1,0:T(8,128)(2,1)S(1)}, u32[]{:S(2)}, u32[]{:S(2)}) collective-permute-start(bf16[1,64,3584]{2,1,0:T(8,128)(2,1)S(1)} %bitcast.29), channel_id=1, source_target_pairs={{0,32},{32,64},{64,96},{96,128},{128,160},{160,192},{192,224},{224... | collective-permute-start | bytes 1376264 | tf_op jit(solution)/shard_map/ppermute | solution.py:39
  207.2 14.7 %all-to-all-done.3 = bf16[8,40,896]{2,1,0:T(8,128)(2,1)S(1)} async-done(((bf16[8,40,896]{2,1,0:T(8,128)(2,1)}), bf16[8,40,896]{2,1,0:T(8,128)(2,1)S(1)}, u32[]{:S(2)}, u32[]{:S(2)}) %all-to-all-start.3) | async-done | bytes 573472 | tf_op jit(solution)/shard_map/all_to_all | solution.py:47
  222.8 3.5 %collective-permute-start.14 = (bf16[1,64,3584]{2,1,0:T(8,128)(2,1)S(1)}, bf16[1,64,3584]{2,1,0:T(8,128)(2,1)S(1)}, u32[]{:S(2)}, u32[]{:S(2)}) collective-permute-start(bf16[1,64,3584]{2,1,0:T(8,128)(2,1)S(1)} %bitcast.30), channel_id=1, source_target_pairs={{0,480},{32,0},{64,32},{96,64},{128,96},{160,128},{192,160},{224,1... | collective-permute-start | bytes 1376264 | tf_op jit(solution)/shard_map/ppermute | solution.py:39
  226.3 10.0 %collective-permute-done.14 = bf16[1,64,3584]{2,1,0:T(8,128)(2,1)S(1)} collective-permute-done((bf16[1,64,3584]{2,1,0:T(8,128)(2,1)S(1)}, bf16[1,64,3584]{2,1,0:T(8,128)(2,1)S(1)}, u32[]{:S(2)}, u32[]{:S(2)}) %collective-permute-start.14) | collective-permute-done | bytes 458784 | tf_op jit(solution)/shard_map/ppermute | solution.py:39
  (61 shorter events, 31.2 us)
Async XLA Ops:
  0.6 10.1 %copy-start.11 = (s32[1,64,1]{1,2,0:T(1,128)S(1)}, s32[1,64,1]{1,2,0:T(1,128)}, u32[]{:S(2)}) copy-start(s32[1,64,1]{1,2,0:T(1,128)} %param.13) | copy-start | bytes 772
  0.6 16.8 %collective-permute-start = (bf16[1792,256]{1,0:T(8,128)(2,1)}, bf16[1792,256]{1,0:T(8,128)(2,1)}, u32[]{:S(2)}, u32[]{:S(2)}) collective-permute-start(bf16[1792,256]{1,0:T(8,128)(2,1)} %bitcast.35), channel_id=1, source_target_pairs={{1,4},{3,6},{4,1},{6,3},{9,12},{11,14},{12,9},{14,11},{17,20},{19,... | collective-permute-start | bytes 2752520 | tf_op jit(solution)/shard_map/ppermute | solution.py:26
  6.0 21.2 %collective-permute-start.1 = (bf16[256,1792]{1,0:T(8,128)(2,1)}, bf16[256,1792]{1,0:T(8,128)(2,1)}, u32[]{:S(2)}, u32[]{:S(2)}) collective-permute-start(bf16[256,1792]{1,0:T(8,128)(2,1)} %bitcast.7), channel_id=1, source_target_pairs={{1,4},{3,6},{4,1},{6,3},{9,12},{11,14},{12,9},{14,11},{17,20},{19,... | collective-permute-start | bytes 2752520 | tf_op jit(solution)/shard_map/ppermute | solution.py:26
  53.0 50.9 %all-to-all-start.2 = ((bf16[8,40,1792]{2,1,0:T(8,128)(2,1)}), bf16[8,40,1792]{2,1,0:T(8,128)(2,1)}, u32[]{:S(2)}, u32[]{:S(2)}) async-start(bf16[8,40,1792]{2,1,0:T(8,128)(2,1)} %shard_map.105), calls=%async_computation.2 | async-start | bytes 2293760 | tf_op jit(solution)/shard_map/all_to_all | solution.py:47
  57.4 18.4 %collective-permute-start.3 = (bf16[1792,256]{1,0:T(8,128)(2,1)S(1)}, bf16[1792,256]{1,0:T(8,128)(2,1)}, u32[]{:S(2)}, u32[]{:S(2)}) collective-permute-start(bf16[1792,256]{1,0:T(8,128)(2,1)S(1)} %bitcast.36), channel_id=1, source_target_pairs={{0,2},{2,0},{5,7},{7,5},{8,10},{10,8},{13,15},{15,13},{16,18},{18,... | collective-permute-start | bytes 2752520 | tf_op jit(solution)/shard_map/ppermute | solution.py:26
  59.0 55.1 %collective-permute-start.6 = (bf16[256,1792]{1,0:T(8,128)(2,1)}, bf16[256,1792]{1,0:T(8,128)(2,1)}, u32[]{:S(2)}, u32[]{:S(2)}) collective-permute-start(bf16[256,1792]{1,0:T(8,128)(2,1)} %bitcast.7), channel_id=1, source_target_pairs={{0,2},{2,0},{5,7},{7,5},{8,10},{10,8},{13,15},{15,13},{16,18},{18,... | collective-permute-start | bytes 2752520 | tf_op jit(solution)/shard_map/ppermute | solution.py:26
  60.6 38.2 %collective-permute-start.4 = (bf16[1792,256]{1,0:T(8,128)(2,1)}, bf16[1792,256]{1,0:T(8,128)(2,1)S(1)}, u32[]{:S(2)}, u32[]{:S(2)}) collective-permute-start(bf16[1792,256]{1,0:T(8,128)(2,1)} %collective-permute-done), channel_id=1, source_target_pairs={{1,3},{3,1},{4,6},{6,4},{9,11},{11,9},{12,14},{14,12},{17,19},{19,... | collective-permute-start | bytes 2752520 | tf_op jit(solution)/shard_map/ppermute | solution.py:26
  68.1 79.8 %collective-permute-start.7 = (bf16[256,1792]{1,0:T(8,128)(2,1)}, bf16[256,1792]{1,0:T(8,128)(2,1)}, u32[]{:S(2)}, u32[]{:S(2)}) collective-permute-start(bf16[256,1792]{1,0:T(8,128)(2,1)} %collective-permute-done.1), channel_id=1, source_target_pairs={{1,3},{3,1},{4,6},{6,4},{9,11},{11,9},{12,14},{14,12},{17,19},{19,... | collective-permute-start | bytes 2752520 | tf_op jit(solution)/shard_map/ppermute | solution.py:26
  71.3 27.6 %collective-permute-start.2 = (bf16[320,896]{1,0:T(8,128)(2,1)S(1)}, bf16[320,896]{1,0:T(8,128)(2,1)S(1)}, u32[]{:S(2)}, u32[]{:S(2)}) collective-permute-start(bf16[320,896]{1,0:T(8,128)(2,1)S(1)} %bitcast.24), channel_id=1, source_target_pairs={{0,1},{1,0},{2,3},{3,2},{4,5},{5,4},{6,7},{7,6},{8,9},{9,8},{10,11... | collective-permute-start | bytes 1720328 | tf_op jit(solution)/shard_map/ppermute | solution.py:26
  102.0 47.2 %collective-permute-start.5 = (bf16[320,512]{1,0:T(8,128)(2,1)}, bf16[320,512]{1,0:T(8,128)(2,1)S(1)}, u32[]{:S(2)}, u32[]{:S(2)}) collective-permute-start(bf16[320,512]{1,0:T(8,128)(2,1)} %get-tuple-element.16), channel_id=1, source_target_pairs={{0,4},{1,5},{2,6},{3,7},{4,0},{5,1},{6,2},{7,3},{8,12},{9,13},{10,... | collective-permute-start | bytes 983048 | tf_op jit(solution)/shard_map/ppermute | solution.py:26
  103.9 45.3 %copy-start.7 = (f32[320,512]{1,0:T(8,128)S(1)}, f32[320,512]{1,0:T(8,128)}, u32[]{:S(2)}) copy-start(f32[320,512]{1,0:T(8,128)} %copy-done.6) | copy-start | bytes 1966084
  103.9 58.1 %collective-permute-start.10 = (bf16[320,1792]{1,0:T(8,128)(2,1)}, bf16[320,1792]{1,0:T(8,128)(2,1)}, u32[]{:S(2)}, u32[]{:S(2)}) collective-permute-start(bf16[320,1792]{1,0:T(8,128)(2,1)} %bitcast.13.own), channel_id=1, source_target_pairs={{0,1},{1,0},{2,3},{3,2},{4,5},{5,4},{6,7},{7,6},{8,9},{9,8},{10,11... | collective-permute-start | bytes 3440648 | tf_op jit(solution)/shard_map/ppermute | solution.py:26
  150.1 3.9 %collective-permute-start.8 = (bf16[160,1792]{1,0:T(8,128)(2,1)S(1)}, bf16[160,1792]{1,0:T(8,128)(2,1)S(1)}, u32[]{:S(2)}, u32[]{:S(2)}) collective-permute-start(bf16[160,1792]{1,0:T(8,128)(2,1)S(1)} %get-tuple-element.18), channel_id=1, source_target_pairs={{0,1},{1,0},{2,3},{3,2},{4,5},{5,4},{6,7},{7,6},{8,9},{9,8},{10,11... | collective-permute-start | bytes 1720328 | tf_op jit(solution)/shard_map/ppermute | solution.py:26
  155.3 42.0 %all-to-all-start.1 = ((bf16[8,40,896]{2,1,0:T(8,128)(2,1)}), bf16[8,40,896]{2,1,0:T(8,128)(2,1)S(1)}, u32[]{:S(2)}, u32[]{:S(2)}) async-start(bf16[8,40,896]{2,1,0:T(8,128)(2,1)} %bitcast.9), calls=%async_computation.1 | async-start | bytes 1146880 | tf_op jit(solution)/shard_map/all_to_all | solution.py:47
  168.0 15.2 %collective-permute-start.11 = (bf16[320,512]{1,0:T(8,128)(2,1)S(1)}, bf16[320,512]{1,0:T(8,128)(2,1)S(1)}, u32[]{:S(2)}, u32[]{:S(2)}) collective-permute-start(bf16[320,512]{1,0:T(8,128)(2,1)S(1)} %get-tuple-element.21), channel_id=1, source_target_pairs={{0,4},{1,5},{2,6},{3,7},{4,0},{5,1},{6,2},{7,3},{8,12},{9,13},{10,... | collective-permute-start | bytes 983048 | tf_op jit(solution)/shard_map/ppermute | solution.py:26
  171.3 18.8 %collective-permute-start.12 = (bf16[320,512]{1,0:T(8,128)(2,1)S(1)}, bf16[320,512]{1,0:T(8,128)(2,1)S(1)}, u32[]{:S(2)}, u32[]{:S(2)}) collective-permute-start(bf16[320,512]{1,0:T(8,128)(2,1)S(1)} %get-tuple-element.23), channel_id=1, source_target_pairs={{0,4},{1,5},{2,6},{3,7},{4,0},{5,1},{6,2},{7,3},{8,12},{9,13},{10,... | collective-permute-start | bytes 983048 | tf_op jit(solution)/shard_map/ppermute | solution.py:26
  191.0 5.0 %collective-permute-start.13 = (bf16[160,1792]{1,0:T(8,128)(2,1)S(1)}, bf16[160,1792]{1,0:T(8,128)(2,1)S(1)}, u32[]{:S(2)}, u32[]{:S(2)}) collective-permute-start(bf16[160,1792]{1,0:T(8,128)(2,1)S(1)} %get-tuple-element.25), channel_id=1, source_target_pairs={{0,1},{1,0},{2,3},{3,2},{4,5},{5,4},{6,7},{7,6},{8,9},{9,8},{10,11... | collective-permute-start | bytes 1720328 | tf_op jit(solution)/shard_map/ppermute | solution.py:26
  197.3 5.7 %copy-start.14 = (f32[1,64,1]{1,2,0:T(1,128)S(1)}, f32[1,64,1]{1,2,0:T(1,128)}, u32[]{:S(2)}) copy-start(f32[1,64,1]{1,2,0:T(1,128)} %param.15) | copy-start | bytes 772
  197.3 5.8 %copy-start.3 = (bf16[1,64,3584]{2,1,0:T(8,128)(2,1)S(1)}, bf16[1,64,3584]{2,1,0:T(8,128)(2,1)}, u32[]{:S(2)}) copy-start(bf16[1,64,3584]{2,1,0:T(8,128)(2,1)} %param.9) | copy-start | bytes 1376260
  197.3 5.8 %copy-start.10 = (s32[1,64,1]{1,2,0:T(1,128)S(1)}, s32[1,64,1]{1,2,0:T(1,128)}, u32[]{:S(2)}) copy-start(s32[1,64,1]{1,2,0:T(1,128)} %param.12) | copy-start | bytes 772
  197.3 24.6 %copy-start.5 = (bf16[1,64,3584]{2,1,0:T(8,128)(2,1)S(1)}, bf16[1,64,3584]{2,1,0:T(8,128)(2,1)}, u32[]{:S(2)}) copy-start(bf16[1,64,3584]{2,1,0:T(8,128)(2,1)} %param.11) | copy-start | bytes 1376260
  197.4 24.6 %all-to-all-start.3 = ((bf16[8,40,896]{2,1,0:T(8,128)(2,1)}), bf16[8,40,896]{2,1,0:T(8,128)(2,1)S(1)}, u32[]{:S(2)}, u32[]{:S(2)}) async-start(bf16[8,40,896]{2,1,0:T(8,128)(2,1)} %bitcast.14), calls=%async_computation.3 | async-start | bytes 1146880 | tf_op jit(solution)/shard_map/all_to_all | solution.py:47
  204.0 22.3 %collective-permute-start.9 = (bf16[1,64,3584]{2,1,0:T(8,128)(2,1)S(1)}, bf16[1,64,3584]{2,1,0:T(8,128)(2,1)S(1)}, u32[]{:S(2)}, u32[]{:S(2)}) collective-permute-start(bf16[1,64,3584]{2,1,0:T(8,128)(2,1)S(1)} %bitcast.29), channel_id=1, source_target_pairs={{0,32},{32,64},{64,96},{96,128},{128,160},{160,192},{192,224},{224... | collective-permute-start | bytes 1376264 | tf_op jit(solution)/shard_map/ppermute | solution.py:39
  222.8 13.5 %collective-permute-start.14 = (bf16[1,64,3584]{2,1,0:T(8,128)(2,1)S(1)}, bf16[1,64,3584]{2,1,0:T(8,128)(2,1)S(1)}, u32[]{:S(2)}, u32[]{:S(2)}) collective-permute-start(bf16[1,64,3584]{2,1,0:T(8,128)(2,1)S(1)} %bitcast.30), channel_id=1, source_target_pairs={{0,480},{32,0},{64,32},{96,64},{128,96},{160,128},{192,160},{224,1... | collective-permute-start | bytes 1376264 | tf_op jit(solution)/shard_map/ppermute | solution.py:39
  (9 other events, 17.0 us)

commit v2 on v1

v2 whole, which is shorter than its diff:
```python
import jax
import jax.numpy as jnp
from jax import lax
from jax.experimental import pallas as pl
from jax.experimental.pallas import tpu as pltpu
from jax.sharding import PartitionSpec as P

EXPERTS = 4
CAP = 20
RINGS = 8
F32 = jnp.float32
BF16 = jnp.bfloat16
NN = (((1,), (0,)), ((), ()))
NT = (((1,), (1,)), ((), ()))
TN = (((0,), (0,)), ((), ()))
CORE, PLANE, PAIR = 1, 2, 4
LIMIT = 32 * 1024 * 1024


def dot(left, right, dims=NN):
    return lax.dot_general(left, right, dims, preferred_element_type=F32)


def swap(value, mask, other=None):
    count = lax.axis_size("expert")
    masks = [mask if other is None or keeps(i) else other for i in range(count)]
    return lax.ppermute(value, "expert", [(i, i ^ m) for i, m in enumerate(masks) if m])


def keeps(index):
    return (index >> 2 & 1) == (index & 1)


def from_behind(value, steps):
    count = lax.axis_size("pipe")
    return lax.ppermute(value, "pipe", [(i, (i + steps) % count) for i in range(count)])


def ring_exchange(value):
    count = lax.axis_size("expert")
    rings = count // 4
    groups = [[z * 4 + b for z in range(rings)] for b in range(4)]
    cut = value.reshape(rings, -1, value.shape[-1])
    got = lax.all_to_all(cut, "expert", split_axis=0, concat_axis=0, tiled=True, axis_index_groups=groups)
    return got.reshape(value.shape)


def call(body, outs, *args, after=(), flag=None):
    shapes = [jax.ShapeDtypeStruct(s, d) for s, d in outs]
    flags = () if flag is None else (flag,)
    lead = [pl.BlockSpec(memory_space=pltpu.SMEM) for _ in flags]
    lead += [pl.BlockSpec(memory_space=pl.ANY) for _ in after]

    def run(*refs):
        body(*refs[: len(flags)], *refs[len(flags) + len(after) :])

    args = (*flags, *after, *args)
    return pl.pallas_call(
        run,
        out_shape=shapes,
        in_specs=lead + [pl.BlockSpec(memory_space=pltpu.VMEM) for _ in args[len(lead) :]],
        out_specs=[pl.BlockSpec(memory_space=pltpu.VMEM) for _ in outs],
        compiler_params=pltpu.CompilerParams(vmem_limit_bytes=LIMIT),
    )(*args)


def senders(routes, expert):
    count = routes.shape[1]
    mine = jnp.broadcast_to(routes == expert, (2 * CAP, count))
    upto = lax.broadcasted_iota(jnp.int32, (count, count), 0) <= lax.broadcasted_iota(jnp.int32, (count, count), 1)
    rank = dot(mine.astype(F32).astype(BF16), upto.astype(F32).astype(BF16)).astype(jnp.int32) - 1
    row = lax.broadcasted_iota(jnp.int32, (2 * CAP, count), 0)
    low = mine & (rank == row)
    high = mine & (rank == row - CAP)
    return low.astype(F32).astype(BF16), high.astype(F32).astype(BF16)


def pack_body(routes, low_rows, high_rows, out):
    wide = out.shape[2]
    step = low_rows.shape[1] // 2
    shift = 0 if high_rows.shape[1] == wide * 2 else wide
    for e in range(EXPERTS):
        low, high = senders(routes[...], e)
        for h in range(2):
            part = dot(low, low_rows[:, pl.ds(h * step, wide)])
            part += dot(high, high_rows[:, pl.ds(h * step + shift, wide)])
            out[2 * e + h] = part.astype(BF16)


def halves(rows):
    row = lax.broadcasted_iota(jnp.int32, (rows // 2, rows), 0)
    col = lax.broadcasted_iota(jnp.int32, (rows // 2, rows), 1)
    block = row // CAP
    low = col == row + block * CAP
    high = col == row + block * CAP + CAP
    return low.astype(F32).astype(BF16), high.astype(F32).astype(BF16)


def choose(flag, body, *weights):
    keep = flag[0] == 1
    pl.when(keep)(lambda: body(*[w[:-1] for w in weights]))
    pl.when(jnp.logical_not(keep))(lambda: body(*[w[1:] for w in weights]))


def act_fwd_body(flag, own, other, *refs):
    *w_in, act, sent = refs
    rows, wide = own.shape
    low, high = halves(rows)

    def run(pieces):
        for k, ref in enumerate((own, other)):
            a = dot(low, ref[...]).astype(BF16)
            b = dot(high, ref[...]).astype(BF16)
            at = pl.ds(k * (rows // 2), rows // 2)
            for q, w in enumerate(pieces):
                n = w.shape[1]
                part = dot(a, w[pl.ds(0, wide), :]) + dot(b, w[pl.ds(wide, wide), :])
                act[at, pl.ds(q * n, n)] = part
                sent[at, pl.ds(q * n, n)] = part.astype(BF16)

    choose(flag, run, w_in)


def act_bwd_body(flag, own, other, *refs):
    *w_in, act, sent = refs
    low, _ = halves(own.shape[0])
    many = low.shape[0]

    def run(pieces):
        for k, ref in enumerate((own, other)):
            v = dot(low, ref[...]).astype(BF16)
            for q, w in enumerate(pieces):
                at = (pl.ds(k * many, many), pl.ds(q * w.shape[1], w.shape[1]))
                part = dot(v, w[...])
                act[at] = part
                sent[at] = part.astype(BF16)

    choose(flag, run, w_in)


def grad_body(flag, own, other, *refs):
    *w_out, grad, sent = refs
    _, high = halves(own.shape[0])
    many = high.shape[0]

    def run(pieces):
        for k, ref in enumerate((own, other)):
            c = dot(high, ref[...]).astype(BF16)
            for q, w in enumerate(pieces):
                at = (pl.ds(k * many, many), pl.ds(q * w.shape[0], w.shape[0]))
                part = dot(c, w[...], NT)
                grad[at] = part
                sent[at] = part.astype(BF16)

    choose(flag, run, w_out)


def out_body(flag, act_f, got_f, act_b, got_b, grad1, got_grad1, grad2, got_grad2, *refs):
    w_in, w_out = refs[:3], refs[3:6]
    own, sent = refs[6:]
    n = grad1.shape[1]
    half = own.shape[0] // 2
    a = act_f[...] + got_f[...].astype(F32)
    h = (a * jax.nn.sigmoid(a)).astype(BF16)
    r = []
    for q, (grad, got) in enumerate(((grad1, got_grad1), (grad2, got_grad2))):
        at = pl.ds(q * n, n)
        a = act_b[:, at] + got_b[:, at].astype(F32)
        g = grad[...] + got[...].astype(F32)
        s = jax.nn.sigmoid(a)
        r.append((g * s * (1.0 + a * (1.0 - s))).astype(BF16))

    def run(ins, outs):
        o = dot(h[:, :n], outs[0][...]) + dot(h[:, n:], outs[1][...])
        u = dot(r[0], ins[0][...], NT) + dot(r[1], ins[1][...], NT)
        for k, part in enumerate((o, u)):
            at = pl.ds(k * half, half)
            own[at, :] = part[:half]
            sent[at, :] = part[half:].astype(BF16)

    choose(flag, run, w_in, w_out)


def finish_body(own, got, out):
    total = (own[...] + got[...].astype(F32)).astype(BF16)
    low, high = halves(out.shape[0])
    half = total.shape[0] // 2
    out[...] = (dot(low, total[:half], TN) + dot(high, total[half:], TN)).astype(BF16)


def merge_body(routes_f, routes_b, probs_f, probs_b, rows_f, rows_c, got, y, dx):
    wide = got.shape[1]
    block = 2 * CAP
    for k, (routes, probs, rows, out) in enumerate(((routes_f, probs_f, rows_f, y), (routes_b, probs_b, rows_c, dx))):
        pick = [senders(routes[...], e)[k] for e in range(EXPERTS)]
        for h in range(2):
            total = None
            for e in range(EXPERTS):
                part = dot(pick[e], got[pl.ds((2 * e + h) * block, block), :], TN)
                total = part if total is None else total + part
            at = pl.ds(h * wide, wide)
            out[:, at] = (rows[:, at].astype(F32) + probs[...] * total).astype(BF16)


def local(
    fwd_tokens,
    bwd_tokens,
    bwd_cotangent,
    fwd_routes,
    bwd_routes,
    fwd_probs,
    bwd_probs,
    expert_in,
    expert_out,
):
    rings = lax.axis_size("expert") // 4
    index = lax.axis_index("expert")
    keep = (index >> 2 & 1) == (index & 1)
    own_in, own_out = expert_in[0, 0], expert_out[0, 0]
    features, hidden = own_in.shape
    quarter = features // 2
    slots = rings * CAP
    tokens = fwd_tokens.shape[1]
    rows_f, rows_b, rows_c = fwd_tokens[0], bwd_tokens[0], bwd_cotangent[0]
    routes_f, routes_b = fwd_routes.reshape(1, tokens), bwd_routes.reshape(1, tokens)
    probs_f, probs_b = fwd_probs.reshape(tokens, 1), bwd_probs.reshape(tokens, 1)

    m_in = swap(own_in, PLANE, PAIR | CORE)
    m_out = swap(own_out, PLANE, PAIR | CORE)
    v_in, v_out = swap(m_in, 0, PLANE), swap(m_out, 0, PLANE)
    w_in, w_out = (own_in, m_in, v_in), (own_out, m_out, v_out)
    flag = keep.astype(jnp.int32).reshape(1)

    (send_f,) = call(pack_body, [((2 * EXPERTS, 2 * CAP, quarter), BF16)], routes_f, rows_f, rows_f)
    (send_b,) = call(pack_body, [((2 * EXPERTS, 2 * CAP, features), BF16)], routes_b, rows_b, rows_c)
    got_b = ring_exchange(send_b).reshape(2 * slots, features)
    send_f, got_b = lax.optimization_barrier((send_f, got_b))
    got_f = ring_exchange(send_f).reshape(2 * slots, quarter)

    pre, piece = (2 * slots, 2 * hidden), (2 * slots, hidden)
    far_b = swap(got_b, CORE)
    grad1, sent_g1 = call(grad_body, [(piece, F32), (piece, BF16)], got_b, far_b, own_out, m_out, flag=flag)
    back_g1 = swap(sent_g1, PAIR)
    act_b, sent_a = call(act_bwd_body, [(pre, F32), (pre, BF16)], got_b, far_b, *w_in, flag=flag)
    back_a = swap(sent_a, PAIR)
    far_f = swap(got_f, CORE)
    act_f, sent_f = call(act_fwd_body, [(pre, F32), (pre, BF16)], got_f, far_f, *w_in, flag=flag)
    back_f = swap(sent_f, PAIR)
    v_out, sent_f, sent_a, back_g1 = lax.optimization_barrier((v_out, sent_f, sent_a, back_g1))
    grad2, sent_g2 = call(grad_body, [(piece, F32), (piece, BF16)], got_b, far_b, m_out, v_out, flag=flag)
    back_g2 = swap(sent_g2, PAIR)
    own, cross = call(
        out_body,
        [((2 * slots, features), F32), ((2 * slots, features), BF16)],
        *(act_f, back_f, act_b, back_a, grad1, back_g1, grad2, back_g2, *w_in, *w_out),
        flag=flag,
    )
    (ret,) = call(finish_body, [((2 * slots, features), BF16)], own, swap(cross, CORE))
    home = ring_exchange(ret)
    shape = (tokens, 2 * features)
    y, dx = call(
        merge_body, [(shape, BF16), (shape, BF16)], routes_f, routes_b, probs_f, probs_b, rows_f, rows_c, home
    )
    return from_behind(y[None], 1), from_behind(dx[None], -1)


def solution(mesh):
    row = P("pipe", "expert", None)
    block = P("pipe", "expert", None, None)
    return jax.shard_map(
        local,
        mesh=mesh,
        in_specs=(row,) * 7 + (block,) * 2,
        out_specs=(row, row),
        check_vma=False,
    )
```

time: 241 us -> 194 us (0.80)
  blocking collectives: 25.8 us -> 0 us
  waiting for transfers between devices: 116 us -> 92.6 us
  Pallas kernels: 16.5 us -> 24.3 us
  other arithmetic: 4.22 us -> 0 us
    ppermute x13 -> x11, waiting for transfers between devices: 91.2 us -> 20.9 us  [swap(): lax.ppermute(value, 'expert', [(i, i ^ m) for i, m in enumerate(masks) if...]
    all_to_all x3, waiting for transfers between devices: 14.7 us -> 55.1 us  [ring_exchange(): lax.all_to_all(cut, 'expert', split_axis=0, concat_axis=0, tiled=True, ax...]
    all_to_all x1 -> x0, blocking collectives: 25.8 us -> none  [ring_exchange(): lax.all_to_all(cut, 'expert', split_axis=0, concat_axis=0, tiled=True, ax...]
    pallas_call x10 -> x9, Pallas kernels: 16.5 us -> 24.3 us  [call(): pl.pallas_call(run, out_shape=shapes, in_specs=lead + [pl.BlockSpec(memor...]
    ppermute x13 -> x11, starting transfers between devices: 45.5 us -> 38.5 us  [swap(): lax.ppermute(value, 'expert', [(i, i ^ m) for i, m in enumerate(masks) if...]
    ppermute x2, waiting for transfers between devices: 9.97 us -> 16.7 us  [from_behind(): lax.ppermute(value, 'pipe', [(i, (i + steps) % count) for i in range(coun...]
    all_to_all x3, starting transfers between devices: 16.7 us -> 21.1 us  [ring_exchange(): lax.all_to_all(cut, 'expert', split_axis=0, concat_axis=0, tiled=True, ax...]
    ppermute x2, starting transfers between devices: 6.74 us -> 11 us  [from_behind(): lax.ppermute(value, 'pipe', [(i, (i + steps) % count) for i in range(coun...]
  transfers between devices with their start and end apart: 18 -> 16, of which waited for: 10 -> 9; matrix products, arithmetic and copies ran while one was open for 2% -> 0% of each run, Pallas kernels for 7% -> 7%
where the time goes in v2:
time: 194 us; the launch traced here: 193 us
  waiting for transfers between devices  92.6 us (48%)
  starting transfers between devices  70.6 us (36%)
  Pallas kernels  24.3 us (13%)
  local copies, waits for them, and re-layouts  4.44 us (2%)
    all_to_all x3, waiting for transfers between devices, ring_exchange(): lax.all_to_all(cut, 'expert', split_axis=0, concat_axis=0, tiled=True, ax...  55.1 us
    ppermute x11, starting transfers between devices, swap(): lax.ppermute(value, 'expert', [(i, i ^ m) for i, m in enumerate(masks) if...  38.5 us
    pallas_call x9, Pallas kernels, call(): pl.pallas_call(run, out_shape=shapes, in_specs=lead + [pl.BlockSpec(memor...  24.3 us
    all_to_all x3, starting transfers between devices, ring_exchange(): lax.all_to_all(cut, 'expert', split_axis=0, concat_axis=0, tiled=True, ax...  21.1 us
    ppermute x11, waiting for transfers between devices, swap(): lax.ppermute(value, 'expert', [(i, i ^ m) for i, m in enumerate(masks) if...  20.9 us
    ppermute x2, waiting for transfers between devices, from_behind(): lax.ppermute(value, 'pipe', [(i, (i + steps) % count) for i in range(coun...  16.7 us
    ppermute x2, starting transfers between devices, from_behind(): lax.ppermute(value, 'pipe', [(i, (i + steps) % count) for i in range(coun...  11 us
    unnamed x22, local copies, waits for them, and re-layouts  4.25 us
  transfers between devices with their start and end apart: 16, of which 9 were waited for; matrix products, arithmetic and copies ran while one was open for 0% of the time, Pallas kernels for 7%

profile of v2, /device:TPU:1, one launch (start us, length us, event | category | flops | bytes accessed | tf_op | source)
XLA Modules:
  0.0 192.9 jit_solution(17065763569308350804)
XLA Ops:
  3.3 2.5 %shard_map.105 = bf16[8,40,1792]{2,1,0:T(8,128)(2,1)} custom-call(s32[1,64]{1,0:T(1,128)S(1)} %bitcast.29, bf16[64,3584]{1,0:T(8,128)(2,1)S(1)} %bitcast.26, bf16[64,3584]{1,0:T(8,128)(2,1)S(1)} %bitcast.24), custom_call_target="tpu_custom_call" | custom-call | tf_op jit(solution)/shard_map/pallas_call | solution.py:58
  5.8 11.0 %all-to-all-start = ((bf16[8,40,1792]{2,1,0:T(8,128)(2,1)}), bf16[8,40,1792]{2,1,0:T(8,128)(2,1)S(1)}, u32[]{:S(2)}, u32[]{:S(2)}) async-start(bf16[8,40,1792]{2,1,0:T(8,128)(2,1)} %shard_map.105), calls=%async_computation | async-start | bytes 2293760 | tf_op jit(solution)/shard_map/all_to_all | solution.py:44
  16.8 4.4 %collective-permute-start.1 = (bf16[1792,256]{1,0:T(8,128)(2,1)}, bf16[1792,256]{1,0:T(8,128)(2,1)}, u32[]{:S(2)}, u32[]{:S(2)}) collective-permute-start(bf16[1792,256]{1,0:T(8,128)(2,1)} %bitcast.10.refs_3_.refs_9_), channel_id=1, source_target_pairs={{0,2},{1,4},{2,0},{3,6},{4,1},{5,7},{6,3},{7,5},{8,10},{9,12},{10,... | collective-permute-start | bytes 2752520 | tf_op jit(solution)/shard_map/ppermute | solution.py:27
  25.1 23.0 %all-to-all-done = bf16[8,40,1792]{2,1,0:T(8,128)(2,1)S(1)} async-done(((bf16[8,40,1792]{2,1,0:T(8,128)(2,1)}), bf16[8,40,1792]{2,1,0:T(8,128)(2,1)S(1)}, u32[]{:S(2)}, u32[]{:S(2)}) %all-to-all-start) | async-done | bytes 1146912 | tf_op jit(solution)/shard_map/all_to_all | solution.py:44
  48.2 4.2 %all-to-all-start.1 = ((bf16[8,40,896]{2,1,0:T(8,128)(2,1)}), bf16[8,40,896]{2,1,0:T(8,128)(2,1)}, u32[]{:S(2)}, u32[]{:S(2)}) async-start(bf16[8,40,896]{2,1,0:T(8,128)(2,1)} %shard_map.104), calls=%async_computation.1 | async-start | bytes 1146880 | tf_op jit(solution)/shard_map/all_to_all | solution.py:44
  52.4 2.5 %collective-permute-start.4 = (bf16[320,1792]{1,0:T(8,128)(2,1)S(1)}, bf16[320,1792]{1,0:T(8,128)(2,1)S(1)}, u32[]{:S(2)}, u32[]{:S(2)}) collective-permute-start(bf16[320,1792]{1,0:T(8,128)(2,1)S(1)} %bitcast.16), channel_id=1, source_target_pairs={{0,1},{1,0},{2,3},{3,2},{4,5},{5,4},{6,7},{7,6},{8,9},{9,8},{10,11... | collective-permute-start | bytes 3440648 | tf_op jit(solution)/shard_map/ppermute | solution.py:27
  54.9 7.5 %collective-permute-start.2 = (bf16[1792,256]{1,0:T(8,128)(2,1)}, bf16[1792,256]{1,0:T(8,128)(2,1)}, u32[]{:S(2)}, u32[]{:S(2)}) collective-permute-start(bf16[1792,256]{1,0:T(8,128)(2,1)} %collective-permute-done.1.refs_4_.refs_10_), channel_id=1, source_target_pairs={{1,3},{3,1},{4,6},{6,4},{9,11},{11,9},{12,14},{14,12},{17,19},{19,... | collective-permute-start | bytes 2752520 | tf_op jit(solution)/shard_map/ppermute | solution.py:27
  62.4 9.0 %collective-permute-done.6.refs_4_.refs_3_.refs_13_ = bf16[256,1792]{1,0:T(8,128)(2,1)S(1)} collective-permute-done((bf16[256,1792]{1,0:T(8,128)(2,1)}, bf16[256,1792]{1,0:T(8,128)(2,1)S(1)}, u32[]{:S(2)}, u32[]{:S(2)}) %collective-permute-start.6) | collective-permute-done | bytes 917536 | tf_op jit(solution)/shard_map/ppermute | solution.py:27
  71.4 7.7 %collective-permute-start.7 = (bf16[256,1792]{1,0:T(8,128)(2,1)S(1)}, bf16[256,1792]{1,0:T(8,128)(2,1)}, u32[]{:S(2)}, u32[]{:S(2)}) collective-permute-start(bf16[256,1792]{1,0:T(8,128)(2,1)S(1)} %collective-permute-done.6.refs_4_.refs_3_.refs_13_), channel_id=1, source_target_pairs={{1,3},{3,1},{4,6},{6,4},{9,11},{11,9},{12,14},{14,12},{17,19},{19,... | collective-permute-start | bytes 2752520 | tf_op jit(solution)/shard_map/ppermute | solution.py:27
  82.0 2.6 %shard_map.108 = (f32[320,256]{1,0:T(8,128)S(1)}, bf16[320,256]{1,0:T(8,128)(2,1)S(1)}) custom-call(s32[1]{0:T(128)} %bitcast.6.refs_0_, bf16[320,1792]{1,0:T(8,128)(2,1)S(1)} %bitcast.17, bf16[320,1792]{1,0:T(8,128)(2,1)S(1)} %collective-permute-done.4.refs_2_, bf16[256,1792]{1,0:T(8,128)(2,1)} %bitcast.11.refs_3_.refs_12_, ...), custom_call_target="tpu_custom_call" | custom-call | tf_op jit(solution)/shard_map/pallas_call | solution.py:58
  89.1 3.1 %shard_map.107 = (f32[320,512]{1,0:T(8,128)S(1)}, bf16[320,512]{1,0:T(8,128)(2,1)S(1)}) custom-call(s32[1]{0:T(128)} %bitcast.6.refs_0_, bf16[320,1792]{1,0:T(8,128)(2,1)S(1)} %bitcast.18, bf16[320,1792]{1,0:T(8,128)(2,1)S(1)} %collective-permute-done.4.refs_2_, bf16[1792,256]{1,0:T(8,128)(2,1)} %bitcast.10.refs_3_.refs_9_, ...), custom_call_target="tpu_custom_call" | custom-call | tf_op jit(solution)/shard_map/pallas_call | solution.py:58
  94.1 3.7 %shard_map.106 = (f32[320,512]{1,0:T(8,128)S(1)}, bf16[320,512]{1,0:T(8,128)(2,1)S(1)}) custom-call(s32[1]{0:T(128)} %bitcast.6.refs_0_, bf16[320,896]{1,0:T(8,128)(2,1)} %bitcast.9.refs_1_, bf16[320,896]{1,0:T(8,128)(2,1)} %collective-permute-done.refs_2_, bf16[1792,256]{1,0:T(8,128)(2,1)} %bitcast.10.refs_3_.refs_9_, ...), custom_call_target="tpu_custom_call" | custom-call | tf_op jit(solution)/shard_map/pallas_call | solution.py:58
  97.8 3.4 %collective-permute-start.3 = (bf16[320,512]{1,0:T(8,128)(2,1)S(1)}, bf16[320,512]{1,0:T(8,128)(2,1)S(1)}, u32[]{:S(2)}, u32[]{:S(2)}) collective-permute-start(bf16[320,512]{1,0:T(8,128)(2,1)S(1)} %get-tuple-element.20), channel_id=1, source_target_pairs={{0,4},{1,5},{2,6},{3,7},{4,0},{5,1},{6,2},{7,3},{8,12},{9,13},{10,... | collective-permute-start | bytes 983048 | tf_op jit(solution)/shard_map/ppermute | solution.py:27
  101.2 2.8 %shard_map.109 = (f32[320,256]{1,0:T(8,128)S(1)}, bf16[320,256]{1,0:T(8,128)(2,1)S(1)}) custom-call(s32[1]{0:T(128)} %bitcast.6.refs_0_, bf16[320,1792]{1,0:T(8,128)(2,1)S(1)} %bitcast.19, bf16[320,1792]{1,0:T(8,128)(2,1)S(1)} %collective-permute-done.4.refs_2_, bf16[256,1792]{1,0:T(8,128)(2,1)S(1)} %collective-permute-done.6.refs_4_.refs_3_.refs_13_, ...), custom_call_target="tpu_custom_call" | custom-call | tf_op jit(solution)/shard_map/pallas_call | solution.py:58
  106.0 7.3 %collective-permute-done.9.refs_8_ = bf16[320,256]{1,0:T(8,128)(2,1)S(1)} collective-permute-done((bf16[320,256]{1,0:T(8,128)(2,1)S(1)}, bf16[320,256]{1,0:T(8,128)(2,1)S(1)}, u32[]{:S(2)}, u32[]{:S(2)}) %collective-permute-start.9) | collective-permute-done | bytes 163872 | tf_op jit(solution)/shard_map/ppermute | solution.py:27
  113.3 4.1 %shard_map.110 = (f32[320,1792]{1,0:T(8,128)S(1)}, bf16[320,1792]{1,0:T(8,128)(2,1)S(1)}) custom-call(s32[1]{0:T(128)} %bitcast.6.refs_0_, f32[320,512]{1,0:T(8,128)S(1)} %get-tuple-element.19.refs_1_, bf16[320,512]{1,0:T(8,128)(2,1)S(1)} %collective-permute-done.3.refs_2_, f32[320,512]{1,0:T(8,128)S(1)} %get-tuple-element.22.refs_3_, ...), custom_call_target="tpu_custom_call" | custom-call | tf_op jit(solution)/shard_map/pallas_call | solution.py:58
  117.5 3.0 %collective-permute-start.10 = (bf16[320,1792]{1,0:T(8,128)(2,1)S(1)}, bf16[320,1792]{1,0:T(8,128)(2,1)S(1)}, u32[]{:S(2)}, u32[]{:S(2)}) collective-permute-start(bf16[320,1792]{1,0:T(8,128)(2,1)S(1)} %get-tuple-element.31), channel_id=1, source_target_pairs={{0,1},{1,0},{2,3},{3,2},{4,5},{5,4},{6,7},{7,6},{8,9},{9,8},{10,11... | collective-permute-start | bytes 3440648 | tf_op jit(solution)/shard_map/ppermute | solution.py:27
  120.5 2.4 %collective-permute-done.10.refs_1_ = bf16[320,1792]{1,0:T(8,128)(2,1)S(1)} collective-permute-done((bf16[320,1792]{1,0:T(8,128)(2,1)S(1)}, bf16[320,1792]{1,0:T(8,128)(2,1)S(1)}, u32[]{:S(2)}, u32[]{:S(2)}) %collective-permute-start.10) | collective-permute-done | bytes 1146912 | tf_op jit(solution)/shard_map/ppermute | solution.py:27
  124.7 5.9 %all-to-all-start.2 = ((bf16[8,40,1792]{2,1,0:T(8,128)(2,1)}), bf16[8,40,1792]{2,1,0:T(8,128)(2,1)S(1)}, u32[]{:S(2)}, u32[]{:S(2)}) async-start(bf16[8,40,1792]{2,1,0:T(8,128)(2,1)} %bitcast.12), calls=%async_computation.2 | async-start | bytes 2293760 | tf_op jit(solution)/shard_map/all_to_all | solution.py:44
  130.8 31.2 %all-to-all-done.2 = bf16[8,40,1792]{2,1,0:T(8,128)(2,1)S(1)} async-done(((bf16[8,40,1792]{2,1,0:T(8,128)(2,1)}), bf16[8,40,1792]{2,1,0:T(8,128)(2,1)S(1)}, u32[]{:S(2)}, u32[]{:S(2)}) %all-to-all-start.2) | async-done | bytes 1146912 | tf_op jit(solution)/shard_map/all_to_all | solution.py:44
  163.7 5.4 %collective-permute-start.11 = (bf16[1,64,3584]{2,1,0:T(8,128)(2,1)S(1)}, bf16[1,64,3584]{2,1,0:T(8,128)(2,1)S(1)}, u32[]{:S(2)}, u32[]{:S(2)}) collective-permute-start(bf16[1,64,3584]{2,1,0:T(8,128)(2,1)S(1)} %bitcast.32), channel_id=1, source_target_pairs={{0,32},{32,64},{64,96},{96,128},{128,160},{160,192},{192,224},{224... | collective-permute-start | bytes 1376264 | tf_op jit(solution)/shard_map/ppermute | solution.py:36
  169.0 5.7 %collective-permute-start.12 = (bf16[1,64,3584]{2,1,0:T(8,128)(2,1)S(1)}, bf16[1,64,3584]{2,1,0:T(8,128)(2,1)S(1)}, u32[]{:S(2)}, u32[]{:S(2)}) collective-permute-start(bf16[1,64,3584]{2,1,0:T(8,128)(2,1)S(1)} %bitcast.31), channel_id=1, source_target_pairs={{0,480},{32,0},{64,32},{96,64},{128,96},{160,128},{192,160},{224,1... | collective-permute-start | bytes 1376264 | tf_op jit(solution)/shard_map/ppermute | solution.py:36
  174.7 8.6 %collective-permute-done.11 = bf16[1,64,3584]{2,1,0:T(8,128)(2,1)S(1)} collective-permute-done((bf16[1,64,3584]{2,1,0:T(8,128)(2,1)S(1)}, bf16[1,64,3584]{2,1,0:T(8,128)(2,1)S(1)}, u32[]{:S(2)}, u32[]{:S(2)}) %collective-permute-start.11) | collective-permute-done | bytes 458784 | tf_op jit(solution)/shard_map/ppermute | solution.py:36
  183.3 8.1 %collective-permute-done.12 = bf16[1,64,3584]{2,1,0:T(8,128)(2,1)S(1)} collective-permute-done((bf16[1,64,3584]{2,1,0:T(8,128)(2,1)S(1)}, bf16[1,64,3584]{2,1,0:T(8,128)(2,1)S(1)}, u32[]{:S(2)}, u32[]{:S(2)}) %collective-permute-start.12) | collective-permute-done | bytes 458784 | tf_op jit(solution)/shard_map/ppermute | solution.py:36
  (41 shorter events, 22.9 us)
Async XLA Ops:
  0.6 1.0 copy-start.2
  5.8 17.4 %copy-start = (bf16[1,64,3584]{2,1,0:T(8,128)(2,1)S(1)}, bf16[1,64,3584]{2,1,0:T(8,128)(2,1)}, u32[]{:S(2)}) copy-start(bf16[1,64,3584]{2,1,0:T(8,128)(2,1)} %param.9) | copy-start | bytes 1376260
  5.8 17.4 %copy-start.5 = (s32[1,64,1]{1,2,0:T(1,128)S(1)}, s32[1,64,1]{1,2,0:T(1,128)}, u32[]{:S(2)}) copy-start(s32[1,64,1]{1,2,0:T(1,128)} %param.12) | copy-start | bytes 772
  5.8 42.4 %all-to-all-start = ((bf16[8,40,1792]{2,1,0:T(8,128)(2,1)}), bf16[8,40,1792]{2,1,0:T(8,128)(2,1)S(1)}, u32[]{:S(2)}, u32[]{:S(2)}) async-start(bf16[8,40,1792]{2,1,0:T(8,128)(2,1)} %shard_map.105), calls=%async_computation | async-start | bytes 2293760 | tf_op jit(solution)/shard_map/all_to_all | solution.py:44
  16.8 38.1 %collective-permute-start.1 = (bf16[1792,256]{1,0:T(8,128)(2,1)}, bf16[1792,256]{1,0:T(8,128)(2,1)}, u32[]{:S(2)}, u32[]{:S(2)}) collective-permute-start(bf16[1792,256]{1,0:T(8,128)(2,1)} %bitcast.10.refs_3_.refs_9_), channel_id=1, source_target_pairs={{0,2},{1,4},{2,0},{3,6},{4,1},{5,7},{6,3},{7,5},{8,10},{9,12},{10,... | collective-permute-start | bytes 2752520 | tf_op jit(solution)/shard_map/ppermute | solution.py:27
  21.3 50.1 %collective-permute-start.6 = (bf16[256,1792]{1,0:T(8,128)(2,1)}, bf16[256,1792]{1,0:T(8,128)(2,1)S(1)}, u32[]{:S(2)}, u32[]{:S(2)}) collective-permute-start(bf16[256,1792]{1,0:T(8,128)(2,1)} %bitcast.11.refs_3_.refs_12_), channel_id=1, source_target_pairs={{0,2},{1,4},{2,0},{3,6},{4,1},{5,7},{6,3},{7,5},{8,10},{9,12},{10,... | collective-permute-start | bytes 2752520 | tf_op jit(solution)/shard_map/ppermute | solution.py:27
  48.2 31.9 %all-to-all-start.1 = ((bf16[8,40,896]{2,1,0:T(8,128)(2,1)}), bf16[8,40,896]{2,1,0:T(8,128)(2,1)}, u32[]{:S(2)}, u32[]{:S(2)}) async-start(bf16[8,40,896]{2,1,0:T(8,128)(2,1)} %shard_map.104), calls=%async_computation.1 | async-start | bytes 1146880 | tf_op jit(solution)/shard_map/all_to_all | solution.py:44
  52.4 29.6 %collective-permute-start.4 = (bf16[320,1792]{1,0:T(8,128)(2,1)S(1)}, bf16[320,1792]{1,0:T(8,128)(2,1)S(1)}, u32[]{:S(2)}, u32[]{:S(2)}) collective-permute-start(bf16[320,1792]{1,0:T(8,128)(2,1)S(1)} %bitcast.16), channel_id=1, source_target_pairs={{0,1},{1,0},{2,3},{3,2},{4,5},{5,4},{6,7},{7,6},{8,9},{9,8},{10,11... | collective-permute-start | bytes 3440648 | tf_op jit(solution)/shard_map/ppermute | solution.py:27
  54.9 34.2 %collective-permute-start.2 = (bf16[1792,256]{1,0:T(8,128)(2,1)}, bf16[1792,256]{1,0:T(8,128)(2,1)}, u32[]{:S(2)}, u32[]{:S(2)}) collective-permute-start(bf16[1792,256]{1,0:T(8,128)(2,1)} %collective-permute-done.1.refs_4_.refs_10_), channel_id=1, source_target_pairs={{1,3},{3,1},{4,6},{6,4},{9,11},{11,9},{12,14},{14,12},{17,19},{19,... | collective-permute-start | bytes 2752520 | tf_op jit(solution)/shard_map/ppermute | solution.py:27
  71.4 29.8 %collective-permute-start.7 = (bf16[256,1792]{1,0:T(8,128)(2,1)S(1)}, bf16[256,1792]{1,0:T(8,128)(2,1)}, u32[]{:S(2)}, u32[]{:S(2)}) collective-permute-start(bf16[256,1792]{1,0:T(8,128)(2,1)S(1)} %collective-permute-done.6.refs_4_.refs_3_.refs_13_), channel_id=1, source_target_pairs={{1,3},{3,1},{4,6},{6,4},{9,11},{11,9},{12,14},{14,12},{17,19},{19,... | collective-permute-start | bytes 2752520 | tf_op jit(solution)/shard_map/ppermute | solution.py:27
  80.0 14.1 %collective-permute-start = (bf16[320,896]{1,0:T(8,128)(2,1)}, bf16[320,896]{1,0:T(8,128)(2,1)}, u32[]{:S(2)}, u32[]{:S(2)}) collective-permute-start(bf16[320,896]{1,0:T(8,128)(2,1)} %bitcast.9.refs_1_), channel_id=1, source_target_pairs={{0,1},{1,0},{2,3},{3,2},{4,5},{5,4},{6,7},{7,6},{8,9},{9,8},{10,11... | collective-permute-start | bytes 1720328 | tf_op jit(solution)/shard_map/ppermute | solution.py:27
  84.6 16.6 %collective-permute-start.8 = (bf16[320,256]{1,0:T(8,128)(2,1)S(1)}, bf16[320,256]{1,0:T(8,128)(2,1)S(1)}, u32[]{:S(2)}, u32[]{:S(2)}) collective-permute-start(bf16[320,256]{1,0:T(8,128)(2,1)S(1)} %get-tuple-element.25), channel_id=1, source_target_pairs={{0,4},{1,5},{2,6},{3,7},{4,0},{5,1},{6,2},{7,3},{8,12},{9,13},{10,... | collective-permute-start | bytes 491528 | tf_op jit(solution)/shard_map/ppermute | solution.py:27
  92.2 13.8 %collective-permute-start.5 = (bf16[320,512]{1,0:T(8,128)(2,1)S(1)}, bf16[320,512]{1,0:T(8,128)(2,1)S(1)}, u32[]{:S(2)}, u32[]{:S(2)}) collective-permute-start(bf16[320,512]{1,0:T(8,128)(2,1)S(1)} %get-tuple-element.23), channel_id=1, source_target_pairs={{0,4},{1,5},{2,6},{3,7},{4,0},{5,1},{6,2},{7,3},{8,12},{9,13},{10,... | collective-permute-start | bytes 983048 | tf_op jit(solution)/shard_map/ppermute | solution.py:27
  97.8 15.5 %collective-permute-start.3 = (bf16[320,512]{1,0:T(8,128)(2,1)S(1)}, bf16[320,512]{1,0:T(8,128)(2,1)S(1)}, u32[]{:S(2)}, u32[]{:S(2)}) collective-permute-start(bf16[320,512]{1,0:T(8,128)(2,1)S(1)} %get-tuple-element.20), channel_id=1, source_target_pairs={{0,4},{1,5},{2,6},{3,7},{4,0},{5,1},{6,2},{7,3},{8,12},{9,13},{10,... | collective-permute-start | bytes 983048 | tf_op jit(solution)/shard_map/ppermute | solution.py:27
  104.0 9.3 %collective-permute-start.9 = (bf16[320,256]{1,0:T(8,128)(2,1)S(1)}, bf16[320,256]{1,0:T(8,128)(2,1)S(1)}, u32[]{:S(2)}, u32[]{:S(2)}) collective-permute-start(bf16[320,256]{1,0:T(8,128)(2,1)S(1)} %get-tuple-element.29), channel_id=1, source_target_pairs={{0,4},{1,5},{2,6},{3,7},{4,0},{5,1},{6,2},{7,3},{8,12},{9,13},{10,... | collective-permute-start | bytes 491528 | tf_op jit(solution)/shard_map/ppermute | solution.py:27
  117.5 5.4 %collective-permute-start.10 = (bf16[320,1792]{1,0:T(8,128)(2,1)S(1)}, bf16[320,1792]{1,0:T(8,128)(2,1)S(1)}, u32[]{:S(2)}, u32[]{:S(2)}) collective-permute-start(bf16[320,1792]{1,0:T(8,128)(2,1)S(1)} %get-tuple-element.31), channel_id=1, source_target_pairs={{0,1},{1,0},{2,3},{3,2},{4,5},{5,4},{6,7},{7,6},{8,9},{9,8},{10,11... | collective-permute-start | bytes 3440648 | tf_op jit(solution)/shard_map/ppermute | solution.py:27
  124.7 5.9 %copy-start.8 = (f32[1,64,1]{1,2,0:T(1,128)S(1)}, f32[1,64,1]{1,2,0:T(1,128)}, u32[]{:S(2)}) copy-start(f32[1,64,1]{1,2,0:T(1,128)} %param.14) | copy-start | bytes 772
  124.7 6.0 %copy-start.9 = (f32[1,64,1]{1,2,0:T(1,128)S(1)}, f32[1,64,1]{1,2,0:T(1,128)}, u32[]{:S(2)}) copy-start(f32[1,64,1]{1,2,0:T(1,128)} %param.15) | copy-start | bytes 772
  124.7 37.3 %copy-start.1 = (bf16[1,64,3584]{2,1,0:T(8,128)(2,1)S(1)}, bf16[1,64,3584]{2,1,0:T(8,128)(2,1)}, u32[]{:S(2)}) copy-start(bf16[1,64,3584]{2,1,0:T(8,128)(2,1)} %param.9) | copy-start | bytes 1376260
  124.7 37.3 %copy-start.3 = (bf16[1,64,3584]{2,1,0:T(8,128)(2,1)S(1)}, bf16[1,64,3584]{2,1,0:T(8,128)(2,1)}, u32[]{:S(2)}) copy-start(bf16[1,64,3584]{2,1,0:T(8,128)(2,1)} %param.11) | copy-start | bytes 1376260
  124.7 37.3 %copy-start.7 = (s32[1,64,1]{1,2,0:T(1,128)S(1)}, s32[1,64,1]{1,2,0:T(1,128)}, u32[]{:S(2)}) copy-start(s32[1,64,1]{1,2,0:T(1,128)} %param.13) | copy-start | bytes 772
  124.7 37.2 %all-to-all-start.2 = ((bf16[8,40,1792]{2,1,0:T(8,128)(2,1)}), bf16[8,40,1792]{2,1,0:T(8,128)(2,1)S(1)}, u32[]{:S(2)}, u32[]{:S(2)}) async-start(bf16[8,40,1792]{2,1,0:T(8,128)(2,1)} %bitcast.12), calls=%async_computation.2 | async-start | bytes 2293760 | tf_op jit(solution)/shard_map/all_to_all | solution.py:44
  163.7 19.6 %collective-permute-start.11 = (bf16[1,64,3584]{2,1,0:T(8,128)(2,1)S(1)}, bf16[1,64,3584]{2,1,0:T(8,128)(2,1)S(1)}, u32[]{:S(2)}, u32[]{:S(2)}) collective-permute-start(bf16[1,64,3584]{2,1,0:T(8,128)(2,1)S(1)} %bitcast.32), channel_id=1, source_target_pairs={{0,32},{32,64},{64,96},{96,128},{128,160},{160,192},{192,224},{224... | collective-permute-start | bytes 1376264 | tf_op jit(solution)/shard_map/ppermute | solution.py:36
  169.0 22.4 %collective-permute-start.12 = (bf16[1,64,3584]{2,1,0:T(8,128)(2,1)S(1)}, bf16[1,64,3584]{2,1,0:T(8,128)(2,1)S(1)}, u32[]{:S(2)}, u32[]{:S(2)}) collective-permute-start(bf16[1,64,3584]{2,1,0:T(8,128)(2,1)S(1)} %bitcast.31), channel_id=1, source_target_pairs={{0,480},{32,0},{64,32},{96,64},{128,96},{160,128},{192,160},{224,1... | collective-permute-start | bytes 1376264 | tf_op jit(solution)/shard_map/ppermute | solution.py:36
  (2 other events, 1.7 us)

commit v3 on v2

--- a/solution.py
+++ b/solution.py
@@ -7,7 +7,7 @@
 
 EXPERTS = 4
 CAP = 20
-RINGS = 8
+LANES = 128
 F32 = jnp.float32
 BF16 = jnp.bfloat16
 NN = (((1,), (0,)), ((), ()))
@@ -62,6 +62,17 @@
         out_specs=[pl.BlockSpec(memory_space=pltpu.VMEM) for _ in outs],
         compiler_params=pltpu.CompilerParams(vmem_limit_bytes=LIMIT),
     )(*args)
+
+
+def gate(held, *after):
+    return pl.pallas_call(
+        lambda *refs: None,
+        out_shape=jax.ShapeDtypeStruct(held.shape, held.dtype),
+        in_specs=[pl.BlockSpec(memory_space=pl.ANY) for _ in (held, *after)],
+        out_specs=pl.BlockSpec(memory_space=pl.ANY),
+        input_output_aliases={0: 0},
+        cost_estimate=pl.CostEstimate(flops=10**11, bytes_accessed=10**9, transcendentals=0),
+    )(held, *after)
 
 
 def senders(routes, expert):
@@ -75,16 +86,32 @@
     return low.astype(F32).astype(BF16), high.astype(F32).astype(BF16)
 
 
-def pack_body(routes, low_rows, high_rows, out):
+def pack_fwd_body(routes, rows, out):
     wide = out.shape[2]
-    step = low_rows.shape[1] // 2
-    shift = 0 if high_rows.shape[1] == wide * 2 else wide
     for e in range(EXPERTS):
         low, high = senders(routes[...], e)
         for h in range(2):
-            part = dot(low, low_rows[:, pl.ds(h * step, wide)])
-            part += dot(high, high_rows[:, pl.ds(h * step + shift, wide)])
-            out[2 * e + h] = part.astype(BF16)
+            first, second = pl.ds(2 * h * wide, wide), pl.ds((2 * h + 1) * wide, wide)
+            out[2 * e + h] = (dot(low, rows[:, first]) + dot(high, rows[:, second])).astype(BF16)
+
+
+def pack_bwd_body(routes, probs, rows, cots, out):
+    wide = out.shape[2] - LANES
+    lane = lax.broadcasted_iota(jnp.int32, (rows.shape[0], LANES), 1)
+    rest = jnp.broadcast_to(probs[...], lane.shape)
+    weight = jnp.zeros(lane.shape, F32)
+    for k in range(3):
+        part = rest.astype(BF16).astype(F32)
+        weight = jnp.where(lane == k, part, weight)
+        rest = rest - part
+    weight = weight.astype(BF16)
+    for e in range(EXPERTS):
+        low, high = senders(routes[...], e)
+        tail = dot(low, weight).astype(BF16)
+        for h in range(2):
+            at = pl.ds(h * wide, wide)
+            out[2 * e + h, :, pl.ds(0, wide)] = (dot(low, rows[:, at]) + dot(high, cots[:, at])).astype(BF16)
+            out[2 * e + h, :, pl.ds(wide, LANES)] = tail
 
 
 def halves(rows):
@@ -128,7 +155,7 @@
 
     def run(pieces):
         for k, ref in enumerate((own, other)):
-            v = dot(low, ref[...]).astype(BF16)
+            v = dot(low, ref[:, : pieces[0].shape[0]]).astype(BF16)
             for q, w in enumerate(pieces):
                 at = (pl.ds(k * many, many), pl.ds(q * w.shape[1], w.shape[1]))
                 part = dot(v, w[...])
@@ -145,7 +172,7 @@
 
     def run(pieces):
         for k, ref in enumerate((own, other)):
-            c = dot(high, ref[...]).astype(BF16)
+            c = dot(high, ref[:, : pieces[0].shape[1]]).astype(BF16)
             for q, w in enumerate(pieces):
                 at = (pl.ds(k * many, many), pl.ds(q * w.shape[0], w.shape[0]))
                 part = dot(c, w[...], NT)
@@ -181,25 +208,42 @@
     choose(flag, run, w_in, w_out)
 
 
-def finish_body(own, got, out):
-    total = (own[...] + got[...].astype(F32)).astype(BF16)
-    low, high = halves(out.shape[0])
-    half = total.shape[0] // 2
-    out[...] = (dot(low, total[:half], TN) + dot(high, total[half:], TN)).astype(BF16)
-
-
-def merge_body(routes_f, routes_b, probs_f, probs_b, rows_f, rows_c, got, y, dx):
+def finish_body(own, got, sent, out_f, out_b):
+    low, high = halves(out_f.shape[0])
+    wide = out_f.shape[1]
+    half = own.shape[0] // 2
+    total = own[...] + got[...].astype(F32)
+    weight = jnp.sum(dot(low, sent[:, 2 * wide :]), axis=1, keepdims=True)
+    ready = (dot(high, sent[:, : 2 * wide]) + weight * total[half:]).astype(BF16)
+    for rows, out in ((total[:half].astype(BF16), out_f), (ready, out_b)):
+        out[...] = (dot(low, rows[:, :wide], TN) + dot(high, rows[:, wide:], TN)).astype(BF16)
+
+
+def homing(routes, got, place):
     wide = got.shape[1]
     block = 2 * CAP
-    for k, (routes, probs, rows, out) in enumerate(((routes_f, probs_f, rows_f, y), (routes_b, probs_b, rows_c, dx))):
-        pick = [senders(routes[...], e)[k] for e in range(EXPERTS)]
-        for h in range(2):
+    picks = [senders(routes[...], e) for e in range(EXPERTS)]
+    for h in range(2):
+        for q in range(2):
             total = None
             for e in range(EXPERTS):
-                part = dot(pick[e], got[pl.ds((2 * e + h) * block, block), :], TN)
+                part = dot(picks[e][q], got[pl.ds((2 * e + h) * block, block), :], TN)
                 total = part if total is None else total + part
-            at = pl.ds(h * wide, wide)
-            out[:, at] = (rows[:, at].astype(F32) + probs[...] * total).astype(BF16)
+            place(pl.ds((2 * h + q) * wide, wide), total)
+
+
+def merge_fwd_body(routes, probs, rows, got, out):
+    def place(at, total):
+        out[:, at] = (rows[:, at].astype(F32) + probs[...] * total).astype(BF16)
+
+    homing(routes, got, place)
+
+
+def merge_bwd_body(routes, got, out):
+    def place(at, total):
+        out[:, at] = total.astype(BF16)
+
+    homing(routes, got, place)
 
 
 def local(
@@ -227,14 +271,18 @@
 
     m_in = swap(own_in, PLANE, PAIR | CORE)
     m_out = swap(own_out, PLANE, PAIR | CORE)
-    v_in, v_out = swap(m_in, 0, PLANE), swap(m_out, 0, PLANE)
+    v_in = swap(m_in, 0, PLANE)
+    early_out, v_in = lax.optimization_barrier((m_out, v_in))
+    v_out = swap(early_out, 0, PLANE)
     w_in, w_out = (own_in, m_in, v_in), (own_out, m_out, v_out)
     flag = keep.astype(jnp.int32).reshape(1)
 
-    (send_f,) = call(pack_body, [((2 * EXPERTS, 2 * CAP, quarter), BF16)], routes_f, rows_f, rows_f)
-    (send_b,) = call(pack_body, [((2 * EXPERTS, 2 * CAP, features), BF16)], routes_b, rows_b, rows_c)
-    got_b = ring_exchange(send_b).reshape(2 * slots, features)
-    send_f, got_b = lax.optimization_barrier((send_f, got_b))
+    (send_f,) = call(pack_fwd_body, [((2 * EXPERTS, 2 * CAP, quarter), BF16)], routes_f, rows_f)
+    (send_b,) = call(
+        pack_bwd_body, [((2 * EXPERTS, 2 * CAP, features + LANES), BF16)], routes_b, probs_b, rows_b, rows_c
+    )
+    got_b = ring_exchange(send_b).reshape(2 * slots, features + LANES)
+    send_f, got_b = lax.optimization_barrier((gate(send_f, m_in), got_b))
     got_f = ring_exchange(send_f).reshape(2 * slots, quarter)
 
     pre, piece = (2 * slots, 2 * hidden), (2 * slots, hidden)
@@ -255,13 +303,15 @@
         *(act_f, back_f, act_b, back_a, grad1, back_g1, grad2, back_g2, *w_in, *w_out),
         flag=flag,
     )
-    (ret,) = call(finish_body, [((2 * slots, features), BF16)], own, swap(cross, CORE))
-    home = ring_exchange(ret)
-    shape = (tokens, 2 * features)
-    y, dx = call(
-        merge_body, [(shape, BF16), (shape, BF16)], routes_f, routes_b, probs_f, probs_b, rows_f, rows_c, home
-    )
-    return from_behind(y[None], 1), from_behind(dx[None], -1)
+    shape = (2 * slots, quarter)
+    ret_f, ret_b = call(finish_body, [(shape, BF16), (shape, BF16)], own, swap(cross, CORE), got_b)
+    next_b, next_routes = from_behind(ret_b, -1), from_behind(routes_b, -1)
+    home_f = ring_exchange(ret_f)
+    next_b = gate(next_b)
+    (y,) = call(merge_fwd_body, [((tokens, 2 * features), BF16)], routes_f, probs_f, rows_f, home_f)
+    home_b = ring_exchange(next_b)
+    (dx,) = call(merge_bwd_body, [((tokens, 2 * features), BF16)], next_routes, home_b)
+    return from_behind(y[None], 1), dx[None]
 
 
 def solution(mesh):

time: 194 us -> 179 us (0.923)
  waiting for transfers between devices: 92.6 us -> 69.4 us
  starting transfers between devices: 70.6 us -> 78.4 us
    ppermute x11, waiting for transfers between devices: 20.9 us -> 9.42 us  [swap(): lax.ppermute(value, 'expert', [(i, i ^ m) for i, m in enumerate(masks) if...]
    all_to_all x3 -> x4, waiting for transfers between devices: 55.1 us -> 44.9 us  [ring_exchange(): lax.all_to_all(cut, 'expert', split_axis=0, concat_axis=0, tiled=True, ax...]
    all_to_all x3 -> x4, starting transfers between devices: 21.1 us -> 26 us  [ring_exchange(): lax.all_to_all(cut, 'expert', split_axis=0, concat_axis=0, tiled=True, ax...]
    ppermute x2 -> x3, starting transfers between devices: 11 us -> 13.9 us  [from_behind(): lax.ppermute(value, 'pipe', [(i, (i + steps) % count) for i in range(coun...]
    ppermute x2 -> x3, waiting for transfers between devices: 16.7 us -> 15.1 us  [from_behind(): lax.ppermute(value, 'pipe', [(i, (i + steps) % count) for i in range(coun...]
    pallas_call x9 -> x10, Pallas kernels: 24.3 us -> 23.2 us  [call(): pl.pallas_call(run, out_shape=shapes, in_specs=lead + [pl.BlockSpec(memor...]
    unnamed x22 -> x25, local copies, waits for them, and re-layouts: 4.25 us -> 5.16 us
  transfers between devices with their start and end apart: 16 -> 18, of which waited for: 9 -> 8; matrix products, arithmetic and copies ran while one was open for 0% -> 0% of each run, Pallas kernels for 7% -> 9%
where the time goes in v3:
time: 179 us; the launch traced here: 178 us
  starting transfers between devices  78.4 us (44%)
  waiting for transfers between devices  69.4 us (39%)
  Pallas kernels  23.2 us (13%)
  local copies, waits for them, and re-layouts  6.01 us (3%)
    all_to_all x4, waiting for transfers between devices, ring_exchange(): lax.all_to_all(cut, 'expert', split_axis=0, concat_axis=0, tiled=True, ax...  44.9 us
    ppermute x11, starting transfers between devices, swap(): lax.ppermute(value, 'expert', [(i, i ^ m) for i, m in enumerate(masks) if...  38.5 us
    all_to_all x4, starting transfers between devices, ring_exchange(): lax.all_to_all(cut, 'expert', split_axis=0, concat_axis=0, tiled=True, ax...  26 us
    pallas_call x10, Pallas kernels, call(): pl.pallas_call(run, out_shape=shapes, in_specs=lead + [pl.BlockSpec(memor...  23.2 us
    ppermute x3, waiting for transfers between devices, from_behind(): lax.ppermute(value, 'pipe', [(i, (i + steps) % count) for i in range(coun...  15.1 us
    ppermute x3, starting transfers between devices, from_behind(): lax.ppermute(value, 'pipe', [(i, (i + steps) % count) for i in range(coun...  13.9 us
    ppermute x11, waiting for transfers between devices, swap(): lax.ppermute(value, 'expert', [(i, i ^ m) for i, m in enumerate(masks) if...  9.42 us
    unnamed x25, local copies, waits for them, and re-layouts  5.16 us
  transfers between devices with their start and end apart: 18, of which 8 were waited for; matrix products, arithmetic and copies ran while one was open for 0% of the time, Pallas kernels for 9%

profile of v3, /device:TPU:1, one launch (start us, length us, event | category | flops | bytes accessed | tf_op | source)
XLA Modules:
  0.0 177.9 jit_solution(1331597855182017438)
XLA Ops:
  0.6 5.4 %collective-permute-start = (bf16[1792,256]{1,0:T(8,128)(2,1)}, bf16[1792,256]{1,0:T(8,128)(2,1)}, u32[]{:S(2)}, u32[]{:S(2)}) collective-permute-start(bf16[1792,256]{1,0:T(8,128)(2,1)} %bitcast.23), channel_id=1, source_target_pairs={{0,2},{1,4},{2,0},{3,6},{4,1},{5,7},{6,3},{7,5},{8,10},{9,12},{10,... | collective-permute-start | bytes 2752520 | tf_op jit(solution)/shard_map/ppermute | solution.py:27
  12.0 13.1 %all-to-all-start = ((bf16[8,40,1920]{2,1,0:T(8,128)(2,1)}), bf16[8,40,1920]{2,1,0:T(8,128)(2,1)S(1)}, u32[]{:S(2)}, u32[]{:S(2)}) async-start(bf16[8,40,1920]{2,1,0:T(8,128)(2,1)} %shard_map.106), calls=%async_computation | async-start | bytes 2457600 | tf_op jit(solution)/shard_map/all_to_all | solution.py:44
  25.1 4.7 %collective-permute-start.2 = (bf16[256,1792]{1,0:T(8,128)(2,1)}, bf16[256,1792]{1,0:T(8,128)(2,1)S(1)}, u32[]{:S(2)}, u32[]{:S(2)}) collective-permute-start(bf16[256,1792]{1,0:T(8,128)(2,1)} %bitcast.11.refs_3_.refs_12_), channel_id=1, source_target_pairs={{0,2},{1,4},{2,0},{3,6},{4,1},{5,7},{6,3},{7,5},{8,10},{9,12},{10,... | collective-permute-start | bytes 2752520 | tf_op jit(solution)/shard_map/ppermute | solution.py:27
  33.7 24.5 %all-to-all-done = bf16[8,40,1920]{2,1,0:T(8,128)(2,1)S(1)} async-done(((bf16[8,40,1920]{2,1,0:T(8,128)(2,1)}), bf16[8,40,1920]{2,1,0:T(8,128)(2,1)S(1)}, u32[]{:S(2)}, u32[]{:S(2)}) %all-to-all-start) | async-done | bytes 1228832 | tf_op jit(solution)/shard_map/all_to_all | solution.py:44
  58.1 4.2 %all-to-all-start.1 = ((bf16[8,40,896]{2,1,0:T(8,128)(2,1)}), bf16[8,40,896]{2,1,0:T(8,128)(2,1)}, u32[]{:S(2)}, u32[]{:S(2)}) async-start(bf16[8,40,896]{2,1,0:T(8,128)(2,1)} %shard_map.105), calls=%async_computation.1 | async-start | bytes 1146880 | tf_op jit(solution)/shard_map/all_to_all | solution.py:44
  64.9 7.9 %collective-permute-start.7 = (bf16[256,1792]{1,0:T(8,128)(2,1)S(1)}, bf16[256,1792]{1,0:T(8,128)(2,1)}, u32[]{:S(2)}, u32[]{:S(2)}) collective-permute-start(bf16[256,1792]{1,0:T(8,128)(2,1)S(1)} %collective-permute-done.2.refs_4_.refs_3_.refs_13_), channel_id=1, source_target_pairs={{1,3},{3,1},{4,6},{6,4},{9,11},{11,9},{12,14},{14,12},{17,19},{19,... | collective-permute-start | bytes 2752520 | tf_op jit(solution)/shard_map/ppermute | solution.py:27
  72.8 8.5 %all-to-all-done.1 = bf16[8,40,896]{2,1,0:T(8,128)(2,1)} async-done(((bf16[8,40,896]{2,1,0:T(8,128)(2,1)}), bf16[8,40,896]{2,1,0:T(8,128)(2,1)}, u32[]{:S(2)}, u32[]{:S(2)}) %all-to-all-start.1) | async-done | bytes 573472 | tf_op jit(solution)/shard_map/all_to_all | solution.py:44
  83.8 2.7 %shard_map.109 = (f32[320,256]{1,0:T(8,128)S(1)}, bf16[320,256]{1,0:T(8,128)(2,1)S(1)}) custom-call(s32[1]{0:T(128)} %bitcast.3.refs_0_, bf16[320,1920]{1,0:T(8,128)(2,1)S(1)} %bitcast.19, bf16[320,1920]{1,0:T(8,128)(2,1)S(1)} %collective-permute-done.5.refs_2_, bf16[256,1792]{1,0:T(8,128)(2,1)} %bitcast.11.refs_3_.refs_12_, ...), custom_call_target="tpu_custom_call" | custom-call | tf_op jit(solution)/shard_map/pallas_call | solution.py:58
  88.7 2.9 %shard_map.108 = (f32[320,512]{1,0:T(8,128)S(1)}, bf16[320,512]{1,0:T(8,128)(2,1)S(1)}) custom-call(s32[1]{0:T(128)} %bitcast.3.refs_0_, bf16[320,1920]{1,0:T(8,128)(2,1)S(1)} %bitcast.20, bf16[320,1920]{1,0:T(8,128)(2,1)S(1)} %collective-permute-done.5.refs_2_, bf16[1792,256]{1,0:T(8,128)(2,1)S(1)} %bitcast.24, ...), custom_call_target="tpu_custom_call" | custom-call | tf_op jit(solution)/shard_map/pallas_call | solution.py:58
  91.6 3.1 %collective-permute-start.6 = (bf16[320,512]{1,0:T(8,128)(2,1)S(1)}, bf16[320,512]{1,0:T(8,128)(2,1)S(1)}, u32[]{:S(2)}, u32[]{:S(2)}) collective-permute-start(bf16[320,512]{1,0:T(8,128)(2,1)S(1)} %get-tuple-element.26), channel_id=1, source_target_pairs={{0,4},{1,5},{2,6},{3,7},{4,0},{5,1},{6,2},{7,3},{8,12},{9,13},{10,... | collective-permute-start | bytes 983048 | tf_op jit(solution)/shard_map/ppermute | solution.py:27
  94.7 3.4 %shard_map.107 = (f32[320,512]{1,0:T(8,128)S(1)}, bf16[320,512]{1,0:T(8,128)(2,1)S(1)}) custom-call(s32[1]{0:T(128)} %bitcast.3.refs_0_, bf16[320,896]{1,0:T(8,128)(2,1)} %bitcast.10.refs_1_, bf16[320,896]{1,0:T(8,128)(2,1)} %collective-permute-done.1.refs_2_, bf16[1792,256]{1,0:T(8,128)(2,1)S(1)} %bitcast.25, ...), custom_call_target="tpu_custom_call" | custom-call | tf_op jit(solution)/shard_map/pallas_call | solution.py:58
  100.3 2.6 %shard_map.110 = (f32[320,256]{1,0:T(8,128)S(1)}, bf16[320,256]{1,0:T(8,128)(2,1)S(1)}) custom-call(s32[1]{0:T(128)} %bitcast.3.refs_0_, bf16[320,1920]{1,0:T(8,128)(2,1)S(1)} %bitcast.21, bf16[320,1920]{1,0:T(8,128)(2,1)S(1)} %collective-permute-done.5.refs_2_, bf16[256,1792]{1,0:T(8,128)(2,1)S(1)} %collective-permute-done.2.refs_4_.refs_3_.refs_13_, ...), custom_call_target="tpu_custom_call" | custom-call | tf_op jit(solution)/shard_map/pallas_call | solution.py:58
  103.0 3.2 %collective-permute-start.9 = (bf16[320,256]{1,0:T(8,128)(2,1)S(1)}, bf16[320,256]{1,0:T(8,128)(2,1)S(1)}, u32[]{:S(2)}, u32[]{:S(2)}) collective-permute-start(bf16[320,256]{1,0:T(8,128)(2,1)S(1)} %get-tuple-element.33), channel_id=1, source_target_pairs={{0,4},{1,5},{2,6},{3,7},{4,0},{5,1},{6,2},{7,3},{8,12},{9,13},{10,... | collective-permute-start | bytes 491528 | tf_op jit(solution)/shard_map/ppermute | solution.py:27
  106.3 7.0 %collective-permute-done.9.refs_8_ = bf16[320,256]{1,0:T(8,128)(2,1)S(1)} collective-permute-done((bf16[320,256]{1,0:T(8,128)(2,1)S(1)}, bf16[320,256]{1,0:T(8,128)(2,1)S(1)}, u32[]{:S(2)}, u32[]{:S(2)}) %collective-permute-start.9) | collective-permute-done | bytes 163872 | tf_op jit(solution)/shard_map/ppermute | solution.py:27
  113.2 3.9 %shard_map.111 = (f32[320,1792]{1,0:T(8,128)S(1)}, bf16[320,1792]{1,0:T(8,128)(2,1)S(1)}) custom-call(s32[1]{0:T(128)} %bitcast.3.refs_0_, f32[320,512]{1,0:T(8,128)S(1)} %get-tuple-element.22.refs_1_, bf16[320,512]{1,0:T(8,128)(2,1)S(1)} %collective-permute-done.4.refs_2_, f32[320,512]{1,0:T(8,128)S(1)} %get-tuple-element.25.refs_3_, ...), custom_call_target="tpu_custom_call" | custom-call | tf_op jit(solution)/shard_map/pallas_call | solution.py:58
  117.1 2.8 %collective-permute-start.10 = (bf16[320,1792]{1,0:T(8,128)(2,1)S(1)}, bf16[320,1792]{1,0:T(8,128)(2,1)S(1)}, u32[]{:S(2)}, u32[]{:S(2)}) collective-permute-start(bf16[320,1792]{1,0:T(8,128)(2,1)S(1)} %get-tuple-element.35), channel_id=1, source_target_pairs={{0,1},{1,0},{2,3},{3,2},{4,5},{5,4},{6,7},{7,6},{8,9},{9,8},{10,11... | collective-permute-start | bytes 3440648 | tf_op jit(solution)/shard_map/ppermute | solution.py:27
  124.1 4.7 %collective-permute-start.13 = (bf16[320,896]{1,0:T(8,128)(2,1)S(1)}, bf16[320,896]{1,0:T(8,128)(2,1)S(1)}, u32[]{:S(2)}, u32[]{:S(2)}) collective-permute-start(bf16[320,896]{1,0:T(8,128)(2,1)S(1)} %get-tuple-element.37), channel_id=1, source_target_pairs={{0,480},{32,0},{64,32},{96,64},{128,96},{160,128},{192,160},{224,1... | collective-permute-start | bytes 1720328 | tf_op jit(solution)/shard_map/ppermute | solution.py:36
  128.8 5.0 %all-to-all-start.2 = ((bf16[8,40,896]{2,1,0:T(8,128)(2,1)}), bf16[8,40,896]{2,1,0:T(8,128)(2,1)S(1)}, u32[]{:S(2)}, u32[]{:S(2)}) async-start(bf16[8,40,896]{2,1,0:T(8,128)(2,1)} %bitcast.12), calls=%async_computation.2 | async-start | bytes 1146880 | tf_op jit(solution)/shard_map/all_to_all | solution.py:44
  133.9 6.9 %collective-permute-done.13.refs_0_ = bf16[320,896]{1,0:T(8,128)(2,1)S(1)} collective-permute-done((bf16[320,896]{1,0:T(8,128)(2,1)S(1)}, bf16[320,896]{1,0:T(8,128)(2,1)S(1)}, u32[]{:S(2)}, u32[]{:S(2)}) %collective-permute-start.13) | collective-permute-done | bytes 573472 | tf_op jit(solution)/shard_map/ppermute | solution.py:36
  141.6 11.2 %all-to-all-done.2 = bf16[8,40,896]{2,1,0:T(8,128)(2,1)S(1)} async-done(((bf16[8,40,896]{2,1,0:T(8,128)(2,1)}), bf16[8,40,896]{2,1,0:T(8,128)(2,1)S(1)}, u32[]{:S(2)}, u32[]{:S(2)}) %all-to-all-start.2) | async-done | bytes 573472 | tf_op jit(solution)/shard_map/all_to_all | solution.py:44
  152.9 3.7 %all-to-all-start.3 = ((bf16[8,40,896]{2,1,0:T(8,128)(2,1)}), bf16[8,40,896]{2,1,0:T(8,128)(2,1)S(1)}, u32[]{:S(2)}, u32[]{:S(2)}) async-start(bf16[8,40,896]{2,1,0:T(8,128)(2,1)} %bitcast.38), calls=%async_computation.3 | async-start | bytes 1146880 | tf_op jit(solution)/shard_map/all_to_all | solution.py:44
  157.5 2.7 %collective-permute-start.11 = (bf16[1,64,3584]{2,1,0:T(8,128)(2,1)S(1)}, bf16[1,64,3584]{2,1,0:T(8,128)(2,1)S(1)}, u32[]{:S(2)}, u32[]{:S(2)}) collective-permute-start(bf16[1,64,3584]{2,1,0:T(8,128)(2,1)S(1)} %bitcast.33), channel_id=1, source_target_pairs={{0,32},{32,64},{64,96},{96,128},{128,160},{160,192},{192,224},{224... | collective-permute-start | bytes 1376264 | tf_op jit(solution)/shard_map/ppermute | solution.py:36
  160.2 6.5 %collective-permute-start.12 = (s32[1,64]{1,0:T(1,128)S(1)}, s32[1,64]{1,0:T(1,128)S(1)}, u32[]{:S(2)}, u32[]{:S(2)}) collective-permute-start(s32[1,64]{1,0:T(1,128)S(1)} %bitcast.37), channel_id=1, source_target_pairs={{0,480},{32,0},{64,32},{96,64},{128,96},{160,128},{192,160},{224,1... | collective-permute-start | bytes 776 | tf_op jit(solution)/shard_map/ppermute | solution.py:36
  166.7 8.2 %collective-permute-done.11 = bf16[1,64,3584]{2,1,0:T(8,128)(2,1)S(1)} collective-permute-done((bf16[1,64,3584]{2,1,0:T(8,128)(2,1)S(1)}, bf16[1,64,3584]{2,1,0:T(8,128)(2,1)S(1)}, u32[]{:S(2)}, u32[]{:S(2)}) %collective-permute-start.11) | collective-permute-done | bytes 458784 | tf_op jit(solution)/shard_map/ppermute | solution.py:36
  (51 shorter events, 28.0 us)
Async XLA Ops:
  0.6 31.1 %collective-permute-start = (bf16[1792,256]{1,0:T(8,128)(2,1)}, bf16[1792,256]{1,0:T(8,128)(2,1)}, u32[]{:S(2)}, u32[]{:S(2)}) collective-permute-start(bf16[1792,256]{1,0:T(8,128)(2,1)} %bitcast.23), channel_id=1, source_target_pairs={{0,2},{1,4},{2,0},{3,6},{4,1},{5,7},{6,3},{7,5},{8,10},{9,12},{10,... | collective-permute-start | bytes 2752520 | tf_op jit(solution)/shard_map/ppermute | solution.py:27
  12.0 17.8 %copy-start.2 = (bf16[1,64,3584]{2,1,0:T(8,128)(2,1)S(1)}, bf16[1,64,3584]{2,1,0:T(8,128)(2,1)}, u32[]{:S(2)}) copy-start(bf16[1,64,3584]{2,1,0:T(8,128)(2,1)} %param.9) | copy-start | bytes 1376260
  12.0 17.8 %copy-start.6 = (s32[1,64,1]{1,2,0:T(1,128)S(1)}, s32[1,64,1]{1,2,0:T(1,128)}, u32[]{:S(2)}) copy-start(s32[1,64,1]{1,2,0:T(1,128)} %param.12) | copy-start | bytes 772
  12.0 46.2 %all-to-all-start = ((bf16[8,40,1920]{2,1,0:T(8,128)(2,1)}), bf16[8,40,1920]{2,1,0:T(8,128)(2,1)S(1)}, u32[]{:S(2)}, u32[]{:S(2)}) async-start(bf16[8,40,1920]{2,1,0:T(8,128)(2,1)} %shard_map.106), calls=%async_computation | async-start | bytes 2457600 | tf_op jit(solution)/shard_map/all_to_all | solution.py:44
  25.1 39.8 %collective-permute-start.2 = (bf16[256,1792]{1,0:T(8,128)(2,1)}, bf16[256,1792]{1,0:T(8,128)(2,1)S(1)}, u32[]{:S(2)}, u32[]{:S(2)}) collective-permute-start(bf16[256,1792]{1,0:T(8,128)(2,1)} %bitcast.11.refs_3_.refs_12_), channel_id=1, source_target_pairs={{0,2},{1,4},{2,0},{3,6},{4,1},{5,7},{6,3},{7,5},{8,10},{9,12},{10,... | collective-permute-start | bytes 2752520 | tf_op jit(solution)/shard_map/ppermute | solution.py:27
  31.8 33.1 %collective-permute-start.3 = (bf16[1792,256]{1,0:T(8,128)(2,1)}, bf16[1792,256]{1,0:T(8,128)(2,1)}, u32[]{:S(2)}, u32[]{:S(2)}) collective-permute-start(bf16[1792,256]{1,0:T(8,128)(2,1)} %collective-permute-done.refs_1_.refs_4_.refs_10_), channel_id=1, source_target_pairs={{1,3},{3,1},{4,6},{6,4},{9,11},{11,9},{12,14},{14,12},{17,19},{19,... | collective-permute-start | bytes 2752520 | tf_op jit(solution)/shard_map/ppermute | solution.py:27
  58.1 23.2 %all-to-all-start.1 = ((bf16[8,40,896]{2,1,0:T(8,128)(2,1)}), bf16[8,40,896]{2,1,0:T(8,128)(2,1)}, u32[]{:S(2)}, u32[]{:S(2)}) async-start(bf16[8,40,896]{2,1,0:T(8,128)(2,1)} %shard_map.105), calls=%async_computation.1 | async-start | bytes 1146880 | tf_op jit(solution)/shard_map/all_to_all | solution.py:44
  62.3 21.4 %collective-permute-start.5 = (bf16[320,1920]{1,0:T(8,128)(2,1)S(1)}, bf16[320,1920]{1,0:T(8,128)(2,1)S(1)}, u32[]{:S(2)}, u32[]{:S(2)}) collective-permute-start(bf16[320,1920]{1,0:T(8,128)(2,1)S(1)} %bitcast.18), channel_id=1, source_target_pairs={{0,1},{1,0},{2,3},{3,2},{4,5},{5,4},{6,7},{7,6},{8,9},{9,8},{10,11... | collective-permute-start | bytes 3686408 | tf_op jit(solution)/shard_map/ppermute | solution.py:27
  64.9 35.5 %collective-permute-start.7 = (bf16[256,1792]{1,0:T(8,128)(2,1)S(1)}, bf16[256,1792]{1,0:T(8,128)(2,1)}, u32[]{:S(2)}, u32[]{:S(2)}) collective-permute-start(bf16[256,1792]{1,0:T(8,128)(2,1)S(1)} %collective-permute-done.2.refs_4_.refs_3_.refs_13_), channel_id=1, source_target_pairs={{1,3},{3,1},{4,6},{6,4},{9,11},{11,9},{12,14},{14,12},{17,19},{19,... | collective-permute-start | bytes 2752520 | tf_op jit(solution)/shard_map/ppermute | solution.py:27
  81.3 13.3 %collective-permute-start.1 = (bf16[320,896]{1,0:T(8,128)(2,1)}, bf16[320,896]{1,0:T(8,128)(2,1)}, u32[]{:S(2)}, u32[]{:S(2)}) collective-permute-start(bf16[320,896]{1,0:T(8,128)(2,1)} %bitcast.10.refs_1_), channel_id=1, source_target_pairs={{0,1},{1,0},{2,3},{3,2},{4,5},{5,4},{6,7},{7,6},{8,9},{9,8},{10,11... | collective-permute-start | bytes 1720328 | tf_op jit(solution)/shard_map/ppermute | solution.py:27
  86.5 13.8 %collective-permute-start.8 = (bf16[320,256]{1,0:T(8,128)(2,1)S(1)}, bf16[320,256]{1,0:T(8,128)(2,1)S(1)}, u32[]{:S(2)}, u32[]{:S(2)}) collective-permute-start(bf16[320,256]{1,0:T(8,128)(2,1)S(1)} %get-tuple-element.29), channel_id=1, source_target_pairs={{0,4},{1,5},{2,6},{3,7},{4,0},{5,1},{6,2},{7,3},{8,12},{9,13},{10,... | collective-permute-start | bytes 491528 | tf_op jit(solution)/shard_map/ppermute | solution.py:27
  91.6 14.6 %collective-permute-start.6 = (bf16[320,512]{1,0:T(8,128)(2,1)S(1)}, bf16[320,512]{1,0:T(8,128)(2,1)S(1)}, u32[]{:S(2)}, u32[]{:S(2)}) collective-permute-start(bf16[320,512]{1,0:T(8,128)(2,1)S(1)} %get-tuple-element.26), channel_id=1, source_target_pairs={{0,4},{1,5},{2,6},{3,7},{4,0},{5,1},{6,2},{7,3},{8,12},{9,13},{10,... | collective-permute-start | bytes 983048 | tf_op jit(solution)/shard_map/ppermute | solution.py:27
  98.1 15.2 %collective-permute-start.4 = (bf16[320,512]{1,0:T(8,128)(2,1)S(1)}, bf16[320,512]{1,0:T(8,128)(2,1)S(1)}, u32[]{:S(2)}, u32[]{:S(2)}) collective-permute-start(bf16[320,512]{1,0:T(8,128)(2,1)S(1)} %get-tuple-element.23), channel_id=1, source_target_pairs={{0,4},{1,5},{2,6},{3,7},{4,0},{5,1},{6,2},{7,3},{8,12},{9,13},{10,... | collective-permute-start | bytes 983048 | tf_op jit(solution)/shard_map/ppermute | solution.py:27
  103.0 10.3 %collective-permute-start.9 = (bf16[320,256]{1,0:T(8,128)(2,1)S(1)}, bf16[320,256]{1,0:T(8,128)(2,1)S(1)}, u32[]{:S(2)}, u32[]{:S(2)}) collective-permute-start(bf16[320,256]{1,0:T(8,128)(2,1)S(1)} %get-tuple-element.33), channel_id=1, source_target_pairs={{0,4},{1,5},{2,6},{3,7},{4,0},{5,1},{6,2},{7,3},{8,12},{9,13},{10,... | collective-permute-start | bytes 491528 | tf_op jit(solution)/shard_map/ppermute | solution.py:27
  117.1 5.2 %collective-permute-start.10 = (bf16[320,1792]{1,0:T(8,128)(2,1)S(1)}, bf16[320,1792]{1,0:T(8,128)(2,1)S(1)}, u32[]{:S(2)}, u32[]{:S(2)}) collective-permute-start(bf16[320,1792]{1,0:T(8,128)(2,1)S(1)} %get-tuple-element.35), channel_id=1, source_target_pairs={{0,1},{1,0},{2,3},{3,2},{4,5},{5,4},{6,7},{7,6},{8,9},{9,8},{10,11... | collective-permute-start | bytes 3440648 | tf_op jit(solution)/shard_map/ppermute | solution.py:27
  124.1 16.7 %collective-permute-start.13 = (bf16[320,896]{1,0:T(8,128)(2,1)S(1)}, bf16[320,896]{1,0:T(8,128)(2,1)S(1)}, u32[]{:S(2)}, u32[]{:S(2)}) collective-permute-start(bf16[320,896]{1,0:T(8,128)(2,1)S(1)} %get-tuple-element.37), channel_id=1, source_target_pairs={{0,480},{32,0},{64,32},{96,64},{128,96},{160,128},{192,160},{224,1... | collective-permute-start | bytes 1720328 | tf_op jit(solution)/shard_map/ppermute | solution.py:36
  128.8 24.1 %all-to-all-start.2 = ((bf16[8,40,896]{2,1,0:T(8,128)(2,1)}), bf16[8,40,896]{2,1,0:T(8,128)(2,1)S(1)}, u32[]{:S(2)}, u32[]{:S(2)}) async-start(bf16[8,40,896]{2,1,0:T(8,128)(2,1)} %bitcast.12), calls=%async_computation.2 | async-start | bytes 1146880 | tf_op jit(solution)/shard_map/all_to_all | solution.py:44
  133.8 22.7 %copy-start.11 = (f32[1,64,1]{1,2,0:T(1,128)S(1)}, f32[1,64,1]{1,2,0:T(1,128)}, u32[]{:S(2)}) copy-start(f32[1,64,1]{1,2,0:T(1,128)} %param.14) | copy-start | bytes 772
  133.9 22.8 %copy-start.7 = (s32[1,64,1]{1,2,0:T(1,128)S(1)}, s32[1,64,1]{1,2,0:T(1,128)}, u32[]{:S(2)}) copy-start(s32[1,64,1]{1,2,0:T(1,128)} %param.12) | copy-start | bytes 772
  141.6 15.0 %copy-start.3 = (bf16[1,64,3584]{2,1,0:T(8,128)(2,1)S(1)}, bf16[1,64,3584]{2,1,0:T(8,128)(2,1)}, u32[]{:S(2)}) copy-start(bf16[1,64,3584]{2,1,0:T(8,128)(2,1)} %param.9) | copy-start | bytes 1376260
  152.9 7.3 %copy-start.9 = (s32[1,64,1]{1,2,0:T(1,128)S(1)}, s32[1,64,1]{1,2,0:T(1,128)}, u32[]{:S(2)}) copy-start(s32[1,64,1]{1,2,0:T(1,128)} %param.13) | copy-start | bytes 772
  152.9 22.6 %all-to-all-start.3 = ((bf16[8,40,896]{2,1,0:T(8,128)(2,1)}), bf16[8,40,896]{2,1,0:T(8,128)(2,1)S(1)}, u32[]{:S(2)}, u32[]{:S(2)}) async-start(bf16[8,40,896]{2,1,0:T(8,128)(2,1)} %bitcast.38), calls=%async_computation.3 | async-start | bytes 1146880 | tf_op jit(solution)/shard_map/all_to_all | solution.py:44
  157.5 17.4 %collective-permute-start.11 = (bf16[1,64,3584]{2,1,0:T(8,128)(2,1)S(1)}, bf16[1,64,3584]{2,1,0:T(8,128)(2,1)S(1)}, u32[]{:S(2)}, u32[]{:S(2)}) collective-permute-start(bf16[1,64,3584]{2,1,0:T(8,128)(2,1)S(1)} %bitcast.33), channel_id=1, source_target_pairs={{0,32},{32,64},{64,96},{96,128},{128,160},{160,192},{192,224},{224... | collective-permute-start | bytes 1376264 | tf_op jit(solution)/shard_map/ppermute | solution.py:36
  160.2 14.7 %collective-permute-start.12 = (s32[1,64]{1,0:T(1,128)S(1)}, s32[1,64]{1,0:T(1,128)S(1)}, u32[]{:S(2)}, u32[]{:S(2)}) collective-permute-start(s32[1,64]{1,0:T(1,128)S(1)} %bitcast.37), channel_id=1, source_target_pairs={{0,480},{32,0},{64,32},{96,64},{128,96},{160,128},{192,160},{224,1... | collective-permute-start | bytes 776 | tf_op jit(solution)/shard_map/ppermute | solution.py:36
  (6 other events, 9.3 us)

commit v4 on v3

--- a/solution.py
+++ b/solution.py
@@ -148,21 +148,28 @@
     choose(flag, run, w_in)
 
 
-def act_bwd_body(flag, own, other, *refs):
-    *w_in, act, sent = refs
-    low, _ = halves(own.shape[0])
+def first_bwd_body(flag, own, other, *refs):
+    w_in, w_out = refs[:3], refs[3:5]
+    act, grad, sent = refs[5:]
+    low, high = halves(own.shape[0])
     many = low.shape[0]
 
-    def run(pieces):
+    def run(ins, outs):
+        (wo,) = outs
+        n, wide = wo.shape
         for k, ref in enumerate((own, other)):
-            v = dot(low, ref[:, : pieces[0].shape[0]]).astype(BF16)
-            for q, w in enumerate(pieces):
-                at = (pl.ds(k * many, many), pl.ds(q * w.shape[1], w.shape[1]))
+            at = pl.ds(k * many, many)
+            v = dot(low, ref[:, :wide]).astype(BF16)
+            c = dot(high, ref[:, :wide]).astype(BF16)
+            for q, w in enumerate(ins):
                 part = dot(v, w[...])
-                act[at] = part
-                sent[at] = part.astype(BF16)
-
-    choose(flag, run, w_in)
+                act[at, pl.ds(q * n, n)] = part
+                sent[at, pl.ds(q * n, n)] = part.astype(BF16)
+            part = dot(c, wo[...], NT)
+            grad[at, :] = part
+            sent[at, pl.ds(2 * n, n)] = part.astype(BF16)
+
+    choose(flag, run, w_in, w_out)
 
 
 def grad_body(flag, own, other, *refs):
@@ -182,7 +189,7 @@
     choose(flag, run, w_out)
 
 
-def out_body(flag, act_f, got_f, act_b, got_b, grad1, got_grad1, grad2, got_grad2, *refs):
+def out_body(flag, act_f, got_f, act_b, grad1, got_b, grad2, got_grad2, *refs):
     w_in, w_out = refs[:3], refs[3:6]
     own, sent = refs[6:]
     n = grad1.shape[1]
@@ -190,10 +197,10 @@
     a = act_f[...] + got_f[...].astype(F32)
     h = (a * jax.nn.sigmoid(a)).astype(BF16)
     r = []
-    for q, (grad, got) in enumerate(((grad1, got_grad1), (grad2, got_grad2))):
+    for q, (grad, got) in enumerate(((grad1, got_b[:, pl.ds(2 * n, n)]), (grad2, got_grad2[...]))):
         at = pl.ds(q * n, n)
         a = act_b[:, at] + got_b[:, at].astype(F32)
-        g = grad[...] + got[...].astype(F32)
+        g = grad[...] + got.astype(F32)
         s = jax.nn.sigmoid(a)
         r.append((g * s * (1.0 + a * (1.0 - s))).astype(BF16))
 
@@ -287,20 +294,23 @@
 
     pre, piece = (2 * slots, 2 * hidden), (2 * slots, hidden)
     far_b = swap(got_b, CORE)
-    grad1, sent_g1 = call(grad_body, [(piece, F32), (piece, BF16)], got_b, far_b, own_out, m_out, flag=flag)
-    back_g1 = swap(sent_g1, PAIR)
-    act_b, sent_a = call(act_bwd_body, [(pre, F32), (pre, BF16)], got_b, far_b, *w_in, flag=flag)
-    back_a = swap(sent_a, PAIR)
+    act_b, grad1, sent_b = call(
+        first_bwd_body,
+        [(pre, F32), (piece, F32), ((2 * slots, 3 * hidden), BF16)],
+        *(got_b, far_b, *w_in, own_out, m_out),
+        flag=flag,
+    )
+    back_b = swap(sent_b, PAIR)
     far_f = swap(got_f, CORE)
     act_f, sent_f = call(act_fwd_body, [(pre, F32), (pre, BF16)], got_f, far_f, *w_in, flag=flag)
     back_f = swap(sent_f, PAIR)
-    v_out, sent_f, sent_a, back_g1 = lax.optimization_barrier((v_out, sent_f, sent_a, back_g1))
+    v_out, sent_f, sent_b = lax.optimization_barrier((v_out, sent_f, sent_b))
     grad2, sent_g2 = call(grad_body, [(piece, F32), (piece, BF16)], got_b, far_b, m_out, v_out, flag=flag)
     back_g2 = swap(sent_g2, PAIR)
     own, cross = call(
         out_body,
         [((2 * slots, features), F32), ((2 * slots, features), BF16)],
-        *(act_f, back_f, act_b, back_a, grad1, back_g1, grad2, back_g2, *w_in, *w_out),
+        *(act_f, back_f, act_b, grad1, back_b, grad2, back_g2, *w_in, *w_out),
         flag=flag,
     )
     shape = (2 * slots, quarter)

time: 179 us -> 179 us (level)
  waiting for transfers between devices: 69.4 us -> 73.4 us
  starting transfers between devices: 78.4 us -> 74.8 us
    ppermute x11 -> x10, waiting for transfers between devices: 9.42 us -> 13.5 us  [swap(): lax.ppermute(value, 'expert', [(i, i ^ m) for i, m in enumerate(masks) if...]
    ppermute x11 -> x10, starting transfers between devices: 38.5 us -> 35.4 us  [swap(): lax.ppermute(value, 'expert', [(i, i ^ m) for i, m in enumerate(masks) if...]
    pallas_call x10 -> x9, Pallas kernels: 23.2 us -> 22.6 us  [call(): pl.pallas_call(run, out_shape=shapes, in_specs=lead + [pl.BlockSpec(memor...]
  transfers between devices with their start and end apart: 18 -> 17, of which waited for: 8 -> 9; matrix products, arithmetic and copies ran while one was open for 0% -> 0% of each run, Pallas kernels for 9% -> 9%
where the time goes in v4:
time: 179 us; the launch traced here: 178 us
  starting transfers between devices  74.8 us (42%)
  waiting for transfers between devices  73.4 us (41%)
  Pallas kernels  22.6 us (13%)
  local copies, waits for them, and re-layouts  6 us (3%)
    all_to_all x4, waiting for transfers between devices, ring_exchange(): lax.all_to_all(cut, 'expert', split_axis=0, concat_axis=0, tiled=True, ax...  44.3 us
    ppermute x10, starting transfers between devices, swap(): lax.ppermute(value, 'expert', [(i, i ^ m) for i, m in enumerate(masks) if...  35.4 us
    all_to_all x4, starting transfers between devices, ring_exchange(): lax.all_to_all(cut, 'expert', split_axis=0, concat_axis=0, tiled=True, ax...  25.5 us
    pallas_call x9, Pallas kernels, call(): pl.pallas_call(run, out_shape=shapes, in_specs=lead + [pl.BlockSpec(memor...  22.6 us
    ppermute x3, waiting for transfers between devices, from_behind(): lax.ppermute(value, 'pipe', [(i, (i + steps) % count) for i in range(coun...  15.6 us
    ppermute x3, starting transfers between devices, from_behind(): lax.ppermute(value, 'pipe', [(i, (i + steps) % count) for i in range(coun...  13.9 us
    ppermute x10, waiting for transfers between devices, swap(): lax.ppermute(value, 'expert', [(i, i ^ m) for i, m in enumerate(masks) if...  13.5 us
    unnamed x25, local copies, waits for them, and re-layouts  5.16 us
  transfers between devices with their start and end apart: 17, of which 9 were waited for; matrix products, arithmetic and copies ran while one was open for 0% of the time, Pallas kernels for 9%

profile of v4, /device:TPU:1, one launch (start us, length us, event | category | flops | bytes accessed | tf_op | source)
XLA Modules:
  0.0 177.7 jit_solution(14488156634197402893)
XLA Ops:
  0.6 5.4 %collective-permute-start = (bf16[1792,256]{1,0:T(8,128)(2,1)}, bf16[1792,256]{1,0:T(8,128)(2,1)}, u32[]{:S(2)}, u32[]{:S(2)}) collective-permute-start(bf16[1792,256]{1,0:T(8,128)(2,1)} %bitcast.22), channel_id=1, source_target_pairs={{0,2},{1,4},{2,0},{3,6},{4,1},{5,7},{6,3},{7,5},{8,10},{9,12},{10,... | collective-permute-start | bytes 2752520 | tf_op jit(solution)/shard_map/ppermute | solution.py:27
  9.5 2.5 %shard_map.106 = bf16[8,40,1920]{2,1,0:T(8,128)(2,1)} custom-call(s32[1,64]{1,0:T(1,128)S(1)} %bitcast.35, f32[64,1]{1,0:T(8,128)S(1)} %copy.13.refs_1_, bf16[64,3584]{1,0:T(8,128)(2,1)S(1)} %bitcast.30, bf16[64,3584]{1,0:T(8,128)(2,1)S(1)} %bitcast.31), custom_call_target="tpu_custom_call" | custom-call | tf_op jit(solution)/shard_map/pallas_call | solution.py:58
  12.0 13.1 %all-to-all-start = ((bf16[8,40,1920]{2,1,0:T(8,128)(2,1)}), bf16[8,40,1920]{2,1,0:T(8,128)(2,1)S(1)}, u32[]{:S(2)}, u32[]{:S(2)}) async-start(bf16[8,40,1920]{2,1,0:T(8,128)(2,1)} %shard_map.106), calls=%async_computation | async-start | bytes 2457600 | tf_op jit(solution)/shard_map/all_to_all | solution.py:44
  25.1 4.7 %collective-permute-start.2 = (bf16[256,1792]{1,0:T(8,128)(2,1)}, bf16[256,1792]{1,0:T(8,128)(2,1)S(1)}, u32[]{:S(2)}, u32[]{:S(2)}) collective-permute-start(bf16[256,1792]{1,0:T(8,128)(2,1)} %bitcast.11.refs_6_.refs_11_), channel_id=1, source_target_pairs={{0,2},{1,4},{2,0},{3,6},{4,1},{5,7},{6,3},{7,5},{8,10},{9,12},{10,... | collective-permute-start | bytes 2752520 | tf_op jit(solution)/shard_map/ppermute | solution.py:27
  33.7 24.4 %all-to-all-done = bf16[8,40,1920]{2,1,0:T(8,128)(2,1)S(1)} async-done(((bf16[8,40,1920]{2,1,0:T(8,128)(2,1)}), bf16[8,40,1920]{2,1,0:T(8,128)(2,1)S(1)}, u32[]{:S(2)}, u32[]{:S(2)}) %all-to-all-start) | async-done | bytes 1228832 | tf_op jit(solution)/shard_map/all_to_all | solution.py:44
  58.2 4.2 %all-to-all-start.1 = ((bf16[8,40,896]{2,1,0:T(8,128)(2,1)}), bf16[8,40,896]{2,1,0:T(8,128)(2,1)}, u32[]{:S(2)}, u32[]{:S(2)}) async-start(bf16[8,40,896]{2,1,0:T(8,128)(2,1)} %shard_map.105), calls=%async_computation.1 | async-start | bytes 1146880 | tf_op jit(solution)/shard_map/all_to_all | solution.py:44
  62.4 2.5 %collective-permute-start.5 = (bf16[320,1920]{1,0:T(8,128)(2,1)S(1)}, bf16[320,1920]{1,0:T(8,128)(2,1)}, u32[]{:S(2)}, u32[]{:S(2)}) collective-permute-start(bf16[320,1920]{1,0:T(8,128)(2,1)S(1)} %bitcast.18), channel_id=1, source_target_pairs={{0,1},{1,0},{2,3},{3,2},{4,5},{5,4},{6,7},{7,6},{8,9},{9,8},{10,11... | collective-permute-start | bytes 3686408 | tf_op jit(solution)/shard_map/ppermute | solution.py:27
  64.9 8.0 %collective-permute-start.7 = (bf16[256,1792]{1,0:T(8,128)(2,1)S(1)}, bf16[256,1792]{1,0:T(8,128)(2,1)}, u32[]{:S(2)}, u32[]{:S(2)}) collective-permute-start(bf16[256,1792]{1,0:T(8,128)(2,1)S(1)} %collective-permute-done.2.refs_7_.refs_3_.refs_12_), channel_id=1, source_target_pairs={{1,3},{3,1},{4,6},{6,4},{9,11},{11,9},{12,14},{14,12},{17,19},{19,... | collective-permute-start | bytes 2752520 | tf_op jit(solution)/shard_map/ppermute | solution.py:27
  72.9 8.4 %all-to-all-done.1 = bf16[8,40,896]{2,1,0:T(8,128)(2,1)} async-done(((bf16[8,40,896]{2,1,0:T(8,128)(2,1)}), bf16[8,40,896]{2,1,0:T(8,128)(2,1)}, u32[]{:S(2)}, u32[]{:S(2)}) %all-to-all-start.1) | async-done | bytes 573472 | tf_op jit(solution)/shard_map/all_to_all | solution.py:44
  83.8 4.6 %shard_map.108 = (f32[320,512]{1,0:T(8,128)S(1)}, f32[320,256]{1,0:T(8,128)S(1)}, bf16[320,768]{1,0:T(8,128)(2,1)S(1)}) custom-call(s32[1]{0:T(128)} %bitcast.3.refs_0_, bf16[320,1920]{1,0:T(8,128)(2,1)S(1)} %bitcast.19, bf16[320,1920]{1,0:T(8,128)(2,1)} %collective-permute-done.5.refs_2_, bf16[1792,256]{1,0:T(8,128)(2,1)S(1)} %bitcast.23, ...), custom_call_target="tpu_custom_call" | custom-call | tf_op jit(solution)/shard_map/pallas_call | solution.py:58
  90.7 3.4 %shard_map.107 = (f32[320,512]{1,0:T(8,128)S(1)}, bf16[320,512]{1,0:T(8,128)(2,1)S(1)}) custom-call(s32[1]{0:T(128)} %bitcast.3.refs_0_, bf16[320,896]{1,0:T(8,128)(2,1)} %bitcast.10.refs_1_, bf16[320,896]{1,0:T(8,128)(2,1)} %collective-permute-done.1.refs_2_, bf16[1792,256]{1,0:T(8,128)(2,1)S(1)} %bitcast.24, ...), custom_call_target="tpu_custom_call" | custom-call | tf_op jit(solution)/shard_map/pallas_call | solution.py:58
  94.1 3.1 %collective-permute-start.4 = (bf16[320,512]{1,0:T(8,128)(2,1)S(1)}, bf16[320,512]{1,0:T(8,128)(2,1)S(1)}, u32[]{:S(2)}, u32[]{:S(2)}) collective-permute-start(bf16[320,512]{1,0:T(8,128)(2,1)S(1)} %get-tuple-element.21), channel_id=1, source_target_pairs={{0,4},{1,5},{2,6},{3,7},{4,0},{5,1},{6,2},{7,3},{8,12},{9,13},{10,... | collective-permute-start | bytes 983048 | tf_op jit(solution)/shard_map/ppermute | solution.py:27
  97.2 3.0 %shard_map.109 = (f32[320,256]{1,0:T(8,128)S(1)}, bf16[320,256]{1,0:T(8,128)(2,1)S(1)}) custom-call(s32[1]{0:T(128)} %bitcast.3.refs_0_, bf16[320,1920]{1,0:T(8,128)(2,1)S(1)} %bitcast.20, bf16[320,1920]{1,0:T(8,128)(2,1)} %collective-permute-done.5.refs_2_, bf16[256,1792]{1,0:T(8,128)(2,1)S(1)} %collective-permute-done.2.refs_7_.refs_3_.refs_12_, ...), custom_call_target="tpu_custom_call" | custom-call | tf_op jit(solution)/shard_map/pallas_call | solution.py:58
  103.2 10.5 %collective-permute-done.8.refs_7_ = bf16[320,256]{1,0:T(8,128)(2,1)S(1)} collective-permute-done((bf16[320,256]{1,0:T(8,128)(2,1)S(1)}, bf16[320,256]{1,0:T(8,128)(2,1)S(1)}, u32[]{:S(2)}, u32[]{:S(2)}) %collective-permute-start.8) | collective-permute-done | bytes 163872 | tf_op jit(solution)/shard_map/ppermute | solution.py:27
  113.7 3.9 %shard_map.110 = (f32[320,1792]{1,0:T(8,128)S(1)}, bf16[320,1792]{1,0:T(8,128)(2,1)S(1)}) custom-call(s32[1]{0:T(128)} %bitcast.3.refs_0_, f32[320,512]{1,0:T(8,128)S(1)} %get-tuple-element.20.refs_1_, bf16[320,512]{1,0:T(8,128)(2,1)S(1)} %collective-permute-done.4.refs_2_, f32[320,512]{1,0:T(8,128)S(1)} %get-tuple-element.23.refs_3_, ...), custom_call_target="tpu_custom_call" | custom-call | tf_op jit(solution)/shard_map/pallas_call | solution.py:58
  117.6 2.7 %collective-permute-start.9 = (bf16[320,1792]{1,0:T(8,128)(2,1)S(1)}, bf16[320,1792]{1,0:T(8,128)(2,1)S(1)}, u32[]{:S(2)}, u32[]{:S(2)}) collective-permute-start(bf16[320,1792]{1,0:T(8,128)(2,1)S(1)} %get-tuple-element.31), channel_id=1, source_target_pairs={{0,1},{1,0},{2,3},{3,2},{4,5},{5,4},{6,7},{7,6},{8,9},{9,8},{10,11... | collective-permute-start | bytes 3440648 | tf_op jit(solution)/shard_map/ppermute | solution.py:27
  120.3 2.4 %collective-permute-done.9.refs_1_ = bf16[320,1792]{1,0:T(8,128)(2,1)S(1)} collective-permute-done((bf16[320,1792]{1,0:T(8,128)(2,1)S(1)}, bf16[320,1792]{1,0:T(8,128)(2,1)S(1)}, u32[]{:S(2)}, u32[]{:S(2)}) %collective-permute-start.9) | collective-permute-done | bytes 1146912 | tf_op jit(solution)/shard_map/ppermute | solution.py:27
  124.4 4.7 %collective-permute-start.12 = (bf16[320,896]{1,0:T(8,128)(2,1)S(1)}, bf16[320,896]{1,0:T(8,128)(2,1)S(1)}, u32[]{:S(2)}, u32[]{:S(2)}) collective-permute-start(bf16[320,896]{1,0:T(8,128)(2,1)S(1)} %get-tuple-element.33), channel_id=1, source_target_pairs={{0,480},{32,0},{64,32},{96,64},{128,96},{160,128},{192,160},{224,1... | collective-permute-start | bytes 1720328 | tf_op jit(solution)/shard_map/ppermute | solution.py:36
  129.2 4.6 %all-to-all-start.2 = ((bf16[8,40,896]{2,1,0:T(8,128)(2,1)}), bf16[8,40,896]{2,1,0:T(8,128)(2,1)S(1)}, u32[]{:S(2)}, u32[]{:S(2)}) async-start(bf16[8,40,896]{2,1,0:T(8,128)(2,1)} %bitcast.12), calls=%async_computation.2 | async-start | bytes 1146880 | tf_op jit(solution)/shard_map/all_to_all | solution.py:44
  133.7 7.4 %collective-permute-done.12.refs_0_ = bf16[320,896]{1,0:T(8,128)(2,1)S(1)} collective-permute-done((bf16[320,896]{1,0:T(8,128)(2,1)S(1)}, bf16[320,896]{1,0:T(8,128)(2,1)S(1)}, u32[]{:S(2)}, u32[]{:S(2)}) %collective-permute-start.12) | collective-permute-done | bytes 573472 | tf_op jit(solution)/shard_map/ppermute | solution.py:36
  142.0 10.8 %all-to-all-done.2 = bf16[8,40,896]{2,1,0:T(8,128)(2,1)S(1)} async-done(((bf16[8,40,896]{2,1,0:T(8,128)(2,1)}), bf16[8,40,896]{2,1,0:T(8,128)(2,1)S(1)}, u32[]{:S(2)}, u32[]{:S(2)}) %all-to-all-start.2) | async-done | bytes 573472 | tf_op jit(solution)/shard_map/all_to_all | solution.py:44
  152.7 3.7 %all-to-all-start.3 = ((bf16[8,40,896]{2,1,0:T(8,128)(2,1)}), bf16[8,40,896]{2,1,0:T(8,128)(2,1)S(1)}, u32[]{:S(2)}, u32[]{:S(2)}) async-start(bf16[8,40,896]{2,1,0:T(8,128)(2,1)} %bitcast.37), calls=%async_computation.3 | async-start | bytes 1146880 | tf_op jit(solution)/shard_map/all_to_all | solution.py:44
  159.7 6.9 %collective-permute-start.11 = (s32[1,64]{1,0:T(1,128)S(1)}, s32[1,64]{1,0:T(1,128)S(1)}, u32[]{:S(2)}, u32[]{:S(2)}) collective-permute-start(s32[1,64]{1,0:T(1,128)S(1)} %bitcast.36), channel_id=1, source_target_pairs={{0,480},{32,0},{64,32},{96,64},{128,96},{160,128},{192,160},{224,1... | collective-permute-start | bytes 776 | tf_op jit(solution)/shard_map/ppermute | solution.py:36
  166.6 8.2 %collective-permute-done.10 = bf16[1,64,3584]{2,1,0:T(8,128)(2,1)S(1)} collective-permute-done((bf16[1,64,3584]{2,1,0:T(8,128)(2,1)S(1)}, bf16[1,64,3584]{2,1,0:T(8,128)(2,1)S(1)}, u32[]{:S(2)}, u32[]{:S(2)}) %collective-permute-start.10) | collective-permute-done | bytes 458784 | tf_op jit(solution)/shard_map/ppermute | solution.py:36
  (48 shorter events, 23.7 us)
Async XLA Ops:
  0.6 31.1 %collective-permute-start = (bf16[1792,256]{1,0:T(8,128)(2,1)}, bf16[1792,256]{1,0:T(8,128)(2,1)}, u32[]{:S(2)}, u32[]{:S(2)}) collective-permute-start(bf16[1792,256]{1,0:T(8,128)(2,1)} %bitcast.22), channel_id=1, source_target_pairs={{0,2},{1,4},{2,0},{3,6},{4,1},{5,7},{6,3},{7,5},{8,10},{9,12},{10,... | collective-permute-start | bytes 2752520 | tf_op jit(solution)/shard_map/ppermute | solution.py:27
  12.0 17.8 %copy-start.2 = (bf16[1,64,3584]{2,1,0:T(8,128)(2,1)S(1)}, bf16[1,64,3584]{2,1,0:T(8,128)(2,1)}, u32[]{:S(2)}) copy-start(bf16[1,64,3584]{2,1,0:T(8,128)(2,1)} %param.9) | copy-start | bytes 1376260
  12.0 17.8 %copy-start.6 = (s32[1,64,1]{1,2,0:T(1,128)S(1)}, s32[1,64,1]{1,2,0:T(1,128)}, u32[]{:S(2)}) copy-start(s32[1,64,1]{1,2,0:T(1,128)} %param.12) | copy-start | bytes 772
  12.0 46.2 %all-to-all-start = ((bf16[8,40,1920]{2,1,0:T(8,128)(2,1)}), bf16[8,40,1920]{2,1,0:T(8,128)(2,1)S(1)}, u32[]{:S(2)}, u32[]{:S(2)}) async-start(bf16[8,40,1920]{2,1,0:T(8,128)(2,1)} %shard_map.106), calls=%async_computation | async-start | bytes 2457600 | tf_op jit(solution)/shard_map/all_to_all | solution.py:44
  25.1 39.8 %collective-permute-start.2 = (bf16[256,1792]{1,0:T(8,128)(2,1)}, bf16[256,1792]{1,0:T(8,128)(2,1)S(1)}, u32[]{:S(2)}, u32[]{:S(2)}) collective-permute-start(bf16[256,1792]{1,0:T(8,128)(2,1)} %bitcast.11.refs_6_.refs_11_), channel_id=1, source_target_pairs={{0,2},{1,4},{2,0},{3,6},{4,1},{5,7},{6,3},{7,5},{8,10},{9,12},{10,... | collective-permute-start | bytes 2752520 | tf_op jit(solution)/shard_map/ppermute | solution.py:27
  31.8 33.1 %collective-permute-start.3 = (bf16[1792,256]{1,0:T(8,128)(2,1)}, bf16[1792,256]{1,0:T(8,128)(2,1)}, u32[]{:S(2)}, u32[]{:S(2)}) collective-permute-start(bf16[1792,256]{1,0:T(8,128)(2,1)} %collective-permute-done.refs_1_.refs_4_.refs_9_), channel_id=1, source_target_pairs={{1,3},{3,1},{4,6},{6,4},{9,11},{11,9},{12,14},{14,12},{17,19},{19,... | collective-permute-start | bytes 2752520 | tf_op jit(solution)/shard_map/ppermute | solution.py:27
  33.7 50.1 %copy-start = (bf16[1,1,1792,256]{3,2,1,0:T(8,128)(2,1)S(1)}, bf16[1,1,1792,256]{3,2,1,0:T(8,128)(2,1)}, u32[]{:S(2)}) copy-start(bf16[1,1,1792,256]{3,2,1,0:T(8,128)(2,1)} %param.16) | copy-start | bytes 2752516
  58.2 23.2 %all-to-all-start.1 = ((bf16[8,40,896]{2,1,0:T(8,128)(2,1)}), bf16[8,40,896]{2,1,0:T(8,128)(2,1)}, u32[]{:S(2)}, u32[]{:S(2)}) async-start(bf16[8,40,896]{2,1,0:T(8,128)(2,1)} %shard_map.105), calls=%async_computation.1 | async-start | bytes 1146880 | tf_op jit(solution)/shard_map/all_to_all | solution.py:44
  62.4 21.4 %collective-permute-start.5 = (bf16[320,1920]{1,0:T(8,128)(2,1)S(1)}, bf16[320,1920]{1,0:T(8,128)(2,1)}, u32[]{:S(2)}, u32[]{:S(2)}) collective-permute-start(bf16[320,1920]{1,0:T(8,128)(2,1)S(1)} %bitcast.18), channel_id=1, source_target_pairs={{0,1},{1,0},{2,3},{3,2},{4,5},{5,4},{6,7},{7,6},{8,9},{9,8},{10,11... | collective-permute-start | bytes 3686408 | tf_op jit(solution)/shard_map/ppermute | solution.py:27
  64.9 32.3 %collective-permute-start.7 = (bf16[256,1792]{1,0:T(8,128)(2,1)S(1)}, bf16[256,1792]{1,0:T(8,128)(2,1)}, u32[]{:S(2)}, u32[]{:S(2)}) collective-permute-start(bf16[256,1792]{1,0:T(8,128)(2,1)S(1)} %collective-permute-done.2.refs_7_.refs_3_.refs_12_), channel_id=1, source_target_pairs={{1,3},{3,1},{4,6},{6,4},{9,11},{11,9},{12,14},{14,12},{17,19},{19,... | collective-permute-start | bytes 2752520 | tf_op jit(solution)/shard_map/ppermute | solution.py:27
  81.4 9.3 %collective-permute-start.1 = (bf16[320,896]{1,0:T(8,128)(2,1)}, bf16[320,896]{1,0:T(8,128)(2,1)}, u32[]{:S(2)}, u32[]{:S(2)}) collective-permute-start(bf16[320,896]{1,0:T(8,128)(2,1)} %bitcast.10.refs_1_), channel_id=1, source_target_pairs={{0,1},{1,0},{2,3},{3,2},{4,5},{5,4},{6,7},{7,6},{8,9},{9,8},{10,11... | collective-permute-start | bytes 1720328 | tf_op jit(solution)/shard_map/ppermute | solution.py:27
  88.4 14.7 %collective-permute-start.6 = (bf16[320,768]{1,0:T(8,128)(2,1)S(1)}, bf16[320,768]{1,0:T(8,128)(2,1)S(1)}, u32[]{:S(2)}, u32[]{:S(2)}) collective-permute-start(bf16[320,768]{1,0:T(8,128)(2,1)S(1)} %get-tuple-element.25), channel_id=1, source_target_pairs={{0,4},{1,5},{2,6},{3,7},{4,0},{5,1},{6,2},{7,3},{8,12},{9,13},{10,... | collective-permute-start | bytes 1474568 | tf_op jit(solution)/shard_map/ppermute | solution.py:27
  94.1 19.6 %collective-permute-start.4 = (bf16[320,512]{1,0:T(8,128)(2,1)S(1)}, bf16[320,512]{1,0:T(8,128)(2,1)S(1)}, u32[]{:S(2)}, u32[]{:S(2)}) collective-permute-start(bf16[320,512]{1,0:T(8,128)(2,1)S(1)} %get-tuple-element.21), channel_id=1, source_target_pairs={{0,4},{1,5},{2,6},{3,7},{4,0},{5,1},{6,2},{7,3},{8,12},{9,13},{10,... | collective-permute-start | bytes 983048 | tf_op jit(solution)/shard_map/ppermute | solution.py:27
  100.2 13.5 %collective-permute-start.8 = (bf16[320,256]{1,0:T(8,128)(2,1)S(1)}, bf16[320,256]{1,0:T(8,128)(2,1)S(1)}, u32[]{:S(2)}, u32[]{:S(2)}) collective-permute-start(bf16[320,256]{1,0:T(8,128)(2,1)S(1)} %get-tuple-element.29), channel_id=1, source_target_pairs={{0,4},{1,5},{2,6},{3,7},{4,0},{5,1},{6,2},{7,3},{8,12},{9,13},{10,... | collective-permute-start | bytes 491528 | tf_op jit(solution)/shard_map/ppermute | solution.py:27
  117.6 5.1 %collective-permute-start.9 = (bf16[320,1792]{1,0:T(8,128)(2,1)S(1)}, bf16[320,1792]{1,0:T(8,128)(2,1)S(1)}, u32[]{:S(2)}, u32[]{:S(2)}) collective-permute-start(bf16[320,1792]{1,0:T(8,128)(2,1)S(1)} %get-tuple-element.31), channel_id=1, source_target_pairs={{0,1},{1,0},{2,3},{3,2},{4,5},{5,4},{6,7},{7,6},{8,9},{9,8},{10,11... | collective-permute-start | bytes 3440648 | tf_op jit(solution)/shard_map/ppermute | solution.py:27
  124.4 16.7 %collective-permute-start.12 = (bf16[320,896]{1,0:T(8,128)(2,1)S(1)}, bf16[320,896]{1,0:T(8,128)(2,1)S(1)}, u32[]{:S(2)}, u32[]{:S(2)}) collective-permute-start(bf16[320,896]{1,0:T(8,128)(2,1)S(1)} %get-tuple-element.33), channel_id=1, source_target_pairs={{0,480},{32,0},{64,32},{96,64},{128,96},{160,128},{192,160},{224,1... | collective-permute-start | bytes 1720328 | tf_op jit(solution)/shard_map/ppermute | solution.py:36
  129.2 23.6 %all-to-all-start.2 = ((bf16[8,40,896]{2,1,0:T(8,128)(2,1)}), bf16[8,40,896]{2,1,0:T(8,128)(2,1)S(1)}, u32[]{:S(2)}, u32[]{:S(2)}) async-start(bf16[8,40,896]{2,1,0:T(8,128)(2,1)} %bitcast.12), calls=%async_computation.2 | async-start | bytes 1146880 | tf_op jit(solution)/shard_map/all_to_all | solution.py:44
  133.7 22.7 %copy-start.11 = (f32[1,64,1]{1,2,0:T(1,128)S(1)}, f32[1,64,1]{1,2,0:T(1,128)}, u32[]{:S(2)}) copy-start(f32[1,64,1]{1,2,0:T(1,128)} %param.14) | copy-start | bytes 772
  133.7 22.8 %copy-start.7 = (s32[1,64,1]{1,2,0:T(1,128)S(1)}, s32[1,64,1]{1,2,0:T(1,128)}, u32[]{:S(2)}) copy-start(s32[1,64,1]{1,2,0:T(1,128)} %param.12) | copy-start | bytes 772
  142.0 14.6 %copy-start.3 = (bf16[1,64,3584]{2,1,0:T(8,128)(2,1)S(1)}, bf16[1,64,3584]{2,1,0:T(8,128)(2,1)}, u32[]{:S(2)}) copy-start(bf16[1,64,3584]{2,1,0:T(8,128)(2,1)} %param.9) | copy-start | bytes 1376260
  152.7 6.9 %copy-start.9 = (s32[1,64,1]{1,2,0:T(1,128)S(1)}, s32[1,64,1]{1,2,0:T(1,128)}, u32[]{:S(2)}) copy-start(s32[1,64,1]{1,2,0:T(1,128)} %param.13) | copy-start | bytes 772
  152.7 22.6 %all-to-all-start.3 = ((bf16[8,40,896]{2,1,0:T(8,128)(2,1)}), bf16[8,40,896]{2,1,0:T(8,128)(2,1)S(1)}, u32[]{:S(2)}, u32[]{:S(2)}) async-start(bf16[8,40,896]{2,1,0:T(8,128)(2,1)} %bitcast.37), calls=%async_computation.3 | async-start | bytes 1146880 | tf_op jit(solution)/shard_map/all_to_all | solution.py:44
  157.3 17.4 %collective-permute-start.10 = (bf16[1,64,3584]{2,1,0:T(8,128)(2,1)S(1)}, bf16[1,64,3584]{2,1,0:T(8,128)(2,1)S(1)}, u32[]{:S(2)}, u32[]{:S(2)}) collective-permute-start(bf16[1,64,3584]{2,1,0:T(8,128)(2,1)S(1)} %bitcast.32), channel_id=1, source_target_pairs={{0,32},{32,64},{64,96},{96,128},{128,160},{160,192},{192,224},{224... | collective-permute-start | bytes 1376264 | tf_op jit(solution)/shard_map/ppermute | solution.py:36
  159.7 15.1 %collective-permute-start.11 = (s32[1,64]{1,0:T(1,128)S(1)}, s32[1,64]{1,0:T(1,128)S(1)}, u32[]{:S(2)}, u32[]{:S(2)}) collective-permute-start(s32[1,64]{1,0:T(1,128)S(1)} %bitcast.36), channel_id=1, source_target_pairs={{0,480},{32,0},{64,32},{96,64},{128,96},{160,128},{192,160},{224,1... | collective-permute-start | bytes 776 | tf_op jit(solution)/shard_map/ppermute | solution.py:36
  (5 other events, 4.4 us)

commit v5 on v3

--- a/solution.py
+++ b/solution.py
@@ -310,8 +310,16 @@
     next_b = gate(next_b)
     (y,) = call(merge_fwd_body, [((tokens, 2 * features), BF16)], routes_f, probs_f, rows_f, home_f)
     home_b = ring_exchange(next_b)
-    (dx,) = call(merge_bwd_body, [((tokens, 2 * features), BF16)], next_routes, home_b)
-    return from_behind(y[None], 1), dx[None]
+    passed = from_behind(y[None], 1)
+    dx, passed = pl.pallas_call(
+        lambda routes, got, _, out, __: merge_bwd_body(routes, got, out),
+        out_shape=[jax.ShapeDtypeStruct((tokens, 2 * features), BF16), jax.ShapeDtypeStruct(passed.shape, BF16)],
+        in_specs=[pl.BlockSpec(memory_space=m) for m in (pltpu.VMEM, pltpu.VMEM, pl.ANY)],
+        out_specs=[pl.BlockSpec(memory_space=m) for m in (pltpu.VMEM, pl.ANY)],
+        input_output_aliases={2: 1},
+        compiler_params=pltpu.CompilerParams(vmem_limit_bytes=LIMIT),
+    )(next_routes, home_b, passed)
+    return passed, dx[None]
 
 
 def solution(mesh):

time: 179 us -> 179 us (level)
    pallas_call x10 -> x9, Pallas kernels: 23.2 us -> 21.6 us  [call(): pl.pallas_call(run, out_shape=shapes, in_specs=lead + [pl.BlockSpec(memor...]
  transfers between devices with their start and end apart: 18 -> 18, of which waited for: 8 -> 9; matrix products, arithmetic and copies ran while one was open for 0% -> 0% of each run, Pallas kernels for 9% -> 9%
where the time goes in v5:
time: 179 us; the launch traced here: 178 us
  starting transfers between devices  78.4 us (44%)
  waiting for transfers between devices  69.4 us (39%)
  Pallas kernels  23.2 us (13%)
  local copies, waits for them, and re-layouts  6 us (3%)
    all_to_all x4, waiting for transfers between devices, ring_exchange(): lax.all_to_all(cut, 'expert', split_axis=0, concat_axis=0, tiled=True, ax...  44.9 us
    ppermute x11, starting transfers between devices, swap(): lax.ppermute(value, 'expert', [(i, i ^ m) for i, m in enumerate(masks) if...  38.5 us
    all_to_all x4, starting transfers between devices, ring_exchange(): lax.all_to_all(cut, 'expert', split_axis=0, concat_axis=0, tiled=True, ax...  26 us
    pallas_call x9, Pallas kernels, call(): pl.pallas_call(run, out_shape=shapes, in_specs=lead + [pl.BlockSpec(memor...  21.6 us
    ppermute x3, waiting for transfers between devices, from_behind(): lax.ppermute(value, 'pipe', [(i, (i + steps) % count) for i in range(coun...  15.1 us
    ppermute x3, starting transfers between devices, from_behind(): lax.ppermute(value, 'pipe', [(i, (i + steps) % count) for i in range(coun...  13.9 us
    ppermute x11, waiting for transfers between devices, swap(): lax.ppermute(value, 'expert', [(i, i ^ m) for i, m in enumerate(masks) if...  9.4 us
    unnamed x25, local copies, waits for them, and re-layouts  5.16 us
  transfers between devices with their start and end apart: 18, of which 9 were waited for; matrix products, arithmetic and copies ran while one was open for 0% of the time, Pallas kernels for 9%

profile of v5, /device:TPU:1, one launch (start us, length us, event | category | flops | bytes accessed | tf_op | source)
XLA Modules:
  0.0 177.9 jit_solution(15882736276530053436)
XLA Ops:
  0.6 5.4 %collective-permute-start.1 = (bf16[1792,256]{1,0:T(8,128)(2,1)}, bf16[1792,256]{1,0:T(8,128)(2,1)}, u32[]{:S(2)}, u32[]{:S(2)}) collective-permute-start(bf16[1792,256]{1,0:T(8,128)(2,1)} %bitcast.23), channel_id=1, source_target_pairs={{0,2},{1,4},{2,0},{3,6},{4,1},{5,7},{6,3},{7,5},{8,10},{9,12},{10,... | collective-permute-start | bytes 2752520 | tf_op jit(solution)/shard_map/ppermute | solution.py:27
  12.0 13.1 %all-to-all-start = ((bf16[8,40,1920]{2,1,0:T(8,128)(2,1)}), bf16[8,40,1920]{2,1,0:T(8,128)(2,1)S(1)}, u32[]{:S(2)}, u32[]{:S(2)}) async-start(bf16[8,40,1920]{2,1,0:T(8,128)(2,1)} %shard_map.106), calls=%async_computation | async-start | bytes 2457600 | tf_op jit(solution)/shard_map/all_to_all | solution.py:44
  25.1 4.7 %collective-permute-start.3 = (bf16[256,1792]{1,0:T(8,128)(2,1)}, bf16[256,1792]{1,0:T(8,128)(2,1)S(1)}, u32[]{:S(2)}, u32[]{:S(2)}) collective-permute-start(bf16[256,1792]{1,0:T(8,128)(2,1)} %bitcast.10.refs_3_.refs_12_), channel_id=1, source_target_pairs={{0,2},{1,4},{2,0},{3,6},{4,1},{5,7},{6,3},{7,5},{8,10},{9,12},{10,... | collective-permute-start | bytes 2752520 | tf_op jit(solution)/shard_map/ppermute | solution.py:27
  33.7 24.5 %all-to-all-done = bf16[8,40,1920]{2,1,0:T(8,128)(2,1)S(1)} async-done(((bf16[8,40,1920]{2,1,0:T(8,128)(2,1)}), bf16[8,40,1920]{2,1,0:T(8,128)(2,1)S(1)}, u32[]{:S(2)}, u32[]{:S(2)}) %all-to-all-start) | async-done | bytes 1228832 | tf_op jit(solution)/shard_map/all_to_all | solution.py:44
  58.2 4.2 %all-to-all-start.1 = ((bf16[8,40,896]{2,1,0:T(8,128)(2,1)}), bf16[8,40,896]{2,1,0:T(8,128)(2,1)}, u32[]{:S(2)}, u32[]{:S(2)}) async-start(bf16[8,40,896]{2,1,0:T(8,128)(2,1)} %shard_map.105), calls=%async_computation.1 | async-start | bytes 1146880 | tf_op jit(solution)/shard_map/all_to_all | solution.py:44
  64.9 7.9 %collective-permute-start.8 = (bf16[256,1792]{1,0:T(8,128)(2,1)S(1)}, bf16[256,1792]{1,0:T(8,128)(2,1)}, u32[]{:S(2)}, u32[]{:S(2)}) collective-permute-start(bf16[256,1792]{1,0:T(8,128)(2,1)S(1)} %collective-permute-done.3.refs_4_.refs_3_.refs_13_), channel_id=1, source_target_pairs={{1,3},{3,1},{4,6},{6,4},{9,11},{11,9},{12,14},{14,12},{17,19},{19,... | collective-permute-start | bytes 2752520 | tf_op jit(solution)/shard_map/ppermute | solution.py:27
  72.8 8.5 %all-to-all-done.1 = bf16[8,40,896]{2,1,0:T(8,128)(2,1)} async-done(((bf16[8,40,896]{2,1,0:T(8,128)(2,1)}), bf16[8,40,896]{2,1,0:T(8,128)(2,1)}, u32[]{:S(2)}, u32[]{:S(2)}) %all-to-all-start.1) | async-done | bytes 573472 | tf_op jit(solution)/shard_map/all_to_all | solution.py:44
  83.8 2.7 %shard_map.109 = (f32[320,256]{1,0:T(8,128)S(1)}, bf16[320,256]{1,0:T(8,128)(2,1)S(1)}) custom-call(s32[1]{0:T(128)} %bitcast.1.refs_0_, bf16[320,1920]{1,0:T(8,128)(2,1)S(1)} %bitcast.19, bf16[320,1920]{1,0:T(8,128)(2,1)S(1)} %collective-permute-done.6.refs_2_, bf16[256,1792]{1,0:T(8,128)(2,1)} %bitcast.10.refs_3_.refs_12_, ...), custom_call_target="tpu_custom_call" | custom-call | tf_op jit(solution)/shard_map/pallas_call | solution.py:58
  88.8 2.8 %shard_map.108 = (f32[320,512]{1,0:T(8,128)S(1)}, bf16[320,512]{1,0:T(8,128)(2,1)S(1)}) custom-call(s32[1]{0:T(128)} %bitcast.1.refs_0_, bf16[320,1920]{1,0:T(8,128)(2,1)S(1)} %bitcast.20, bf16[320,1920]{1,0:T(8,128)(2,1)S(1)} %collective-permute-done.6.refs_2_, bf16[1792,256]{1,0:T(8,128)(2,1)S(1)} %bitcast.24, ...), custom_call_target="tpu_custom_call" | custom-call | tf_op jit(solution)/shard_map/pallas_call | solution.py:58
  91.6 3.1 %collective-permute-start.7 = (bf16[320,512]{1,0:T(8,128)(2,1)S(1)}, bf16[320,512]{1,0:T(8,128)(2,1)S(1)}, u32[]{:S(2)}, u32[]{:S(2)}) collective-permute-start(bf16[320,512]{1,0:T(8,128)(2,1)S(1)} %get-tuple-element.28), channel_id=1, source_target_pairs={{0,4},{1,5},{2,6},{3,7},{4,0},{5,1},{6,2},{7,3},{8,12},{9,13},{10,... | collective-permute-start | bytes 983048 | tf_op jit(solution)/shard_map/ppermute | solution.py:27
  94.7 3.4 %shard_map.107 = (f32[320,512]{1,0:T(8,128)S(1)}, bf16[320,512]{1,0:T(8,128)(2,1)S(1)}) custom-call(s32[1]{0:T(128)} %bitcast.1.refs_0_, bf16[320,896]{1,0:T(8,128)(2,1)} %bitcast.9.refs_1_, bf16[320,896]{1,0:T(8,128)(2,1)} %collective-permute-done.2.refs_2_, bf16[1792,256]{1,0:T(8,128)(2,1)S(1)} %bitcast.25, ...), custom_call_target="tpu_custom_call" | custom-call | tf_op jit(solution)/shard_map/pallas_call | solution.py:58
  103.0 3.3 %collective-permute-start.10 = (bf16[320,256]{1,0:T(8,128)(2,1)S(1)}, bf16[320,256]{1,0:T(8,128)(2,1)S(1)}, u32[]{:S(2)}, u32[]{:S(2)}) collective-permute-start(bf16[320,256]{1,0:T(8,128)(2,1)S(1)} %get-tuple-element.35), channel_id=1, source_target_pairs={{0,4},{1,5},{2,6},{3,7},{4,0},{5,1},{6,2},{7,3},{8,12},{9,13},{10,... | collective-permute-start | bytes 491528 | tf_op jit(solution)/shard_map/ppermute | solution.py:27
  106.3 7.0 %collective-permute-done.10.refs_8_ = bf16[320,256]{1,0:T(8,128)(2,1)S(1)} collective-permute-done((bf16[320,256]{1,0:T(8,128)(2,1)S(1)}, bf16[320,256]{1,0:T(8,128)(2,1)S(1)}, u32[]{:S(2)}, u32[]{:S(2)}) %collective-permute-start.10) | collective-permute-done | bytes 163872 | tf_op jit(solution)/shard_map/ppermute | solution.py:27
  113.3 3.9 %shard_map.111 = (f32[320,1792]{1,0:T(8,128)S(1)}, bf16[320,1792]{1,0:T(8,128)(2,1)S(1)}) custom-call(s32[1]{0:T(128)} %bitcast.1.refs_0_, f32[320,512]{1,0:T(8,128)S(1)} %get-tuple-element.24.refs_1_, bf16[320,512]{1,0:T(8,128)(2,1)S(1)} %collective-permute-done.5.refs_2_, f32[320,512]{1,0:T(8,128)S(1)} %get-tuple-element.27.refs_3_, ...), custom_call_target="tpu_custom_call" | custom-call | tf_op jit(solution)/shard_map/pallas_call | solution.py:58
  117.1 2.8 %collective-permute-start.11 = (bf16[320,1792]{1,0:T(8,128)(2,1)S(1)}, bf16[320,1792]{1,0:T(8,128)(2,1)S(1)}, u32[]{:S(2)}, u32[]{:S(2)}) collective-permute-start(bf16[320,1792]{1,0:T(8,128)(2,1)S(1)} %get-tuple-element.37), channel_id=1, source_target_pairs={{0,1},{1,0},{2,3},{3,2},{4,5},{5,4},{6,7},{7,6},{8,9},{9,8},{10,11... | collective-permute-start | bytes 3440648 | tf_op jit(solution)/shard_map/ppermute | solution.py:27
  124.1 4.7 %collective-permute-start.12 = (bf16[320,896]{1,0:T(8,128)(2,1)S(1)}, bf16[320,896]{1,0:T(8,128)(2,1)S(1)}, u32[]{:S(2)}, u32[]{:S(2)}) collective-permute-start(bf16[320,896]{1,0:T(8,128)(2,1)S(1)} %get-tuple-element.38), channel_id=1, source_target_pairs={{0,480},{32,0},{64,32},{96,64},{128,96},{160,128},{192,160},{224,1... | collective-permute-start | bytes 1720328 | tf_op jit(solution)/shard_map/ppermute | solution.py:36
  128.8 5.0 %all-to-all-start.3 = ((bf16[8,40,896]{2,1,0:T(8,128)(2,1)}), bf16[8,40,896]{2,1,0:T(8,128)(2,1)S(1)}, u32[]{:S(2)}, u32[]{:S(2)}) async-start(bf16[8,40,896]{2,1,0:T(8,128)(2,1)} %bitcast.14), calls=%async_computation.3 | async-start | bytes 1146880 | tf_op jit(solution)/shard_map/all_to_all | solution.py:44
  133.9 6.9 %collective-permute-done.12.refs_0_ = bf16[320,896]{1,0:T(8,128)(2,1)S(1)} collective-permute-done((bf16[320,896]{1,0:T(8,128)(2,1)S(1)}, bf16[320,896]{1,0:T(8,128)(2,1)S(1)}, u32[]{:S(2)}, u32[]{:S(2)}) %collective-permute-start.12) | collective-permute-done | bytes 573472 | tf_op jit(solution)/shard_map/ppermute | solution.py:36
  141.6 11.2 %all-to-all-done.3 = bf16[8,40,896]{2,1,0:T(8,128)(2,1)S(1)} async-done(((bf16[8,40,896]{2,1,0:T(8,128)(2,1)}), bf16[8,40,896]{2,1,0:T(8,128)(2,1)S(1)}, u32[]{:S(2)}, u32[]{:S(2)}) %all-to-all-start.3) | async-done | bytes 573472 | tf_op jit(solution)/shard_map/all_to_all | solution.py:44
  152.9 3.7 %all-to-all-start.2 = ((bf16[8,40,896]{2,1,0:T(8,128)(2,1)}), bf16[8,40,896]{2,1,0:T(8,128)(2,1)S(1)}, u32[]{:S(2)}, u32[]{:S(2)}) async-start(bf16[8,40,896]{2,1,0:T(8,128)(2,1)} %bitcast.38), calls=%async_computation.2 | async-start | bytes 1146880 | tf_op jit(solution)/shard_map/all_to_all | solution.py:44
  157.5 2.7 %collective-permute-start.13 = (bf16[1,64,3584]{2,1,0:T(8,128)(2,1)S(1)}, bf16[1,64,3584]{2,1,0:T(8,128)(2,1)S(1)}, u32[]{:S(2)}, u32[]{:S(2)}) collective-permute-start(bf16[1,64,3584]{2,1,0:T(8,128)(2,1)S(1)} %bitcast.33), channel_id=1, source_target_pairs={{0,32},{32,64},{64,96},{96,128},{128,160},{160,192},{192,224},{224... | collective-permute-start | bytes 1376264 | tf_op jit(solution)/shard_map/ppermute | solution.py:36
  160.2 6.5 %collective-permute-start = (s32[1,64]{1,0:T(1,128)S(1)}, s32[1,64]{1,0:T(1,128)S(1)}, u32[]{:S(2)}, u32[]{:S(2)}) collective-permute-start(s32[1,64]{1,0:T(1,128)S(1)} %bitcast.37), channel_id=1, source_target_pairs={{0,480},{32,0},{64,32},{96,64},{128,96},{160,128},{192,160},{224,1... | collective-permute-start | bytes 776 | tf_op jit(solution)/shard_map/ppermute | solution.py:36
  166.7 2.9 %collective-permute-done.routes = s32[1,64]{1,0:T(1,128)S(1)} collective-permute-done((s32[1,64]{1,0:T(1,128)S(1)}, s32[1,64]{1,0:T(1,128)S(1)}, u32[]{:S(2)}, u32[]{:S(2)}) %collective-permute-start) | collective-permute-done | bytes 288 | tf_op jit(solution)/shard_map/ppermute | solution.py:36
  169.6 5.2 %collective-permute-done.13._ = bf16[1,64,3584]{2,1,0:T(8,128)(2,1)S(1)} collective-permute-done((bf16[1,64,3584]{2,1,0:T(8,128)(2,1)S(1)}, bf16[1,64,3584]{2,1,0:T(8,128)(2,1)S(1)}, u32[]{:S(2)}, u32[]{:S(2)}) %collective-permute-start.13) | collective-permute-done | bytes 458784 | tf_op jit(solution)/shard_map/ppermute | solution.py:36
  (51 shorter events, 30.7 us)
Async XLA Ops:
  0.6 31.1 %collective-permute-start.1 = (bf16[1792,256]{1,0:T(8,128)(2,1)}, bf16[1792,256]{1,0:T(8,128)(2,1)}, u32[]{:S(2)}, u32[]{:S(2)}) collective-permute-start(bf16[1792,256]{1,0:T(8,128)(2,1)} %bitcast.23), channel_id=1, source_target_pairs={{0,2},{1,4},{2,0},{3,6},{4,1},{5,7},{6,3},{7,5},{8,10},{9,12},{10,... | collective-permute-start | bytes 2752520 | tf_op jit(solution)/shard_map/ppermute | solution.py:27
  12.0 17.8 %copy-start.2 = (bf16[1,64,3584]{2,1,0:T(8,128)(2,1)S(1)}, bf16[1,64,3584]{2,1,0:T(8,128)(2,1)}, u32[]{:S(2)}) copy-start(bf16[1,64,3584]{2,1,0:T(8,128)(2,1)} %param.9) | copy-start | bytes 1376260
  12.0 17.8 %copy-start.6 = (s32[1,64,1]{1,2,0:T(1,128)S(1)}, s32[1,64,1]{1,2,0:T(1,128)}, u32[]{:S(2)}) copy-start(s32[1,64,1]{1,2,0:T(1,128)} %param.12) | copy-start | bytes 772
  12.0 46.2 %all-to-all-start = ((bf16[8,40,1920]{2,1,0:T(8,128)(2,1)}), bf16[8,40,1920]{2,1,0:T(8,128)(2,1)S(1)}, u32[]{:S(2)}, u32[]{:S(2)}) async-start(bf16[8,40,1920]{2,1,0:T(8,128)(2,1)} %shard_map.106), calls=%async_computation | async-start | bytes 2457600 | tf_op jit(solution)/shard_map/all_to_all | solution.py:44
  25.1 39.8 %collective-permute-start.3 = (bf16[256,1792]{1,0:T(8,128)(2,1)}, bf16[256,1792]{1,0:T(8,128)(2,1)S(1)}, u32[]{:S(2)}, u32[]{:S(2)}) collective-permute-start(bf16[256,1792]{1,0:T(8,128)(2,1)} %bitcast.10.refs_3_.refs_12_), channel_id=1, source_target_pairs={{0,2},{1,4},{2,0},{3,6},{4,1},{5,7},{6,3},{7,5},{8,10},{9,12},{10,... | collective-permute-start | bytes 2752520 | tf_op jit(solution)/shard_map/ppermute | solution.py:27
  31.8 33.1 %collective-permute-start.4 = (bf16[1792,256]{1,0:T(8,128)(2,1)}, bf16[1792,256]{1,0:T(8,128)(2,1)}, u32[]{:S(2)}, u32[]{:S(2)}) collective-permute-start(bf16[1792,256]{1,0:T(8,128)(2,1)} %collective-permute-done.1.refs_1_.refs_4_.refs_10_), channel_id=1, source_target_pairs={{1,3},{3,1},{4,6},{6,4},{9,11},{11,9},{12,14},{14,12},{17,19},{19,... | collective-permute-start | bytes 2752520 | tf_op jit(solution)/shard_map/ppermute | solution.py:27
  58.2 23.2 %all-to-all-start.1 = ((bf16[8,40,896]{2,1,0:T(8,128)(2,1)}), bf16[8,40,896]{2,1,0:T(8,128)(2,1)}, u32[]{:S(2)}, u32[]{:S(2)}) async-start(bf16[8,40,896]{2,1,0:T(8,128)(2,1)} %shard_map.105), calls=%async_computation.1 | async-start | bytes 1146880 | tf_op jit(solution)/shard_map/all_to_all | solution.py:44
  62.4 21.4 %collective-permute-start.6 = (bf16[320,1920]{1,0:T(8,128)(2,1)S(1)}, bf16[320,1920]{1,0:T(8,128)(2,1)S(1)}, u32[]{:S(2)}, u32[]{:S(2)}) collective-permute-start(bf16[320,1920]{1,0:T(8,128)(2,1)S(1)} %bitcast.18), channel_id=1, source_target_pairs={{0,1},{1,0},{2,3},{3,2},{4,5},{5,4},{6,7},{7,6},{8,9},{9,8},{10,11... | collective-permute-start | bytes 3686408 | tf_op jit(solution)/shard_map/ppermute | solution.py:27
  64.9 35.4 %collective-permute-start.8 = (bf16[256,1792]{1,0:T(8,128)(2,1)S(1)}, bf16[256,1792]{1,0:T(8,128)(2,1)}, u32[]{:S(2)}, u32[]{:S(2)}) collective-permute-start(bf16[256,1792]{1,0:T(8,128)(2,1)S(1)} %collective-permute-done.3.refs_4_.refs_3_.refs_13_), channel_id=1, source_target_pairs={{1,3},{3,1},{4,6},{6,4},{9,11},{11,9},{12,14},{14,12},{17,19},{19,... | collective-permute-start | bytes 2752520 | tf_op jit(solution)/shard_map/ppermute | solution.py:27
  81.4 13.3 %collective-permute-start.2 = (bf16[320,896]{1,0:T(8,128)(2,1)}, bf16[320,896]{1,0:T(8,128)(2,1)}, u32[]{:S(2)}, u32[]{:S(2)}) collective-permute-start(bf16[320,896]{1,0:T(8,128)(2,1)} %bitcast.9.refs_1_), channel_id=1, source_target_pairs={{0,1},{1,0},{2,3},{3,2},{4,5},{5,4},{6,7},{7,6},{8,9},{9,8},{10,11... | collective-permute-start | bytes 1720328 | tf_op jit(solution)/shard_map/ppermute | solution.py:27
  86.5 13.8 %collective-permute-start.9 = (bf16[320,256]{1,0:T(8,128)(2,1)S(1)}, bf16[320,256]{1,0:T(8,128)(2,1)S(1)}, u32[]{:S(2)}, u32[]{:S(2)}) collective-permute-start(bf16[320,256]{1,0:T(8,128)(2,1)S(1)} %get-tuple-element.31), channel_id=1, source_target_pairs={{0,4},{1,5},{2,6},{3,7},{4,0},{5,1},{6,2},{7,3},{8,12},{9,13},{10,... | collective-permute-start | bytes 491528 | tf_op jit(solution)/shard_map/ppermute | solution.py:27
  91.6 14.7 %collective-permute-start.7 = (bf16[320,512]{1,0:T(8,128)(2,1)S(1)}, bf16[320,512]{1,0:T(8,128)(2,1)S(1)}, u32[]{:S(2)}, u32[]{:S(2)}) collective-permute-start(bf16[320,512]{1,0:T(8,128)(2,1)S(1)} %get-tuple-element.28), channel_id=1, source_target_pairs={{0,4},{1,5},{2,6},{3,7},{4,0},{5,1},{6,2},{7,3},{8,12},{9,13},{10,... | collective-permute-start | bytes 983048 | tf_op jit(solution)/shard_map/ppermute | solution.py:27
  98.1 15.2 %collective-permute-start.5 = (bf16[320,512]{1,0:T(8,128)(2,1)S(1)}, bf16[320,512]{1,0:T(8,128)(2,1)S(1)}, u32[]{:S(2)}, u32[]{:S(2)}) collective-permute-start(bf16[320,512]{1,0:T(8,128)(2,1)S(1)} %get-tuple-element.25), channel_id=1, source_target_pairs={{0,4},{1,5},{2,6},{3,7},{4,0},{5,1},{6,2},{7,3},{8,12},{9,13},{10,... | collective-permute-start | bytes 983048 | tf_op jit(solution)/shard_map/ppermute | solution.py:27
  103.0 10.3 %collective-permute-start.10 = (bf16[320,256]{1,0:T(8,128)(2,1)S(1)}, bf16[320,256]{1,0:T(8,128)(2,1)S(1)}, u32[]{:S(2)}, u32[]{:S(2)}) collective-permute-start(bf16[320,256]{1,0:T(8,128)(2,1)S(1)} %get-tuple-element.35), channel_id=1, source_target_pairs={{0,4},{1,5},{2,6},{3,7},{4,0},{5,1},{6,2},{7,3},{8,12},{9,13},{10,... | collective-permute-start | bytes 491528 | tf_op jit(solution)/shard_map/ppermute | solution.py:27
  117.1 5.2 %collective-permute-start.11 = (bf16[320,1792]{1,0:T(8,128)(2,1)S(1)}, bf16[320,1792]{1,0:T(8,128)(2,1)S(1)}, u32[]{:S(2)}, u32[]{:S(2)}) collective-permute-start(bf16[320,1792]{1,0:T(8,128)(2,1)S(1)} %get-tuple-element.37), channel_id=1, source_target_pairs={{0,1},{1,0},{2,3},{3,2},{4,5},{5,4},{6,7},{7,6},{8,9},{9,8},{10,11... | collective-permute-start | bytes 3440648 | tf_op jit(solution)/shard_map/ppermute | solution.py:27
  124.1 16.7 %collective-permute-start.12 = (bf16[320,896]{1,0:T(8,128)(2,1)S(1)}, bf16[320,896]{1,0:T(8,128)(2,1)S(1)}, u32[]{:S(2)}, u32[]{:S(2)}) collective-permute-start(bf16[320,896]{1,0:T(8,128)(2,1)S(1)} %get-tuple-element.38), channel_id=1, source_target_pairs={{0,480},{32,0},{64,32},{96,64},{128,96},{160,128},{192,160},{224,1... | collective-permute-start | bytes 1720328 | tf_op jit(solution)/shard_map/ppermute | solution.py:36
  128.8 24.0 %all-to-all-start.3 = ((bf16[8,40,896]{2,1,0:T(8,128)(2,1)}), bf16[8,40,896]{2,1,0:T(8,128)(2,1)S(1)}, u32[]{:S(2)}, u32[]{:S(2)}) async-start(bf16[8,40,896]{2,1,0:T(8,128)(2,1)} %bitcast.14), calls=%async_computation.3 | async-start | bytes 1146880 | tf_op jit(solution)/shard_map/all_to_all | solution.py:44
  133.9 22.7 %copy-start.11 = (f32[1,64,1]{1,2,0:T(1,128)S(1)}, f32[1,64,1]{1,2,0:T(1,128)}, u32[]{:S(2)}) copy-start(f32[1,64,1]{1,2,0:T(1,128)} %param.14) | copy-start | bytes 772
  133.9 22.8 %copy-start.7 = (s32[1,64,1]{1,2,0:T(1,128)S(1)}, s32[1,64,1]{1,2,0:T(1,128)}, u32[]{:S(2)}) copy-start(s32[1,64,1]{1,2,0:T(1,128)} %param.12) | copy-start | bytes 772
  141.6 15.0 %copy-start.3 = (bf16[1,64,3584]{2,1,0:T(8,128)(2,1)S(1)}, bf16[1,64,3584]{2,1,0:T(8,128)(2,1)}, u32[]{:S(2)}) copy-start(bf16[1,64,3584]{2,1,0:T(8,128)(2,1)} %param.9) | copy-start | bytes 1376260
  152.9 7.3 %copy-start.9 = (s32[1,64,1]{1,2,0:T(1,128)S(1)}, s32[1,64,1]{1,2,0:T(1,128)}, u32[]{:S(2)}) copy-start(s32[1,64,1]{1,2,0:T(1,128)} %param.13) | copy-start | bytes 772
  152.9 22.6 %all-to-all-start.2 = ((bf16[8,40,896]{2,1,0:T(8,128)(2,1)}), bf16[8,40,896]{2,1,0:T(8,128)(2,1)S(1)}, u32[]{:S(2)}, u32[]{:S(2)}) async-start(bf16[8,40,896]{2,1,0:T(8,128)(2,1)} %bitcast.38), calls=%async_computation.2 | async-start | bytes 1146880 | tf_op jit(solution)/shard_map/all_to_all | solution.py:44
  157.5 17.4 %collective-permute-start.13 = (bf16[1,64,3584]{2,1,0:T(8,128)(2,1)S(1)}, bf16[1,64,3584]{2,1,0:T(8,128)(2,1)S(1)}, u32[]{:S(2)}, u32[]{:S(2)}) collective-permute-start(bf16[1,64,3584]{2,1,0:T(8,128)(2,1)S(1)} %bitcast.33), channel_id=1, source_target_pairs={{0,32},{32,64},{64,96},{96,128},{128,160},{160,192},{192,224},{224... | collective-permute-start | bytes 1376264 | tf_op jit(solution)/shard_map/ppermute | solution.py:36
  160.2 9.4 %collective-permute-start = (s32[1,64]{1,0:T(1,128)S(1)}, s32[1,64]{1,0:T(1,128)S(1)}, u32[]{:S(2)}, u32[]{:S(2)}) collective-permute-start(s32[1,64]{1,0:T(1,128)S(1)} %bitcast.37), channel_id=1, source_target_pairs={{0,480},{32,0},{64,32},{96,64},{128,96},{160,128},{192,160},{224,1... | collective-permute-start | bytes 776 | tf_op jit(solution)/shard_map/ppermute | solution.py:36
  (6 other events, 9.3 us)
